TPU v7x, 128 devices: a whole 4x4x4 slice. The times are simulated.
128 devices in a mesh: tok: 4 (over x), vocab: 32 (over y, z, core).
Axes of the slice: x: 4, y: 4, z: 4, core: 2. Of those that a mesh axis runs over, the one named last changes fastest.
Arguments:
- hidden: bfloat16 [1024, 4096], P('tok', 'vocab'), may hold values from -64 to 64
- head_weight: bfloat16 [4096, 77824], P(None, 'vocab'), may hold values from -2 to 2
- teacher_logits: bfloat16 [256, 4, 77824], P('vocab', None, 'tok'), may hold values from -18 to 300
- token_ids: int32 [1024], P('tok'), may hold values from 0 to 77823
- token_weight: float32 [1024], P('tok'), may hold values from 8 to 80
Outputs:
- divergence: float32 [1024], P('tok')
- cross_entropy: float32 [1024], P('tok')
- hidden_grad: bfloat16 [4096, 1024], P('vocab', 'tok')
All inputs are finite; a program needn't handle non-finite values.
Results may differ from a plain program's by a relative error of at most 0.02.
Values may be sent and summed in bfloat16 or wider, within the bound.
No kernel may reach another device: no remote copies, remote signals or barrier semaphores. Data moves between devices by JAX's collectives and lax.ppermute only.
A program may use at most 192 MiB of HBM per device.

v0:
```python
import jax
import jax.numpy as jnp
from jax import lax
from jax.sharding import PartitionSpec as P

CE_WEIGHT = 0.5


def on_device(hidden, head_weight, teacher_logits, token_ids, token_weight):
    tok_rows = hidden.shape[0]
    local_vocab = head_weight.shape[1]
    student = jnp.dot(
        lax.all_gather(hidden, "vocab", axis=1, tiled=True),
        head_weight,
        preferred_element_type=jnp.float32,
    )
    teacher = lax.all_to_all(
        lax.all_to_all(teacher_logits, "tok", split_axis=1, concat_axis=2, tiled=True),
        "vocab",
        split_axis=2,
        concat_axis=0,
        tiled=True,
    )
    teacher = teacher.reshape(tok_rows, local_vocab).astype(jnp.float32)
    column = lax.axis_index("vocab") * local_vocab + jnp.arange(local_vocab, dtype=jnp.int32)
    onehot = column[None, :] == token_ids[:, None]
    picked_part = jnp.sum(jnp.where(onehot, student, 0.0), axis=1)
    student_peak = jnp.max(student, axis=1)
    teacher_peak = jnp.max(teacher, axis=1)
    student_top, teacher_top = lax.pmax((student_peak, teacher_peak), "vocab")
    student_exp = jnp.exp(student - student_top[:, None])
    teacher_exp = jnp.exp(teacher - teacher_top[:, None])
    student_total, teacher_total, cross_total, picked = lax.psum(
        (
            jnp.sum(student_exp, axis=1),
            jnp.sum(teacher_exp, axis=1),
            jnp.sum(teacher_exp * (teacher - student), axis=1),
            picked_part,
        ),
        "vocab",
    )
    student_lse = student_top + jnp.log(student_total)
    teacher_lse = teacher_top + jnp.log(teacher_total)
    divergence = cross_total / teacher_total + student_lse - teacher_lse
    cross_entropy = student_lse - picked
    student_prob = student_exp / student_total[:, None]
    teacher_prob = teacher_exp / teacher_total[:, None]
    logit_grad = (
        token_weight[:, None]
        * (student_prob - teacher_prob + CE_WEIGHT * (student_prob - onehot.astype(jnp.float32)))
    ).astype(jnp.bfloat16)
    partial_grad = lax.dot_general(
        head_weight, logit_grad, (((1,), (1,)), ((), ())), preferred_element_type=jnp.float32
    )
    summed = lax.psum(partial_grad.astype(jnp.bfloat16), "vocab").astype(jnp.float32)
    share_rows = summed.shape[0] // lax.axis_size("vocab")
    hidden_grad = lax.dynamic_slice_in_dim(
        summed, lax.axis_index("vocab") * share_rows, share_rows, 0
    )
    return (divergence, cross_entropy, hidden_grad.astype(jnp.bfloat16))


def solution(mesh):
    return jax.shard_map(
        on_device,
        mesh=mesh,
        in_specs=(P("tok", "vocab"), P(None, "vocab"), P("vocab", None, "tok"), P("tok"), P("tok")),
        out_specs=(P("tok"), P("tok"), P("vocab", "tok")),
        check_vma=False,
    )
```

profile of v0, /device:TPU:0, one launch (start us, length us, event | category | flops | bytes accessed | tf_op | source)
XLA Modules:
  0.0 952.7 jit_solution(3790172972748303044)
XLA Ops:
  7.2 0.7 all-gather.2.cloned.1.call-update
  7.9 1.7 copy.20
  9.6 21.4 %all_to_all.27 = bf16[8,4,19456]{2,0,1:T(8,128)(2,1)S(1)} all-to-all(bf16[8,4,19456]{2,0,1:T(8,128)(2,1)S(1)} %copy.20), channel_id=1, replica_groups=mesh['tok'=4,'vocab'=32] {'tok'}, dimensions={1} | all-to-all | bytes 2490368 | tf_op jit(solution)/shard_map/all_to_all | solution.py:18
  30.9 58.5 %copy.22 = bf16[8,1,77824]{0,1,2:T(2,128)(2,1)} copy(bf16[8,1,77824]{2,0,1:T(8,128)(2,1)S(1)} %bitcast.48) | data formatting | bytes 2490368 | tf_op jit(solution)/shard_map/all_to_all | solution.py:18
  89.4 0.5 broadcast.13
  89.9 422.2 %reduce.3 = bf16[77824,8]{1,0:T(8,128)(2,1)} reduce(bf16[77824,1,8]{2,1,0:T(2,128)(2,1)} %bitcast.43, bf16[]{:T(256)} %broadcast.13), dimensions={1}, to_apply=%bitcast.38.reduce_sub_computation | reduce | bytes 2490370
  512.1 23.1 %reshape.35 = bf16[32,2,9728]{2,1,0:T(2,128)(2,1)} reshape(bf16[77824,8]{1,0:T(8,128)(2,1)} %reduce.3) | data formatting | bytes 2490368
  535.1 8.3 all-to-all-start.1
  543.5 19.1 %all-to-all-done.1 = bf16[32,2,9728]{2,1,0:T(2,128)(2,1)S(1)} async-done(((bf16[32,2,9728]{2,1,0:T(2,128)(2,1)}), bf16[32,2,9728]{2,1,0:T(2,128)(2,1)S(1)}, u32[]{:S(2)}, u32[]{:S(2)}) %all-to-all-start.1) | async-done | bytes 1245216 | tf_op jit(solution)/shard_map/all_to_all | solution.py:17
  562.6 47.3 %reshape.36 = bf16[77824,1,8]{2,1,0:T(2,128)(2,1)} reshape(bf16[32,2,9728]{2,1,0:T(2,128)(2,1)S(1)} %all-to-all-done.1) | data formatting | bytes 2490368
  609.9 69.1 %copy.23 = bf16[8,1,77824]{2,0,1:T(8,128)(2,1)S(1)} copy(bf16[8,1,77824]{0,1,2:T(2,128)(2,1)} %bitcast.44) | data formatting | bytes 2490368 | tf_op jit(solution)/shard_map/all_to_all | solution.py:17
  679.0 0.3 fusion.12
  679.4 1.7 fusion.13
  681.1 13.9 %fusion.24 = (f32[256]{0:T(256)S(1)}, f32[256,2432]{1,0:T(8,128)}) fusion(bf16[256,4096]{1,0:T(8,128)(2,1)} %all-gather.2.cloned.1.call-done, bf16[4096,2432]{1,0:T(8,128)(2,1)} %param.6), kind=kOutput, calls=%fused_computation.35 | convolution fusion | flops 5100896256 | bytes 24511488 | tf_op jit(solution)/shard_map/dot_general | solution.py:12
  695.0 64.4 %all-reduce.1 = (f32[256]{0:T(256)S(1)}, f32[256]{0:T(256)S(1)}) all-reduce(f32[256]{0:T(256)S(1)} %reshape.34, f32[256]{0:T(256)S(1)} %get-tuple-element.29), channel_id=1, replica_groups=mesh['tok'=4,'vocab'=32] {'vocab'}, use_global_device_ids=true, to_apply=%region_1.2 | all-reduce | flops 512 | bytes 4096 | tf_op jit(solution)/shard_map/pmax | solution.py:30
  759.6 0.6 exponential_reduce_fusion
  760.2 0.1 reduce_sum.40
  760.3 4.8 fusion.1
  765.1 62.7 %all-reduce = (f32[256]{0:T(256)S(1)}, f32[256]{0:T(256)S(1)}, f32[256]{0:T(256)S(1)}, f32[256]{0:T(256)S(1)}) all-reduce(f32[256]{0:T(256)S(1)} %reduce_sum.40, f32[256]{0:T(256)S(1)} %get-tuple-element.20, f32[256]{0:T(256)S(1)} %get-tuple-element.19, f32[256]{0:T(256)S(1)} %get-tuple-element.18), channel_id=1, replica_groups=mesh['tok'=4,'vocab'=32] {'vocab'}, use_global_device_ids=true, to_apply=%region_5.6 | all-reduce | flops 1024 | bytes 8192 | tf_op jit(solution)/shard_map/psum | solution.py:33
  827.8 14.3 %fusion = bf16[4096,256]{0,1:T(8,128)(2,1)} fusion(bf16[4096,2432]{1,0:T(8,128)(2,1)} %param.6, f32[32,8,1,2432]{3,0,1,2:T(8,128)S(1)} %copy-done, f32[256,2432]{1,0:T(8,128)} %get-tuple-element.30, f32[256]{0:T(256)S(1)} %get-tuple-element.21, f32[256]{0:T(256)S(1)} %get-tuple-element.23, f32[256]{0:T(256)S(1)} %copy-done.2, s32[2432]{0:T(1024)S(1)} %iota_add_fusion, ...), kind=kOutput, calls=%fused_computation.1 | convolution fusion | flops 5108793344 | bytes 27016704 | tf_op jit(solution)/shard_map/dot_general | solution.py:52
  842.2 0.6 fusion.22
  842.8 101.5 %all-reduce.4.cloned.1.call-done = bf16[4096,256]{0,1:T(8,128)(2,1)} async-done(((bf16[4096,256]{0,1:T(8,128)(2,1)}), bf16[4096,256]{0,1:T(8,128)(2,1)}) %all-reduce.4.cloned.1.call-update) | async-done | bytes 2097168 | tf_op jit(solution)/shard_map/psum | solution.py:55
  944.3 0.8 convert_convert_fusion
  945.1 0.7 copy.28
  (16 shorter events, 0.5 us)
Async XLA Ops:
  7.2 673.9 %all-gather.2.cloned.1.call-start = ((), (), s32[]{:S(2)}) async-start(), calls=%async_computation.2 | async-start | bytes 2162688 | tf_op jit(solution)/shard_map/all_gather | solution.py:13
  535.1 27.5 %all-to-all-start.1 = ((bf16[32,2,9728]{2,1,0:T(2,128)(2,1)}), bf16[32,2,9728]{2,1,0:T(2,128)(2,1)S(1)}, u32[]{:S(2)}, u32[]{:S(2)}) async-start(bf16[32,2,9728]{2,1,0:T(2,128)(2,1)} %reshape.35), calls=%async_computation.1 | async-start | bytes 2490368 | tf_op jit(solution)/shard_map/all_to_all | solution.py:17
  543.5 400.8 %all-reduce.4.cloned.1.call-start = ((), (), s32[]{:S(2)}) async-start(), calls=%async_computation.3 | async-start | bytes 4194304 | tf_op jit(solution)/shard_map/psum | solution.py:55
  681.1 79.2 %copy-start.1 = (s32[256]{0:T(256)S(1)}, s32[256]{0:T(256)}, u32[]{:S(2)}) copy-start(s32[256]{0:T(256)} %param.8) | copy-start | bytes 3076
  760.3 67.5 %copy-start = (f32[32,8,1,2432]{3,0,1,2:T(8,128)S(1)}, f32[32,8,1,2432]{3,0,1,2:T(8,128)}, u32[]{:S(2)}) copy-start(f32[32,8,1,2432]{3,0,1,2:T(8,128)} %fusion.13) | copy-start | bytes 7471108
  760.3 67.5 %copy-start.2 = (f32[256]{0:T(256)S(1)}, f32[256]{0:T(256)}, u32[]{:S(2)}) copy-start(f32[256]{0:T(256)} %param.9) | copy-start | bytes 3076
Sparse Core Ops, SparseCore 0:
  10.2 47.3 all-gather.1
  842.3 101.9 all-reduce.3
where the time goes:
time: 956 us; the launch traced here: 953 us
  other arithmetic  431 us (45%)
  local copies, waits for them, and re-layouts  201 us (21%)
  blocking collectives  148 us (15%)
  waiting for transfers between devices  121 us (13%)
  matrix products  28.3 us (3%)
  between operations  14.1 us (1%)
    unnamed x1, other arithmetic  422 us
    psum x1, waiting for transfers between devices, on_device(): lax.psum(partial_grad.astype(jnp.bfloat16), 'vocab').astype(jnp.float32)  102 us
    unnamed x11, local copies, waits for them, and re-layouts  73.2 us
    all_to_all x1, local copies, waits for them, and re-layouts, on_device(): lax.all_to_all(lax.all_to_all(teacher_logits, 'tok', split_axis=1, concat...  69.1 us
    pmax x1, blocking collectives, on_device(): student_top, teacher_top = lax.pmax((student_peak, teacher_peak), 'vocab')  64.4 us
    psum x1, blocking collectives, on_device(): lax.psum((jnp.sum(student_exp, axis=1), jnp.sum(teacher_exp, axis=1), jnp...  62.7 us
    all_to_all x1, local copies, waits for them, and re-layouts, on_device(): lax.all_to_all(teacher_logits, 'tok', split_axis=1, concat_axis=2, tiled=...  58.5 us
    all_to_all x1, blocking collectives, on_device(): lax.all_to_all(teacher_logits, 'tok', split_axis=1, concat_axis=2, tiled=...  21.4 us
  transfers between devices with their start and end apart: 3, of which 2 were waited for; matrix products, arithmetic and copies ran while one was open for 66% of the time, Pallas kernels for 0%

commit v1 on v0

v1 whole, which is shorter than its diff:
```python
import functools

import jax
import jax.numpy as jnp
from jax import lax
from jax.experimental import pallas as pl
from jax.experimental.pallas import tpu as pltpu
from jax.sharding import PartitionSpec as P

CE_WEIGHT = 0.5
RING = 4
CHIPS = RING * RING
SHIFTS = (0, 1, -1, 2)
MIB = 1 << 20
TAIL = 16


def params(limit):
    return pltpu.CompilerParams(vmem_limit_bytes=limit * MIB)


def cost(flops, read):
    return pl.CostEstimate(flops=flops, bytes_accessed=read, transcendentals=0)


def member(y, z, core):
    return ((y % RING) * RING + z % RING) * 2 + core % 2


def moves(dy=0, dz=0, dcore=0):
    return [
        (member(y, z, c), member(y + dy, z + dz, c + dcore))
        for y in range(RING)
        for z in range(RING)
        for c in range(2)
    ]


def swap_core(x):
    return lax.ppermute(x, "vocab", moves(dcore=1))


def from_ring(x, axis):
    return [x] + [lax.ppermute(x, "vocab", moves(**{axis: d})) for d in SHIFTS[1:]]


def eye(n):
    return lax.broadcasted_iota(jnp.int32, (n, n), 0) == lax.broadcasted_iota(jnp.int32, (n, n), 1)


def to_column(row):
    n = row.shape[1]
    return jnp.sum(jnp.where(eye(n), row, 0.0), axis=1, keepdims=True)


def to_row(column):
    n = column.shape[0]
    return jnp.sum(jnp.where(eye(n), column, 0.0), axis=0, keepdims=True)


def relayout_kernel(x_ref, o_ref):
    for b in range(x_ref.shape[1]):
        o_ref[b, 0] = x_ref[:, b, :]


def relayout(teacher_logits, local_vocab):
    rows, tiles, width = teacher_logits.shape
    shards = width // local_vocab
    return pl.pallas_call(
        relayout_kernel,
        grid=(shards,),
        in_specs=[pl.BlockSpec((rows, tiles, local_vocab), lambda i: (0, 0, i))],
        out_specs=pl.BlockSpec((tiles, 1, rows, local_vocab), lambda i: (0, i, 0, 0)),
        out_shape=jax.ShapeDtypeStruct((tiles, shards, rows, local_vocab), jnp.bfloat16),
        compiler_params=params(16),
        name="teacher_relayout",
    )(teacher_logits)


def teacher_lse_kernel(where_ref, x_ref, o_ref, acc):
    pairs = x_ref.shape[0] // 16

    def block(i):
        x = x_ref[pl.ds(pl.multiple_of(i * 16, 16), 16), :].astype(jnp.float32)
        return x[:8], x[8:]

    first, second = block(0)
    acc[...] = jnp.maximum(first, second)

    def widen(i, _):
        a, b = block(i)
        acc[...] = jnp.maximum(acc[...], jnp.maximum(a, b))
        return 0

    lax.fori_loop(1, pairs, widen, 0)
    top = jnp.max(acc[...], axis=1, keepdims=True)
    acc[...] = jnp.zeros_like(acc)

    def add(i, _):
        a, b = block(i)
        acc[...] += jnp.exp(a - top) + jnp.exp(b - top)
        return 0

    lax.fori_loop(0, pairs, add, 0)
    lse = top + jnp.log(jnp.sum(acc[...], axis=1, keepdims=True))
    lane = lax.broadcasted_iota(jnp.int32, o_ref.shape, 1)
    row = lax.broadcasted_iota(jnp.int32, o_ref.shape, 0)
    placed = jnp.where(lane == where_ref[0] * 8 + row, lse, 0.0)
    o_ref[...] = jnp.broadcast_to(jnp.sum(placed, axis=0, keepdims=True), o_ref.shape)


def teacher_lse(rows, where):
    n, width = rows.shape
    return pl.pallas_call(
        teacher_lse_kernel,
        grid_spec=pltpu.PrefetchScalarGridSpec(
            num_scalar_prefetch=1,
            grid=(1,),
            in_specs=[pl.BlockSpec((n, width), lambda i, m: (0, 0))],
            out_specs=pl.BlockSpec((8, n), lambda i, m: (0, 0)),
            scratch_shapes=[pltpu.VMEM((8, width), jnp.float32)],
        ),
        out_shape=jax.ShapeDtypeStruct((8, n), jnp.float32),
        compiler_params=params(16),
        name="teacher_lse",
    )(where, rows)


BLOCK = 512


def student_kernel(width, meta_ref, *refs):
    own, other = refs[0:RING], refs[RING : 2 * RING]
    w_ref, lse_ref, s_ref, stat_ref, hidden, peak, total = refs[2 * RING :]
    step = pl.program_id(0)
    rows = hidden.shape[0]

    @pl.when(step == 0)
    def _():
        core = meta_ref[0]
        for i in range(CHIPS):
            at = slice((i % RING) * rows, (i % RING + 1) * rows)
            chip = meta_ref[1 + i]
            hidden[:, pl.ds(pl.multiple_of((chip * 2 + core) * 128, 128), 128)] = own[i // RING][at, :]
            hidden[:, pl.ds(pl.multiple_of((chip * 2 + 1 - core) * 128, 128), 128)] = other[i // RING][at, :]
        peak[...] = jnp.full_like(peak, -jnp.inf)
        total[...] = jnp.zeros_like(total)

    s = jnp.dot(hidden[...], w_ref[...], preferred_element_type=jnp.float32)
    s_ref[...] = s
    column = step * BLOCK + lax.broadcasted_iota(jnp.int32, s.shape, 1)
    s = jnp.where(column < width, s, -jnp.inf)
    old = peak[:, :1]
    new = jnp.maximum(old, jnp.max(s, axis=1, keepdims=True))
    sums = total[:, :1] * jnp.exp(old - new) + jnp.sum(jnp.exp(s - new), axis=1, keepdims=True)
    peak[...] = jnp.broadcast_to(new, peak.shape)
    total[...] = jnp.broadcast_to(sums, total.shape)

    @pl.when(step == pl.num_programs(0) - 1)
    def _():
        row = lax.broadcasted_iota(jnp.int32, stat_ref.shape, 0)
        stat_ref[...] = jnp.where(
            row == 0, to_row(peak[:, :1]), jnp.where(row == 1, to_row(total[:, :1]), lse_ref[...])
        )


def student_logits(meta, own, other, head_weight, lse_rows):
    depth, width = head_weight.shape
    rows = own[0].shape[0] // RING
    steps = pl.cdiv(width, BLOCK)
    whole = pl.BlockSpec((RING * rows, 128), lambda i, m: (0, 0))
    return pl.pallas_call(
        functools.partial(student_kernel, width),
        grid_spec=pltpu.PrefetchScalarGridSpec(
            num_scalar_prefetch=1,
            grid=(steps,),
            in_specs=[whole] * (2 * RING)
            + [
                pl.BlockSpec((depth, BLOCK), lambda i, m: (0, i)),
                pl.BlockSpec((8, rows), lambda i, m: (0, 0)),
            ],
            out_specs=[
                pl.BlockSpec((rows, BLOCK), lambda i, m: (0, i)),
                pl.BlockSpec((8, rows), lambda i, m: (0, 0)),
            ],
            scratch_shapes=[
                pltpu.VMEM((rows, depth), jnp.bfloat16),
                pltpu.VMEM((rows, 128), jnp.float32),
                pltpu.VMEM((rows, 128), jnp.float32),
            ],
        ),
        out_shape=[
            jax.ShapeDtypeStruct((rows, width), jnp.float32),
            jax.ShapeDtypeStruct((8, rows), jnp.float32),
        ],
        compiler_params=params(40),
        cost_estimate=cost(2 * rows * depth * width, 2 * depth * width),
        name="student_logits",
    )(meta, *own, *other, head_weight, lse_rows)


def ring_sum(parts):
    return (parts[0] + parts[3]) + (parts[1] + parts[2])


def split_bf16(x):
    high = x.astype(jnp.bfloat16).astype(jnp.float32)
    rest = x - high
    middle = rest.astype(jnp.bfloat16).astype(jnp.float32)
    return high, middle, rest - middle


def grad_matmul(w_ref, grad):
    chips, share, width = w_ref.shape[0], w_ref.shape[2], w_ref.shape[3]
    out = lax.dot_general(
        w_ref[...].reshape(chips * share, width),
        grad,
        (((1,), (1,)), ((), ())),
        preferred_element_type=jnp.float32,
    )
    return out.astype(jnp.bfloat16).reshape(chips, share, grad.shape[0])


ROWS = 32


def grad_kernel(meta_ref, *refs):
    stats = refs[0:RING]
    s_ref, t_ref, id_ref, weight_ref, w_ref, grad_ref, part_ref, tail_ref, column, sums = refs[RING:]

    @pl.when(pl.program_id(0) == 0)
    def _():
        rows, width = s_ref.shape

        def pick(i, j, k, row):
            at = (j * 2 + k) * 8 + row
            return stats[i][at : at + 1, :]

        grid = [(i, j, k) for i in range(RING) for j in range(RING) for k in range(2)]
        top = functools.reduce(jnp.maximum, [pick(*g, 0) for g in grid])
        share = {g: pick(*g, 1) * jnp.exp(pick(*g, 0) - top) for g in grid}
        total = ring_sum(
            [ring_sum([share[i, j, 0] + share[i, j, 1] for j in range(RING)]) for i in range(RING)]
        )
        teacher_row = functools.reduce(jnp.add, [pick(*g, 2) for g in grid])
        column[:, 0:1] = to_column(top + jnp.log(total))
        column[:, 1:2] = to_column(teacher_row)
        column[:, 2:3] = to_column(weight_ref[...])
        column[:, 3:4] = to_column(id_ref[...].astype(jnp.float32))
        first = meta_ref[1]

        def chunk(i, _):
            at = pl.ds(pl.multiple_of(i * ROWS, ROWS), ROWS)
            student_lse, teacher_lse = column[at, 0:1], column[at, 1:2]
            weight = column[at, 2:3]
            target = column[at, 3:4].astype(jnp.int32) - first
            lane = lax.broadcasted_iota(jnp.int32, (ROWS, 128), 1)
            cross = jnp.zeros((ROWS, 128), jnp.float32)
            picked = jnp.zeros((ROWS, 128), jnp.float32)
            for j in range(width // 128):
                cols = slice(j * 128, (j + 1) * 128)
                student_logp = s_ref[at, cols] - student_lse
                teacher_logp = t_ref[at, cols].astype(jnp.float32) - teacher_lse
                student_prob = jnp.exp(student_logp)
                teacher_prob = jnp.exp(teacher_logp)
                hit = lane == target - j * 128
                onehot = jnp.where(hit, 1.0, 0.0)
                cross += teacher_prob * (teacher_logp - student_logp)
                picked += jnp.where(hit, -student_logp, 0.0)
                grad = weight * ((student_prob - teacher_prob) + CE_WEIGHT * (student_prob - onehot))
                grad_ref[at, cols] = grad.astype(jnp.bfloat16)
            sums[at, 0:1] = jnp.sum(cross, axis=1, keepdims=True)
            sums[at, 1:2] = jnp.sum(picked, axis=1, keepdims=True)
            return 0

        lax.fori_loop(0, rows // ROWS, chunk, 0)
        lines = split_bf16(to_row(sums[:, 0:1])) + split_bf16(to_row(sums[:, 1:2]))
        row = lax.broadcasted_iota(jnp.int32, tail_ref.shape, 0)
        tail = jnp.zeros(tail_ref.shape, jnp.float32)
        for k, line in enumerate(lines):
            tail = jnp.where(row == k, line, tail)
        tail_ref[...] = tail.astype(jnp.bfloat16)

    part_ref[...] = grad_matmul(w_ref, grad_ref[...])


CHIP_BLOCK = 4


def logit_grad(meta, stats, student, teacher, ids, weights, shares):
    chips, cores, share, width = shares.shape
    rows = student.shape[0]
    whole = lambda shape: pl.BlockSpec(shape, lambda i, m: (0,) * len(shape))
    return pl.pallas_call(
        grad_kernel,
        grid_spec=pltpu.PrefetchScalarGridSpec(
            num_scalar_prefetch=1,
            grid=(chips // CHIP_BLOCK,),
            in_specs=[whole(stats[0].shape)] * RING
            + [
                whole((rows, width)),
                whole((rows, width)),
                whole((1, rows)),
                whole((1, rows)),
                pl.BlockSpec((CHIP_BLOCK, 1, share, width), lambda i, m: (i, 1 - m[0], 0, 0)),
            ],
            out_specs=[
                whole((rows, width)),
                pl.BlockSpec((CHIP_BLOCK, share, rows), lambda i, m: (i, 0, 0)),
                whole((TAIL, rows)),
            ],
            scratch_shapes=[
                pltpu.VMEM((rows, 128), jnp.float32),
                pltpu.VMEM((rows, 128), jnp.float32),
            ],
        ),
        out_shape=[
            jax.ShapeDtypeStruct((rows, width), jnp.bfloat16),
            jax.ShapeDtypeStruct((chips, share, rows), jnp.bfloat16),
            jax.ShapeDtypeStruct((TAIL, rows), jnp.bfloat16),
        ],
        compiler_params=params(40),
        cost_estimate=cost(rows * chips * share * width * 2, chips * share * width * 2),
        name="logit_grad",
    )(meta, *stats, student, teacher, ids, weights, shares)


def own_kernel(meta_ref, grad_ref, w_ref, part_ref):
    part_ref[...] = grad_matmul(w_ref, grad_ref[...])


def own_share(meta, grad, shares):
    chips, cores, share, width = shares.shape
    rows = grad.shape[0]
    return pl.pallas_call(
        own_kernel,
        grid_spec=pltpu.PrefetchScalarGridSpec(
            num_scalar_prefetch=1,
            grid=(chips // CHIP_BLOCK,),
            in_specs=[
                pl.BlockSpec((rows, width), lambda i, m: (0, 0)),
                pl.BlockSpec((CHIP_BLOCK, 1, share, width), lambda i, m: (i, m[0], 0, 0)),
            ],
            out_specs=pl.BlockSpec((CHIP_BLOCK, share, rows), lambda i, m: (i, 0, 0)),
        ),
        out_shape=jax.ShapeDtypeStruct((chips, share, rows), jnp.bfloat16),
        compiler_params=params(32),
        cost_estimate=cost(rows * chips * share * width * 2, chips * share * width * 2),
        name="own_share",
    )(meta, grad, shares)


def join_kernel(a_ref, b_ref, ta_ref, tb_ref, o_ref):
    share = a_ref.shape[1]
    total = a_ref[...].astype(jnp.float32) + b_ref[...].astype(jnp.float32)
    o_ref[:, 0:share, :] = total.astype(jnp.bfloat16)
    tail = jnp.concatenate(
        [ta_ref[...].astype(jnp.float32)[0 : TAIL // 2], tb_ref[...].astype(jnp.float32)[0 : TAIL // 2]]
    ).astype(jnp.bfloat16)
    for i in range(o_ref.shape[0]):
        o_ref[i, share : share + TAIL, :] = tail


def join(a, b, tail_a, tail_b):
    chips, share, rows = a.shape
    block = pl.BlockSpec((CHIP_BLOCK, share, rows), lambda i: (i, 0, 0))
    tail = pl.BlockSpec((TAIL, rows), lambda i: (0, 0))
    return pl.pallas_call(
        join_kernel,
        grid=(chips // CHIP_BLOCK,),
        in_specs=[block, block, tail, tail],
        out_specs=pl.BlockSpec((CHIP_BLOCK, share + TAIL, rows), lambda i: (i, 0, 0)),
        out_shape=jax.ShapeDtypeStruct((chips, share + TAIL, rows), jnp.bfloat16),
        compiler_params=params(16),
        name="chip_sum",
    )(a, b, tail_a, tail_b)


def final_kernel(x_ref, div_ref, ce_ref, o_ref):
    chips = x_ref.shape[0]
    share = x_ref.shape[1] - TAIL
    total = x_ref[0, 0:share, :].astype(jnp.float32)
    for i in range(1, chips):
        total += x_ref[i, 0:share, :].astype(jnp.float32)
    o_ref[...] = total.astype(jnp.bfloat16)
    div = jnp.zeros(div_ref.shape, jnp.float32)
    ce = jnp.zeros(ce_ref.shape, jnp.float32)
    for i in range(chips):
        tail = x_ref[i, share : share + TAIL, :].astype(jnp.float32)
        line = lambda k: tail[k : k + 1]
        value = lambda k: (line(k) + line(k + 1)) + line(k + 2)
        half = TAIL // 2
        div += value(0) + value(half)
        ce += value(3) + value(half + 3)
    div_ref[...] = div
    ce_ref[...] = ce


def final(blocks):
    chips, height, rows = blocks.shape
    return pl.pallas_call(
        final_kernel,
        out_shape=[
            jax.ShapeDtypeStruct((1, rows), jnp.float32),
            jax.ShapeDtypeStruct((1, rows), jnp.float32),
            jax.ShapeDtypeStruct((height - TAIL, rows), jnp.bfloat16),
        ],
        compiler_params=params(16),
        name="final_sum",
    )(blocks)


def on_device(hidden, head_weight, teacher_logits, token_ids, token_weight):
    rows, share = hidden.shape
    depth, width = head_weight.shape
    me = lax.axis_index("vocab")
    core, chip = me % 2, me // 2
    y, z = chip // RING, chip % RING
    sources = [((y - dy) % RING) * RING + (z - dz) % RING for dy in SHIFTS for dz in SHIFTS]

    along_z = jnp.concatenate(from_ring(hidden, "dz"), axis=0)
    own = from_ring(along_z, "dy")
    other = [swap_core(x) for x in own]

    blocks = relayout(teacher_logits, width).reshape(rows, width)
    blocks = lax.all_to_all(blocks, "tok", 0, 0, tiled=True)
    lse_rows = teacher_lse(blocks, me.reshape(1))
    teacher = lax.all_to_all(blocks, "vocab", 0, 0, tiled=True)

    meta = jnp.stack([core] + sources).astype(jnp.int32)
    student, stat = student_logits(meta, own, other, head_weight, lse_rows)
    stat = jnp.concatenate([stat, swap_core(stat)], axis=0)
    stats = from_ring(jnp.concatenate(from_ring(stat, "dz"), axis=0), "dy")

    meta = jnp.stack([core, me * width]).astype(jnp.int32)
    shares = head_weight.reshape(CHIPS, 2, share, width)
    grad, part, tail = logit_grad(
        meta, stats, student, teacher, token_ids.reshape(1, rows), token_weight.reshape(1, rows), shares
    )
    from_core, from_tail = swap_core(part), swap_core(tail)
    mine = own_share(meta, grad, shares)
    summed = join(mine, from_core, tail, from_tail)

    same_core = [[member(i // RING, i % RING, c) for i in range(CHIPS)] for c in range(2)]
    blocks = lax.all_to_all(
        summed.reshape(CHIPS * (share + TAIL), rows), "vocab", 0, 0, axis_index_groups=same_core, tiled=True
    )
    divergence, cross_entropy, hidden_grad = final(blocks.reshape(CHIPS, share + TAIL, rows))
    return divergence.reshape(rows), cross_entropy.reshape(rows), hidden_grad


def solution(mesh):
    return jax.shard_map(
        on_device,
        mesh=mesh,
        in_specs=(P("tok", "vocab"), P(None, "vocab"), P("vocab", None, "tok"), P("tok"), P("tok")),
        out_specs=(P("tok"), P("tok"), P("vocab", "tok")),
        check_vma=False,
    )
```

time: 956 us -> 124 us (0.13)
  other arithmetic: 431 us -> 0.07 us
  local copies, waits for them, and re-layouts: 201 us -> 11.3 us
  blocking collectives: 148 us -> 22.4 us
  waiting for transfers between devices: 121 us -> 18.5 us
  Pallas kernels: 0 us -> 35.2 us
  matrix products: 28.3 us -> 0 us
  starting transfers between devices: 8.41 us -> 34.7 us
  between operations: 14.1 us -> 1.02 us
    unnamed x1 -> x0, other arithmetic: 422 us -> none
    all_to_all x2 -> x0, local copies, waits for them, and re-layouts: 128 us -> none  [the longest x1 69.1 us: on_device(): lax.all_to_all(lax.all_to_all(teacher_logits, 'tok', split_axis=1, concat...]
    psum x1 -> x0, waiting for transfers between devices: 102 us -> none  [on_device(): lax.psum(partial_grad.astype(jnp.bfloat16), 'vocab').astype(jnp.float32)]
    pmax x1 -> x0, blocking collectives: 64.4 us -> none  [on_device(): student_top, teacher_top = lax.pmax((student_peak, teacher_peak), 'vocab')]
    psum x1 -> x0, blocking collectives: 62.7 us -> none  [on_device(): lax.psum((jnp.sum(student_exp, axis=1), jnp.sum(teacher_exp, axis=1), jnp...]
    unnamed x11 -> x20, local copies, waits for them, and re-layouts: 73.2 us -> 11.2 us
    pallas_call x0 -> x7, Pallas kernels: none -> 35.2 us  [the longest x1 12.5 us: student_logits(): pl.pallas_call(functools.partial(student_kernel, width), grid_spec=pltpu....]
    dot_general x2 -> x0, matrix products: 28.3 us -> none  [the longest x1 14.3 us: on_device(): lax.dot_general(head_weight, logit_grad, (((1,), (1,)), ((), ())), prefer...]
  transfers between devices with their start and end apart: 3 -> 21, of which waited for: 2 -> 8; matrix products, arithmetic and copies ran while one was open for 66% -> 0% of each run, Pallas kernels for 0% -> 19%
where the time goes in v1:
time: 124 us; the launch traced here: 123 us
  Pallas kernels  35.2 us (28%)
  starting transfers between devices  34.7 us (28%)
  blocking collectives  22.4 us (18%)
  waiting for transfers between devices  18.5 us (15%)
  local copies, waits for them, and re-layouts  11.3 us (9%)
    all_to_all x1, blocking collectives, on_device(): lax.all_to_all(summed.reshape(CHIPS * (share + TAIL), rows), 'vocab', 0,...  22.4 us
    ppermute x12, starting transfers between devices, from_ring(): lax.ppermute(x, 'vocab', moves(**{axis: d}))  22.4 us
    ppermute x12, waiting for transfers between devices, from_ring(): lax.ppermute(x, 'vocab', moves(**{axis: d}))  16.3 us
    pallas_call x1, Pallas kernels, student_logits(): pl.pallas_call(functools.partial(student_kernel, width), grid_spec=pltpu....  12.5 us
    unnamed x20, local copies, waits for them, and re-layouts  11.2 us
    pallas_call x1, Pallas kernels, logit_grad(): pl.pallas_call(grad_kernel, grid_spec=pltpu.PrefetchScalarGridSpec(num_sc...  10.2 us
    all_to_all x1, starting transfers between devices, on_device(): teacher = lax.all_to_all(blocks, 'vocab', 0, 0, tiled=True)  6.53 us
    pallas_call x1, Pallas kernels, own_share(): pl.pallas_call(own_kernel, grid_spec=pltpu.PrefetchScalarGridSpec(num_sca...  4.84 us
  transfers between devices with their start and end apart: 21, of which 8 were waited for; matrix products, arithmetic and copies ran while one was open for 0% of the time, Pallas kernels for 19%

profile of v1, /device:TPU:0, one launch (start us, length us, event | category | flops | bytes accessed | tf_op | source)
XLA Modules:
  0.0 123.2 jit_solution(8518321652878162603)
XLA Ops:
  0.6 4.2 %collective-permute-start.1 = (bf16[256,128]{1,0:T(8,128)(2,1)}, bf16[256,128]{1,0:T(8,128)(2,1)S(1)}, u32[]{:S(2)}, u32[]{:S(2)}) collective-permute-start(bf16[256,128]{1,0:T(8,128)(2,1)} %param.5), channel_id=1, source_target_pairs={{0,6},{1,7},{2,0},{3,1},{4,2},{5,3},{6,4},{7,5},{8,14},{9,15},{10,... | collective-permute-start | bytes 196616 | tf_op jit(solution)/shard_map/ppermute | solution.py:44
  4.8 1.9 %collective-permute-start.2 = (bf16[256,128]{1,0:T(8,128)(2,1)}, bf16[256,128]{1,0:T(8,128)(2,1)S(1)}, u32[]{:S(2)}, u32[]{:S(2)}) collective-permute-start(bf16[256,128]{1,0:T(8,128)(2,1)} %param.5), channel_id=1, source_target_pairs={{0,4},{1,5},{2,6},{3,7},{4,0},{5,1},{6,2},{7,3},{8,12},{9,13},{10,... | collective-permute-start | bytes 196616 | tf_op jit(solution)/shard_map/ppermute | solution.py:44
  6.7 1.3 %copy-done.3 = bf16[8,4,19456]{2,1,0:T(4,128)(2,1)S(1)} copy-done((bf16[8,4,19456]{2,1,0:T(4,128)(2,1)S(1)}, bf16[8,4,19456]{2,1,0:T(4,128)(2,1)}, u32[]{:S(2)}) %copy-start.3) | copy-done | bytes 1245208
  8.0 4.3 %teacher_relayout.1 = bf16[4,8,8,2432]{3,2,1,0:T(8,128)(2,1)} custom-call(bf16[8,4,19456]{2,1,0:T(4,128)(2,1)S(1)} %copy-done.3), custom_call_target="tpu_custom_call" | custom-call | tf_op jit(solution)/shard_map/teacher_relayout/pallas_call | solution.py:69
  12.3 4.4 %all-to-all-start = ((bf16[4,64,2432]{2,1,0:T(8,128)(2,1)}), bf16[4,64,2432]{2,1,0:T(8,128)(2,1)}, u32[]{:S(2)}, u32[]{:S(2)}) async-start(bf16[4,64,2432]{2,1,0:T(8,128)(2,1)} %bitcast.19), calls=%async_computation | async-start | bytes 2490368 | tf_op jit(solution)/shard_map/all_to_all | solution.py:426
  16.8 3.3 %collective-permute-start.5 = (bf16[1024,128]{1,0:T(8,128)(2,1)S(1)}, bf16[1024,128]{1,0:T(8,128)(2,1)S(1)}, u32[]{:S(2)}, u32[]{:S(2)}) collective-permute-start(bf16[1024,128]{1,0:T(8,128)(2,1)S(1)} %constant_dynamic-update-slice_fusion.refs_0_), channel_id=1, source_target_pairs={{0,16},{1,17},{2,18},{3,19},{4,20},{5,21},{6,22},{7,23},{8,24},{9,... | collective-permute-start | bytes 786440 | tf_op jit(solution)/shard_map/ppermute | solution.py:44
  22.1 5.5 %collective-permute-done.5.refs_3_ = bf16[1024,128]{1,0:T(8,128)(2,1)S(1)} collective-permute-done((bf16[1024,128]{1,0:T(8,128)(2,1)S(1)}, bf16[1024,128]{1,0:T(8,128)(2,1)S(1)}, u32[]{:S(2)}, u32[]{:S(2)}) %collective-permute-start.5) | collective-permute-done | bytes 262176 | tf_op jit(solution)/shard_map/ppermute | solution.py:44
  27.7 4.0 %collective-permute-done.4.refs_2_ = bf16[1024,128]{1,0:T(8,128)(2,1)S(1)} collective-permute-done((bf16[1024,128]{1,0:T(8,128)(2,1)S(1)}, bf16[1024,128]{1,0:T(8,128)(2,1)S(1)}, u32[]{:S(2)}, u32[]{:S(2)}) %collective-permute-start.4) | collective-permute-done | bytes 262176 | tf_op jit(solution)/shard_map/ppermute | solution.py:44
  32.1 1.3 %all-to-all-done = bf16[4,64,2432]{2,1,0:T(8,128)(2,1)} async-done(((bf16[4,64,2432]{2,1,0:T(8,128)(2,1)}), bf16[4,64,2432]{2,1,0:T(8,128)(2,1)}, u32[]{:S(2)}, u32[]{:S(2)}) %all-to-all-start) | async-done | bytes 1245216 | tf_op jit(solution)/shard_map/all_to_all | solution.py:426
  33.4 6.5 %all-to-all-start.1 = ((bf16[32,8,2432]{2,1,0:T(8,128)(2,1)}), bf16[32,8,2432]{2,1,0:T(8,128)(2,1)S(1)}, u32[]{:S(2)}, u32[]{:S(2)}) async-start(bf16[32,8,2432]{2,1,0:T(8,128)(2,1)} %bitcast.21), calls=%async_computation.1 | async-start | bytes 2490368 | tf_op jit(solution)/shard_map/all_to_all | solution.py:428
  40.2 2.3 %teacher_lse.1.refs_9_ = f32[8,256]{1,0:T(8,128)S(1)} custom-call(s32[1]{0:T(128)} %bitcast.18.where_ref, bf16[256,2432]{1,0:T(8,128)(2,1)} %bitcast.20.x_ref), custom_call_target="tpu_custom_call" | custom-call | tf_op jit(solution)/shard_map/teacher_lse/pallas_call | solution.py:114
  42.6 12.5 %student_logits.1 = (f32[256,2432]{1,0:T(8,128)S(1)}, f32[8,256]{1,0:T(8,128)S(1)}) custom-call(s32[17]{0:T(128)S(1)} %stack.80.meta_ref, bf16[1024,128]{1,0:T(8,128)(2,1)S(1)} %constant_dynamic-update-slice_fusion.refs_0_, bf16[1024,128]{1,0:T(8,128)(2,1)S(1)} %collective-permute-done.3.refs_1_, bf16[1024,128]{1,0:T(8,128)(2,1)S(1)} %collective-permute-done.4.refs_2_, ...), custom_call_target="tpu_custom_call" | custom-call | flops 5100273664 | bytes 19922944 | tf_op jit(solution)/shard_map/student_logits/pallas_call | solution.py:172
  55.1 1.4 %copy-done.1 = f32[256,2432]{1,0:T(8,128)} copy-done((f32[256,2432]{1,0:T(8,128)}, f32[256,2432]{1,0:T(8,128)S(1)}, u32[]{:S(2)}) %copy-start.1) | copy-done | bytes 2490392
  57.7 1.8 %collective-permute-start.11 = (f32[16,256]{1,0:T(8,128)S(1)}, f32[16,256]{1,0:T(8,128)S(1)}, u32[]{:S(2)}, u32[]{:S(2)}) collective-permute-start(f32[16,256]{1,0:T(8,128)S(1)} %get-tuple-element.19), channel_id=1, source_target_pairs={{0,2},{1,3},{2,4},{3,5},{4,6},{5,7},{6,0},{7,1},{8,10},{9,11},{10,... | collective-permute-start | bytes 49160 | tf_op jit(solution)/shard_map/ppermute | solution.py:44
  59.5 2.7 %collective-permute-start.13 = (f32[16,256]{1,0:T(8,128)S(1)}, f32[16,256]{1,0:T(8,128)S(1)}, u32[]{:S(2)}, u32[]{:S(2)}) collective-permute-start(f32[16,256]{1,0:T(8,128)S(1)} %get-tuple-element.19), channel_id=1, source_target_pairs={{0,4},{1,5},{2,6},{3,7},{4,0},{5,1},{6,2},{7,3},{8,12},{9,13},{10,... | collective-permute-start | bytes 49160 | tf_op jit(solution)/shard_map/ppermute | solution.py:44
  62.2 1.5 %collective-permute-start.12 = (f32[16,256]{1,0:T(8,128)S(1)}, f32[16,256]{1,0:T(8,128)S(1)}, u32[]{:S(2)}, u32[]{:S(2)}) collective-permute-start(f32[16,256]{1,0:T(8,128)S(1)} %get-tuple-element.19), channel_id=1, source_target_pairs={{0,6},{1,7},{2,0},{3,1},{4,2},{5,3},{6,4},{7,5},{8,14},{9,15},{10,... | collective-permute-start | bytes 49160 | tf_op jit(solution)/shard_map/ppermute | solution.py:44
  63.6 2.3 %collective-permute-done.12 = f32[16,256]{1,0:T(8,128)S(1)} collective-permute-done((f32[16,256]{1,0:T(8,128)S(1)}, f32[16,256]{1,0:T(8,128)S(1)}, u32[]{:S(2)}, u32[]{:S(2)}) %collective-permute-start.12) | collective-permute-done | bytes 16416 | tf_op jit(solution)/shard_map/ppermute | solution.py:44
  65.9 3.1 %collective-permute-start.16 = (f32[64,256]{1,0:T(8,128)S(1)}, f32[64,256]{1,0:T(8,128)S(1)}, u32[]{:S(2)}, u32[]{:S(2)}) collective-permute-start(f32[64,256]{1,0:T(8,128)S(1)} %constant_dynamic-update-slice_fusion.6.refs_0_), channel_id=1, source_target_pairs={{0,16},{1,17},{2,18},{3,19},{4,20},{5,21},{6,22},{7,23},{8,24},{9,... | collective-permute-start | bytes 196616 | tf_op jit(solution)/shard_map/ppermute | solution.py:44
  73.3 2.4 %collective-permute-done.14.refs_1_ = f32[64,256]{1,0:T(8,128)S(1)} collective-permute-done((f32[64,256]{1,0:T(8,128)S(1)}, f32[64,256]{1,0:T(8,128)S(1)}, u32[]{:S(2)}, u32[]{:S(2)}) %collective-permute-start.14) | collective-permute-done | bytes 65568 | tf_op jit(solution)/shard_map/ppermute | solution.py:44
  75.6 1.7 %copy-done.2 = f32[256,2432]{1,0:T(8,128)S(1)} copy-done((f32[256,2432]{1,0:T(8,128)S(1)}, f32[256,2432]{1,0:T(8,128)}, u32[]{:S(2)}) %copy-start.2) | copy-done | bytes 2490392
  77.3 10.2 %logit_grad.1 = (bf16[256,2432]{1,0:T(8,128)(2,1)S(1)}, bf16[16,128,256]{2,1,0:T(8,128)(2,1)S(1)}, bf16[16,256]{1,0:T(8,128)(2,1)S(1)}) custom-call(s32[2]{0:T(128)S(1)} %pad_add_fusion.meta_ref, f32[64,256]{1,0:T(8,128)S(1)} %constant_dynamic-update-slice_fusion.6.refs_0_, f32[64,256]{1,0:T(8,128)S(1)} %collective-permute-done.14.refs_1_, ...), custom_call_target="tpu_custom_call" | custom-call | flops 2550136832 | bytes 9961472 | tf_op jit(solution)/shard_map/logit_grad/pallas_call | solution.py:294
  88.1 6.7 %copy-done = bf16[4096,2432]{1,0:T(8,128)(2,1)S(1)} copy-done((bf16[4096,2432]{1,0:T(8,128)(2,1)S(1)}, bf16[4096,2432]{1,0:T(8,128)(2,1)}, u32[]{:S(2)}) %copy-start) | copy-done | bytes 19922968
  94.7 4.8 %own_share.1.a_ref = bf16[16,128,256]{2,1,0:T(8,128)(2,1)S(1)} custom-call(s32[2]{0:T(128)S(1)} %pad_add_fusion.meta_ref, bf16[256,2432]{1,0:T(8,128)(2,1)S(1)} %get-tuple-element.13.grad_ref, bf16[16,2,128,2432]{3,2,1,0:T(8,128)(2,1)S(1)} %bitcast.29), custom_call_target="tpu_custom_call" | custom-call | flops 2550136832 | bytes 9961472 | tf_op jit(solution)/shard_map/own_share/pallas_call | solution.py:335
  99.9 22.4 %all_to_all.28.x_ref = bf16[16,144,256]{2,1,0:T(8,128)(2,1)S(1)} all-to-all(bf16[16,144,256]{2,1,0:T(8,128)(2,1)S(1)} %chip_sum.1), channel_id=1, replica_groups={{0,2,4,6,8,10,12,14,16,18,20,22,24,26,28,30},{1,3,5,7,9,11,13,15,17,19,..., dimensions={0} | all-to-all | bytes 2359296 | tf_op jit(solution)/shard_map/all_to_all | solution.py:445
  (51 shorter events, 9.9 us)
Async XLA Ops:
  0.6 16.1 %collective-permute-start.1 = (bf16[256,128]{1,0:T(8,128)(2,1)}, bf16[256,128]{1,0:T(8,128)(2,1)S(1)}, u32[]{:S(2)}, u32[]{:S(2)}) collective-permute-start(bf16[256,128]{1,0:T(8,128)(2,1)} %param.5), channel_id=1, source_target_pairs={{0,6},{1,7},{2,0},{3,1},{4,2},{5,3},{6,4},{7,5},{8,14},{9,15},{10,... | collective-permute-start | bytes 196616 | tf_op jit(solution)/shard_map/ppermute | solution.py:44
  4.8 11.9 %collective-permute-start = (bf16[256,128]{1,0:T(8,128)(2,1)}, bf16[256,128]{1,0:T(8,128)(2,1)S(1)}, u32[]{:S(2)}, u32[]{:S(2)}) collective-permute-start(bf16[256,128]{1,0:T(8,128)(2,1)} %param.5), channel_id=1, source_target_pairs={{0,2},{1,3},{2,4},{3,5},{4,6},{5,7},{6,0},{7,1},{8,10},{9,11},{10,... | collective-permute-start | bytes 196616 | tf_op jit(solution)/shard_map/ppermute | solution.py:44
  4.8 12.0 %collective-permute-start.2 = (bf16[256,128]{1,0:T(8,128)(2,1)}, bf16[256,128]{1,0:T(8,128)(2,1)S(1)}, u32[]{:S(2)}, u32[]{:S(2)}) collective-permute-start(bf16[256,128]{1,0:T(8,128)(2,1)} %param.5), channel_id=1, source_target_pairs={{0,4},{1,5},{2,6},{3,7},{4,0},{5,1},{6,2},{7,3},{8,12},{9,13},{10,... | collective-permute-start | bytes 196616 | tf_op jit(solution)/shard_map/ppermute | solution.py:44
  12.3 21.1 %all-to-all-start = ((bf16[4,64,2432]{2,1,0:T(8,128)(2,1)}), bf16[4,64,2432]{2,1,0:T(8,128)(2,1)}, u32[]{:S(2)}, u32[]{:S(2)}) async-start(bf16[4,64,2432]{2,1,0:T(8,128)(2,1)} %bitcast.19), calls=%async_computation | async-start | bytes 2490368 | tf_op jit(solution)/shard_map/all_to_all | solution.py:426
  16.8 10.8 %collective-permute-start.5 = (bf16[1024,128]{1,0:T(8,128)(2,1)S(1)}, bf16[1024,128]{1,0:T(8,128)(2,1)S(1)}, u32[]{:S(2)}, u32[]{:S(2)}) collective-permute-start(bf16[1024,128]{1,0:T(8,128)(2,1)S(1)} %constant_dynamic-update-slice_fusion.refs_0_), channel_id=1, source_target_pairs={{0,16},{1,17},{2,18},{3,19},{4,20},{5,21},{6,22},{7,23},{8,24},{9,... | collective-permute-start | bytes 786440 | tf_op jit(solution)/shard_map/ppermute | solution.py:44
  20.1 11.5 %collective-permute-start.4 = (bf16[1024,128]{1,0:T(8,128)(2,1)S(1)}, bf16[1024,128]{1,0:T(8,128)(2,1)S(1)}, u32[]{:S(2)}, u32[]{:S(2)}) collective-permute-start(bf16[1024,128]{1,0:T(8,128)(2,1)S(1)} %constant_dynamic-update-slice_fusion.refs_0_), channel_id=1, source_target_pairs={{0,24},{1,25},{2,26},{3,27},{4,28},{5,29},{6,30},{7,31},{8,0},{9,1... | collective-permute-start | bytes 786440 | tf_op jit(solution)/shard_map/ppermute | solution.py:44
  21.1 10.5 %collective-permute-start.3 = (bf16[1024,128]{1,0:T(8,128)(2,1)S(1)}, bf16[1024,128]{1,0:T(8,128)(2,1)S(1)}, u32[]{:S(2)}, u32[]{:S(2)}) collective-permute-start(bf16[1024,128]{1,0:T(8,128)(2,1)S(1)} %constant_dynamic-update-slice_fusion.refs_0_), channel_id=1, source_target_pairs={{0,8},{1,9},{2,10},{3,11},{4,12},{5,13},{6,14},{7,15},{8,16},{9,17... | collective-permute-start | bytes 786440 | tf_op jit(solution)/shard_map/ppermute | solution.py:44
  22.1 20.4 %collective-permute-start.6 = (bf16[1024,128]{1,0:T(8,128)(2,1)S(1)}, bf16[1024,128]{1,0:T(8,128)(2,1)S(1)}, u32[]{:S(2)}, u32[]{:S(2)}) collective-permute-start(bf16[1024,128]{1,0:T(8,128)(2,1)S(1)} %constant_dynamic-update-slice_fusion.refs_0_), channel_id=1, source_target_pairs={{0,1},{1,0},{2,3},{3,2},{4,5},{5,4},{6,7},{7,6},{8,9},{9,8},{10,11... | collective-permute-start | bytes 786440 | tf_op jit(solution)/shard_map/ppermute | solution.py:40
  27.6 14.9 %collective-permute-start.9 = (bf16[1024,128]{1,0:T(8,128)(2,1)S(1)}, bf16[1024,128]{1,0:T(8,128)(2,1)S(1)}, u32[]{:S(2)}, u32[]{:S(2)}) collective-permute-start(bf16[1024,128]{1,0:T(8,128)(2,1)S(1)} %collective-permute-done.5.refs_3_), channel_id=1, source_target_pairs={{0,1},{1,0},{2,3},{3,2},{4,5},{5,4},{6,7},{7,6},{8,9},{9,8},{10,11... | collective-permute-start | bytes 786440 | tf_op jit(solution)/shard_map/ppermute | solution.py:40
  31.6 10.9 %collective-permute-start.8 = (bf16[1024,128]{1,0:T(8,128)(2,1)S(1)}, bf16[1024,128]{1,0:T(8,128)(2,1)S(1)}, u32[]{:S(2)}, u32[]{:S(2)}) collective-permute-start(bf16[1024,128]{1,0:T(8,128)(2,1)S(1)} %collective-permute-done.4.refs_2_), channel_id=1, source_target_pairs={{0,1},{1,0},{2,3},{3,2},{4,5},{5,4},{6,7},{7,6},{8,9},{9,8},{10,11... | collective-permute-start | bytes 786440 | tf_op jit(solution)/shard_map/ppermute | solution.py:40
  31.6 10.9 %collective-permute-start.7 = (bf16[1024,128]{1,0:T(8,128)(2,1)S(1)}, bf16[1024,128]{1,0:T(8,128)(2,1)S(1)}, u32[]{:S(2)}, u32[]{:S(2)}) collective-permute-start(bf16[1024,128]{1,0:T(8,128)(2,1)S(1)} %collective-permute-done.3.refs_1_), channel_id=1, source_target_pairs={{0,1},{1,0},{2,3},{3,2},{4,5},{5,4},{6,7},{7,6},{8,9},{9,8},{10,11... | collective-permute-start | bytes 786440 | tf_op jit(solution)/shard_map/ppermute | solution.py:40
  33.4 42.2 %all-to-all-start.1 = ((bf16[32,8,2432]{2,1,0:T(8,128)(2,1)}), bf16[32,8,2432]{2,1,0:T(8,128)(2,1)S(1)}, u32[]{:S(2)}, u32[]{:S(2)}) async-start(bf16[32,8,2432]{2,1,0:T(8,128)(2,1)} %bitcast.21), calls=%async_computation.1 | async-start | bytes 2490368 | tf_op jit(solution)/shard_map/all_to_all | solution.py:428
  42.5 33.1 %copy-start.4 = (s32[256]{0:T(256)S(1)}, s32[256]{0:T(256)}, u32[]{:S(2)}) copy-start(s32[256]{0:T(256)} %param.8) | copy-start | bytes 3076
  42.5 33.1 %copy-start.5 = (f32[256]{0:T(256)S(1)}, f32[256]{0:T(256)}, u32[]{:S(2)}) copy-start(f32[256]{0:T(256)} %param.9) | copy-start | bytes 3076
  56.5 1.2 collective-permute-start.10
  57.7 5.9 %collective-permute-start.11 = (f32[16,256]{1,0:T(8,128)S(1)}, f32[16,256]{1,0:T(8,128)S(1)}, u32[]{:S(2)}, u32[]{:S(2)}) collective-permute-start(f32[16,256]{1,0:T(8,128)S(1)} %get-tuple-element.19), channel_id=1, source_target_pairs={{0,2},{1,3},{2,4},{3,5},{4,6},{5,7},{6,0},{7,1},{8,10},{9,11},{10,... | collective-permute-start | bytes 49160 | tf_op jit(solution)/shard_map/ppermute | solution.py:44
  59.5 6.4 %collective-permute-start.13 = (f32[16,256]{1,0:T(8,128)S(1)}, f32[16,256]{1,0:T(8,128)S(1)}, u32[]{:S(2)}, u32[]{:S(2)}) collective-permute-start(f32[16,256]{1,0:T(8,128)S(1)} %get-tuple-element.19), channel_id=1, source_target_pairs={{0,4},{1,5},{2,6},{3,7},{4,0},{5,1},{6,2},{7,3},{8,12},{9,13},{10,... | collective-permute-start | bytes 49160 | tf_op jit(solution)/shard_map/ppermute | solution.py:44
  62.2 3.7 %collective-permute-start.12 = (f32[16,256]{1,0:T(8,128)S(1)}, f32[16,256]{1,0:T(8,128)S(1)}, u32[]{:S(2)}, u32[]{:S(2)}) collective-permute-start(f32[16,256]{1,0:T(8,128)S(1)} %get-tuple-element.19), channel_id=1, source_target_pairs={{0,6},{1,7},{2,0},{3,1},{4,2},{5,3},{6,4},{7,5},{8,14},{9,15},{10,... | collective-permute-start | bytes 49160 | tf_op jit(solution)/shard_map/ppermute | solution.py:44
  65.9 6.2 %collective-permute-start.16 = (f32[64,256]{1,0:T(8,128)S(1)}, f32[64,256]{1,0:T(8,128)S(1)}, u32[]{:S(2)}, u32[]{:S(2)}) collective-permute-start(f32[64,256]{1,0:T(8,128)S(1)} %constant_dynamic-update-slice_fusion.6.refs_0_), channel_id=1, source_target_pairs={{0,16},{1,17},{2,18},{3,19},{4,20},{5,21},{6,22},{7,23},{8,24},{9,... | collective-permute-start | bytes 196616 | tf_op jit(solution)/shard_map/ppermute | solution.py:44
  69.0 4.3 %collective-permute-start.15 = (f32[64,256]{1,0:T(8,128)S(1)}, f32[64,256]{1,0:T(8,128)S(1)}, u32[]{:S(2)}, u32[]{:S(2)}) collective-permute-start(f32[64,256]{1,0:T(8,128)S(1)} %constant_dynamic-update-slice_fusion.6.refs_0_), channel_id=1, source_target_pairs={{0,24},{1,25},{2,26},{3,27},{4,28},{5,29},{6,30},{7,31},{8,0},{9,1... | collective-permute-start | bytes 196616 | tf_op jit(solution)/shard_map/ppermute | solution.py:44
  70.1 5.5 %collective-permute-start.14 = (f32[64,256]{1,0:T(8,128)S(1)}, f32[64,256]{1,0:T(8,128)S(1)}, u32[]{:S(2)}, u32[]{:S(2)}) collective-permute-start(f32[64,256]{1,0:T(8,128)S(1)} %constant_dynamic-update-slice_fusion.6.refs_0_), channel_id=1, source_target_pairs={{0,8},{1,9},{2,10},{3,11},{4,12},{5,13},{6,14},{7,15},{8,16},{9,17... | collective-permute-start | bytes 196616 | tf_op jit(solution)/shard_map/ppermute | solution.py:44
  87.5 12.1 %collective-permute-start.17 = (bf16[16,128,256]{2,1,0:T(8,128)(2,1)S(1)}, bf16[16,128,256]{2,1,0:T(8,128)(2,1)S(1)}, u32[]{:S(2)}, u32[]{:S(2)}) collective-permute-start(bf16[16,128,256]{2,1,0:T(8,128)(2,1)S(1)} %get-tuple-element.14), channel_id=1, source_target_pairs={{0,1},{1,0},{2,3},{3,2},{4,5},{5,4},{6,7},{7,6},{8,9},{9,8},{10,11... | collective-permute-start | bytes 3145736 | tf_op jit(solution)/shard_map/ppermute | solution.py:40
  87.6 12.0 %collective-permute-start.18 = (bf16[16,256]{1,0:T(8,128)(2,1)S(1)}, bf16[16,256]{1,0:T(8,128)(2,1)S(1)}, u32[]{:S(2)}, u32[]{:S(2)}) collective-permute-start(bf16[16,256]{1,0:T(8,128)(2,1)S(1)} %get-tuple-element.15.ta_ref), channel_id=1, source_target_pairs={{0,1},{1,0},{2,3},{3,2},{4,5},{5,4},{6,7},{7,6},{8,9},{9,8},{10,11... | collective-permute-start | bytes 24584 | tf_op jit(solution)/shard_map/ppermute | solution.py:40
  88.1 6.7 %copy-start = (bf16[4096,2432]{1,0:T(8,128)(2,1)S(1)}, bf16[4096,2432]{1,0:T(8,128)(2,1)}, u32[]{:S(2)}) copy-start(bf16[4096,2432]{1,0:T(8,128)(2,1)} %refs_8_.1) | copy-start | bytes 59768836
  (4 other events, 8.9 us)

commit v2 on v0

v2 whole, which is shorter than its diff:
```python
import functools

import jax
import jax.numpy as jnp
from jax import lax
from jax.experimental import pallas as pl
from jax.experimental.pallas import tpu as pltpu
from jax.sharding import PartitionSpec as P

CE_WEIGHT = 0.5
RING = 4
CHIPS = RING * RING
SHIFTS = (0, 1, -1, 2)
MIB = 1 << 20
SMEM = pl.BlockSpec(memory_space=pltpu.SMEM)
VMEM = pl.BlockSpec(memory_space=pltpu.VMEM)
HBM = pl.BlockSpec(memory_space=pltpu.HBM)
TAIL = 16


def params(limit):
    return pltpu.CompilerParams(vmem_limit_bytes=limit * MIB)


def cost(flops, read):
    return pl.CostEstimate(flops=flops, bytes_accessed=read, transcendentals=0)


def in_vmem(x):
    return pltpu.with_memory_space_constraint(x, pltpu.VMEM)


def in_hbm(x):
    return pltpu.with_memory_space_constraint(x, pltpu.HBM)


def after(x, *others):
    return lax.optimization_barrier((x,) + others)[0]


def member(y, z, core):
    return ((y % RING) * RING + z % RING) * 2 + core % 2


def moves(dy=0, dz=0, dcore=0):
    return [
        (member(y, z, c), member(y + dy, z + dz, c + dcore))
        for y in range(RING)
        for z in range(RING)
        for c in range(2)
    ]


def swap_core(x):
    return lax.ppermute(x, "vocab", moves(dcore=1))


def from_ring(x, axis):
    return [x] + [lax.ppermute(x, "vocab", moves(**{axis: d})) for d in SHIFTS[1:]]


def eye(n):
    return lax.broadcasted_iota(jnp.int32, (n, n), 0) == lax.broadcasted_iota(jnp.int32, (n, n), 1)


def to_column(row):
    n = row.shape[1]
    return jnp.sum(jnp.where(eye(n), row, 0.0), axis=1, keepdims=True)


def to_row(column):
    n = column.shape[0]
    return jnp.sum(jnp.where(eye(n), column, 0.0), axis=0, keepdims=True)


def load_kernel(x_ref, o_ref, sem):
    copy = pltpu.make_async_copy(x_ref, o_ref, sem)
    copy.start()
    copy.wait()


def load(x):
    return pl.pallas_call(
        load_kernel,
        in_specs=[HBM],
        out_specs=VMEM,
        out_shape=jax.ShapeDtypeStruct(x.shape, x.dtype),
        scratch_shapes=[pltpu.SemaphoreType.DMA],
        compiler_params=params(4),
        cost_estimate=cost(0, 2 * x.size),
        name="load_head",
    )(in_hbm(x))


def regroup_kernel(x_ref, o_ref, sem):
    tiles, shards, rows, width = o_ref.shape
    copies = [
        pltpu.make_async_copy(x_ref.at[b, :, pl.ds(k * width, width)], o_ref.at[b, k], sem.at[b, k])
        for b in range(tiles)
        for k in range(shards)
    ]
    for copy in copies:
        copy.start()
    for copy in copies:
        copy.wait()


def regroup(teacher_logits, local_vocab):
    tiles, rows, width = teacher_logits.shape
    shards = width // local_vocab
    return pl.pallas_call(
        regroup_kernel,
        in_specs=[pl.BlockSpec(memory_space=pl.ANY)],
        out_specs=pl.BlockSpec(memory_space=pl.ANY),
        out_shape=jax.ShapeDtypeStruct((tiles, shards, rows, local_vocab), jnp.bfloat16),
        scratch_shapes=[pltpu.SemaphoreType.DMA((tiles, shards))],
        compiler_params=params(4),
        name="teacher_regroup",
    )(teacher_logits)


def teacher_lse_kernel(meta_ref, x_ref, stat_ref, o_ref, acc):
    pairs = x_ref.shape[0] // 16

    def block(i):
        x = x_ref[pl.ds(pl.multiple_of(i * 16, 16), 16), :].astype(jnp.float32)
        return x[:8], x[8:]

    first, second = block(0)
    acc[...] = jnp.maximum(first, second)

    def widen(i, _):
        a, b = block(i)
        acc[...] = jnp.maximum(acc[...], jnp.maximum(a, b))
        return 0

    lax.fori_loop(1, pairs, widen, 0)
    top = jnp.max(acc[...], axis=1, keepdims=True)
    acc[...] = jnp.zeros_like(acc)

    def add(i, _):
        a, b = block(i)
        acc[...] += jnp.exp(a - top) + jnp.exp(b - top)
        return 0

    lax.fori_loop(0, pairs, add, 0)
    lse = top + jnp.log(jnp.sum(acc[...], axis=1, keepdims=True))
    lane = lax.broadcasted_iota(jnp.int32, o_ref.shape, 1)
    row = lax.broadcasted_iota(jnp.int32, o_ref.shape, 0)
    placed = jnp.where(lane == meta_ref[2] * 8 + row, lse, 0.0)
    o_ref[...] = jnp.where(row == 2, jnp.sum(placed, axis=0, keepdims=True), stat_ref[...])


def teacher_lse(rows, meta, stat):
    n, width = rows.shape
    return pl.pallas_call(
        teacher_lse_kernel,
        in_specs=[SMEM, VMEM, VMEM],
        out_specs=VMEM,
        scratch_shapes=[pltpu.VMEM((8, width), jnp.float32)],
        out_shape=jax.ShapeDtypeStruct((8, n), jnp.float32),
        compiler_params=params(4),
        name="teacher_lse",
    )(meta, rows, stat)


ROWS = 32
BLOCK = 512


def column_blocks(width):
    return [(first, min(BLOCK, width - first)) for first in range(0, width, BLOCK)]


def student_kernel(meta_ref, *refs):
    own, other = refs[0:RING], refs[RING : 2 * RING]
    w_ref, s_ref, stat_ref, hidden, logits, sem = refs[2 * RING :]
    rows, width = s_ref.shape
    share = own[0].shape[1]
    core = meta_ref[0]
    for i in range(CHIPS):
        at = slice((i % RING) * rows, (i % RING + 1) * rows)
        chip = meta_ref[3 + i] * 2
        hidden[:, pl.ds(pl.multiple_of((chip + core) * share, share), share)] = own[i // RING][at, :]
        hidden[:, pl.ds(pl.multiple_of((chip + 1 - core) * share, share), share)] = other[i // RING][at, :]
    peaks, totals, copies = [], [], []
    for k, (first, size) in enumerate(column_blocks(width)):
        cols = pl.ds(first, size)
        s = jnp.dot(hidden[...], w_ref[:, cols], preferred_element_type=jnp.float32)
        logits[:, cols] = s
        copies.append(pltpu.make_async_copy(logits.at[:, cols], s_ref.at[:, cols], sem.at[k]))
        copies[k].start()
        peaks.append(jnp.max(s, axis=1, keepdims=True))
        totals.append(jnp.sum(jnp.exp(s - peaks[k]), axis=1, keepdims=True))
    peak = functools.reduce(jnp.maximum, peaks)
    total = functools.reduce(jnp.add, [t * jnp.exp(p - peak) for p, t in zip(peaks, totals)])
    row = lax.broadcasted_iota(jnp.int32, stat_ref.shape, 0)
    stat_ref[...] = jnp.where(row == 0, to_row(peak), jnp.where(row == 1, to_row(total), 0.0))
    for copy in copies:
        copy.wait()


def student_logits(meta, own, other, head_weight):
    depth, width = head_weight.shape
    rows = own[0].shape[0] // RING
    return pl.pallas_call(
        student_kernel,
        in_specs=[SMEM] + [VMEM] * (2 * RING + 1),
        out_specs=[HBM, VMEM],
        out_shape=[
            pltpu.HBM((rows, width), jnp.float32),
            jax.ShapeDtypeStruct((8, rows), jnp.float32),
        ],
        scratch_shapes=[
            pltpu.VMEM((rows, depth), jnp.bfloat16),
            pltpu.VMEM((rows, width), jnp.float32),
            pltpu.SemaphoreType.DMA((len(column_blocks(width)),)),
        ],
        compiler_params=params(12),
        cost_estimate=cost(2 * rows * depth * width, 2 * depth * width),
        name="student_logits",
    )(meta, *own, *other, in_vmem(head_weight))


def ring_sum(parts):
    return (parts[0] + parts[3]) + (parts[1] + parts[2]) if len(parts) == RING else parts[0] + parts[1]


def merged(blocks):
    top = functools.reduce(jnp.maximum, [x[0:1] for x in blocks])
    total = ring_sum([x[1:2] * jnp.exp(x[0:1] - top) for x in blocks])
    return top, total, ring_sum([x[2:3] for x in blocks])


def merge_kernel(*refs):
    o_ref = refs[-1]
    top, total, lse = merged([x[...] for x in refs[:-1]])
    row = lax.broadcasted_iota(jnp.int32, o_ref.shape, 0)
    o_ref[...] = jnp.where(row == 0, top, jnp.where(row == 1, total, lse))


def merge(*blocks):
    return pl.pallas_call(
        merge_kernel,
        out_shape=jax.ShapeDtypeStruct(blocks[0].shape, jnp.float32),
        compiler_params=params(4),
        name="merge_stats",
    )(*blocks)


def split_bf16(x):
    high = x.astype(jnp.bfloat16).astype(jnp.float32)
    rest = x - high
    middle = rest.astype(jnp.bfloat16).astype(jnp.float32)
    return high, middle, rest - middle


CHIP_BLOCK = 4


def share_matmul(w_ref, grad_ref, part_ref):
    chips, share, width = w_ref.shape
    for i in range(0, chips, CHIP_BLOCK):
        out = lax.dot_general(
            w_ref[i : i + CHIP_BLOCK].reshape(CHIP_BLOCK * share, width),
            grad_ref[...],
            (((1,), (1,)), ((), ())),
            preferred_element_type=jnp.float32,
        )
        part_ref[i : i + CHIP_BLOCK] = out.astype(jnp.bfloat16).reshape(CHIP_BLOCK, share, out.shape[1])


def grad_kernel(meta_ref, *refs):
    stats = refs[0:RING]
    s_ref, t_ref, id_ref, weight_ref, w_ref = refs[RING : RING + 5]
    grad_ref, part_ref, tail_ref, own_w_ref, column, cross, picked, logits, head, s_sem, w_sem, own_sem = refs[RING + 5 :]
    rows, width = s_ref.shape
    chips, share, _ = part_ref.shape
    heads = w_ref.reshape(chips, 2, share, width)
    s_copy = pltpu.make_async_copy(s_ref, logits, s_sem)
    w_copy = pltpu.make_async_copy(heads.at[:, 1 - meta_ref[0]], head, w_sem)
    own_copy = pltpu.make_async_copy(heads.at[:, meta_ref[0]], own_w_ref, own_sem)
    s_copy.start()

    top, sums, teacher_row = merged([x[...] for x in stats])
    column[:, 0:1] = to_column(top + jnp.log(sums))
    column[:, 1:2] = to_column(teacher_row)
    column[:, 2:3] = to_column(weight_ref[...])
    column[:, 3:4] = to_column(id_ref[...].astype(jnp.float32))
    lane = lax.broadcasted_iota(jnp.int32, (ROWS, 128), 1)
    s_copy.wait()
    w_copy.start()

    def chunk(i, _):
        at = pl.ds(pl.multiple_of(i * ROWS, ROWS), ROWS)
        student_lse, teacher_lse, weight = column[at, 0:1], column[at, 1:2], column[at, 2:3]
        target = column[at, 3:4].astype(jnp.int32) - meta_ref[1]
        gap = jnp.zeros((ROWS, 128), jnp.float32)
        pick = jnp.zeros((ROWS, 128), jnp.float32)
        for j in range(0, width, 128):
            cols = slice(j, j + 128)
            student_logp = logits[at, cols] - student_lse
            teacher_logp = t_ref[at, cols].astype(jnp.float32) - teacher_lse
            student_prob = jnp.exp(student_logp)
            teacher_prob = jnp.exp(teacher_logp)
            hit = lane == target - j
            onehot = jnp.where(hit, 1.0, 0.0)
            gap += teacher_prob * (teacher_logp - student_logp)
            pick += jnp.where(hit, -student_logp, 0.0)
            grad = weight * ((student_prob - teacher_prob) + CE_WEIGHT * (student_prob - onehot))
            grad_ref[at, cols] = grad.astype(jnp.bfloat16)
        cross[at, :] = gap
        picked[at, :] = pick
        return 0

    lax.fori_loop(0, rows // ROWS, chunk, 0)
    w_copy.wait()
    own_copy.start()
    share_matmul(head, grad_ref, part_ref)

    gap = to_row(jnp.sum(cross[...], axis=1, keepdims=True))
    pick = to_row(jnp.sum(picked[...], axis=1, keepdims=True))
    row = lax.broadcasted_iota(jnp.int32, tail_ref.shape, 0)
    tail = jnp.zeros(tail_ref.shape, jnp.float32)
    for k, line in enumerate(split_bf16(gap) + split_bf16(pick)):
        tail = jnp.where(row == k, line, tail)
    tail_ref[...] = tail.astype(jnp.bfloat16)
    own_copy.wait()


def logit_grad(meta, stats, student, teacher, ids, weights, head_weight):
    depth, width = head_weight.shape
    share = depth // CHIPS // 2
    rows = student.shape[0]
    return pl.pallas_call(
        grad_kernel,
        in_specs=[SMEM] + [VMEM] * RING + [HBM] + [VMEM] * 3 + [HBM],
        out_specs=[VMEM] * 4,
        out_shape=[
            jax.ShapeDtypeStruct((rows, width), jnp.bfloat16),
            jax.ShapeDtypeStruct((CHIPS, share, rows), jnp.bfloat16),
            jax.ShapeDtypeStruct((TAIL, rows), jnp.bfloat16),
            jax.ShapeDtypeStruct((CHIPS, share, width), jnp.bfloat16),
        ],
        scratch_shapes=[
            pltpu.VMEM((rows, 128), jnp.float32),
            pltpu.VMEM((rows, 128), jnp.float32),
            pltpu.VMEM((rows, 128), jnp.float32),
            pltpu.VMEM((rows, width), jnp.float32),
            pltpu.VMEM((CHIPS, share, width), jnp.bfloat16),
            pltpu.SemaphoreType.DMA,
            pltpu.SemaphoreType.DMA,
            pltpu.SemaphoreType.DMA,
        ],
        compiler_params=params(20),
        cost_estimate=cost(rows * depth * width, 2 * depth * width),
        name="logit_grad",
    )(meta, *stats, in_hbm(student), teacher, ids, weights, in_hbm(head_weight))


def own_kernel(grad_ref, w_ref, part_ref):
    share_matmul(w_ref, grad_ref, part_ref)


def own_share(grad, own_w):
    chips, share, width = own_w.shape
    rows = grad.shape[0]
    return pl.pallas_call(
        own_kernel,
        in_specs=[VMEM, VMEM],
        out_specs=VMEM,
        out_shape=jax.ShapeDtypeStruct((chips, share, rows), jnp.bfloat16),
        compiler_params=params(6),
        cost_estimate=cost(2 * rows * chips * share * width, 2 * chips * share * width),
        name="own_share",
    )(grad, in_vmem(own_w))


def join_kernel(a_ref, b_ref, ta_ref, tb_ref, o_ref):
    share = a_ref.shape[1]
    total = a_ref[...].astype(jnp.float32) + b_ref[...].astype(jnp.float32)
    o_ref[:, 0:share, :] = total.astype(jnp.bfloat16)
    tail = jnp.concatenate(
        [ta_ref[...].astype(jnp.float32)[0 : TAIL // 2], tb_ref[...].astype(jnp.float32)[0 : TAIL // 2]]
    ).astype(jnp.bfloat16)
    for i in range(o_ref.shape[0]):
        o_ref[i, share : share + TAIL, :] = tail


def join(a, b, tail_a, tail_b):
    chips, share, rows = a.shape
    block = pl.BlockSpec((CHIP_BLOCK, share, rows), lambda i: (i, 0, 0))
    tail = pl.BlockSpec((TAIL, rows), lambda i: (0, 0))
    return pl.pallas_call(
        join_kernel,
        grid=(chips // CHIP_BLOCK,),
        in_specs=[block, block, tail, tail],
        out_specs=pl.BlockSpec((CHIP_BLOCK, share + TAIL, rows), lambda i: (i, 0, 0)),
        out_shape=jax.ShapeDtypeStruct((chips, share + TAIL, rows), jnp.bfloat16),
        compiler_params=params(16),
        name="chip_sum",
    )(a, b, tail_a, tail_b)


def final_kernel(x_ref, div_ref, ce_ref, o_ref):
    chips = x_ref.shape[0]
    share = x_ref.shape[1] - TAIL
    total = x_ref[0, 0:share, :].astype(jnp.float32)
    for i in range(1, chips):
        total += x_ref[i, 0:share, :].astype(jnp.float32)
    o_ref[...] = total.astype(jnp.bfloat16)
    div = jnp.zeros(div_ref.shape, jnp.float32)
    ce = jnp.zeros(ce_ref.shape, jnp.float32)
    for i in range(chips):
        tail = x_ref[i, share : share + TAIL, :].astype(jnp.float32)
        line = lambda k: tail[k : k + 1]
        value = lambda k: (line(k) + line(k + 1)) + line(k + 2)
        half = TAIL // 2
        div += value(0) + value(half)
        ce += value(3) + value(half + 3)
    div_ref[...] = div
    ce_ref[...] = ce


def final(blocks):
    chips, height, rows = blocks.shape
    return pl.pallas_call(
        final_kernel,
        out_shape=[
            jax.ShapeDtypeStruct((1, rows), jnp.float32),
            jax.ShapeDtypeStruct((1, rows), jnp.float32),
            jax.ShapeDtypeStruct((height - TAIL, rows), jnp.bfloat16),
        ],
        compiler_params=params(16),
        name="final_sum",
    )(blocks)


def on_device(hidden, head_weight, teacher_logits, token_ids, token_weight):
    rows, share = hidden.shape
    depth, width = head_weight.shape
    me = lax.axis_index("vocab")
    core, chip = me % 2, me // 2
    y, z = chip // RING, chip % RING
    sources = [((y - dy) % RING) * RING + (z - dz) % RING for dy in SHIFTS for dz in SHIFTS]

    meta = jnp.stack([core, me * width, me] + sources).astype(jnp.int32)

    along_z = jnp.concatenate(from_ring(hidden, "dz"), axis=0)
    own = from_ring(along_z, "dy")
    blocks = jnp.transpose(after(teacher_logits, along_z, meta), (1, 0, 2))
    blocks = regroup(blocks, width).reshape(rows, width)
    head = load(after(head_weight, blocks))
    blocks = lax.all_to_all(blocks, "tok", 0, 0, tiled=True)
    other = [swap_core(x) for x in own]
    student, stat = student_logits(meta, own, other, head)

    blocks = after(blocks, stat)
    teacher = lax.all_to_all(blocks, "vocab", 0, 0, tiled=True)
    stat = teacher_lse(blocks, meta, stat)
    stat = merge(stat, swap_core(stat))
    stats = from_ring(merge(*from_ring(stat, "dz")), "dy")

    grad, part, tail, own_w = logit_grad(
        meta, stats, student, teacher, token_ids.reshape(1, rows), token_weight.reshape(1, rows), head_weight
    )
    from_core, from_tail = swap_core(part), swap_core(tail)
    mine = own_share(grad, own_w)
    summed = join(mine, from_core, tail, from_tail)

    same_core = [[member(i // RING, i % RING, c) for i in range(CHIPS)] for c in range(2)]
    blocks = lax.all_to_all(
        summed.reshape(CHIPS * (share + TAIL), rows), "vocab", 0, 0, axis_index_groups=same_core, tiled=True
    )
    divergence, cross_entropy, hidden_grad = final(blocks.reshape(CHIPS, share + TAIL, rows))
    return divergence.reshape(rows), cross_entropy.reshape(rows), hidden_grad


def solution(mesh):
    return jax.shard_map(
        on_device,
        mesh=mesh,
        in_specs=(P("tok", "vocab"), P(None, "vocab"), P("vocab", None, "tok"), P("tok"), P("tok")),
        out_specs=(P("tok"), P("tok"), P("vocab", "tok")),
        check_vma=False,
    )
```

time: 956 us -> 109 us (0.11)
  other arithmetic: 431 us -> 0 us
  local copies, waits for them, and re-layouts: 201 us -> 2.68 us
  blocking collectives: 148 us -> 22.6 us
  waiting for transfers between devices: 121 us -> 14.5 us
  Pallas kernels: 0 us -> 31.9 us
  matrix products: 28.3 us -> 0 us
  starting transfers between devices: 8.41 us -> 36.1 us
  between operations: 14.1 us -> 0.84 us
    unnamed x1 -> x0, other arithmetic: 422 us -> none
    all_to_all x2 -> x0, local copies, waits for them, and re-layouts: 128 us -> none  [the longest x1 69.1 us: on_device(): lax.all_to_all(lax.all_to_all(teacher_logits, 'tok', split_axis=1, concat...]
    psum x1 -> x0, waiting for transfers between devices: 102 us -> none  [on_device(): lax.psum(partial_grad.astype(jnp.bfloat16), 'vocab').astype(jnp.float32)]
    unnamed x11 -> x7, local copies, waits for them, and re-layouts: 73.2 us -> 0.92 us
    pmax x1 -> x0, blocking collectives: 64.4 us -> none  [on_device(): student_top, teacher_top = lax.pmax((student_peak, teacher_peak), 'vocab')]
    psum x1 -> x0, blocking collectives: 62.7 us -> none  [on_device(): lax.psum((jnp.sum(student_exp, axis=1), jnp.sum(teacher_exp, axis=1), jnp...]
    pallas_call x0 -> x10, Pallas kernels: none -> 31.9 us  [the longest x1 9.94 us: logit_grad(): pl.pallas_call(grad_kernel, in_specs=[SMEM] + [VMEM] * RING + [HBM] + [VM...]
    dot_general x2 -> x0, matrix products: 28.3 us -> none  [the longest x1 14.3 us: on_device(): lax.dot_general(head_weight, logit_grad, (((1,), (1,)), ((), ())), prefer...]
  transfers between devices with their start and end apart: 3 -> 21, of which waited for: 2 -> 7; matrix products, arithmetic and copies ran while one was open for 66% -> 2% of each run, Pallas kernels for 0% -> 19%
where the time goes in v2:
time: 109 us
  starting transfers between devices  36.1 us (33%)
  Pallas kernels  31.9 us (29%)
  blocking collectives  22.6 us (21%)
  waiting for transfers between devices  14.5 us (13%)
  local copies, waits for them, and re-layouts  2.68 us (2%)
    ppermute x12, starting transfers between devices, from_ring(): lax.ppermute(x, 'vocab', moves(**{axis: d}))  25 us
    all_to_all x1, blocking collectives, on_device(): lax.all_to_all(summed.reshape(CHIPS * (share + TAIL), rows), 'vocab', 0,...  22.6 us
    ppermute x12, waiting for transfers between devices, from_ring(): lax.ppermute(x, 'vocab', moves(**{axis: d}))  13.5 us
    pallas_call x1, Pallas kernels, logit_grad(): pl.pallas_call(grad_kernel, in_specs=[SMEM] + [VMEM] * RING + [HBM] + [VM...  9.94 us
    pallas_call x1, Pallas kernels, student_logits(): pl.pallas_call(student_kernel, in_specs=[SMEM] + [VMEM] * (2 * RING + 1),...  7.54 us
    pallas_call x1, Pallas kernels, load(): pl.pallas_call(load_kernel, in_specs=[HBM], out_specs=VMEM, out_shape=jax...  6.67 us
    all_to_all x1, starting transfers between devices, on_device(): teacher = lax.all_to_all(blocks, 'vocab', 0, 0, tiled=True)  5.26 us
    all_to_all x1, starting transfers between devices, on_device(): blocks = lax.all_to_all(blocks, 'tok', 0, 0, tiled=True)  4.31 us
  transfers between devices with their start and end apart: 21, of which 7 were waited for; matrix products, arithmetic and copies ran while one was open for 2% of the time, Pallas kernels for 19%

profile of v2, /device:TPU:0, one launch (start us, length us, event | category | flops | bytes accessed | tf_op | source)
XLA Modules:
  0.0 108.5 jit_solution(5322716791005637318)
XLA Ops:
  0.6 2.1 %collective-permute-start = (bf16[256,128]{1,0:T(8,128)(2,1)}, bf16[256,128]{1,0:T(8,128)(2,1)S(1)}, u32[]{:S(2)}, u32[]{:S(2)}) collective-permute-start(bf16[256,128]{1,0:T(8,128)(2,1)} %param.5), channel_id=1, source_target_pairs={{0,2},{1,3},{2,4},{3,5},{4,6},{5,7},{6,0},{7,1},{8,10},{9,11},{10,... | collective-permute-start | bytes 196616 | tf_op jit(solution)/shard_map/ppermute | solution.py:59
  2.7 2.2 %collective-permute-start.1 = (bf16[256,128]{1,0:T(8,128)(2,1)}, bf16[256,128]{1,0:T(8,128)(2,1)S(1)}, u32[]{:S(2)}, u32[]{:S(2)}) collective-permute-start(bf16[256,128]{1,0:T(8,128)(2,1)} %param.5), channel_id=1, source_target_pairs={{0,6},{1,7},{2,0},{3,1},{4,2},{5,3},{6,4},{7,5},{8,14},{9,15},{10,... | collective-permute-start | bytes 196616 | tf_op jit(solution)/shard_map/ppermute | solution.py:59
  4.9 1.8 %collective-permute-start.2 = (bf16[256,128]{1,0:T(8,128)(2,1)}, bf16[256,128]{1,0:T(8,128)(2,1)S(1)}, u32[]{:S(2)}, u32[]{:S(2)}) collective-permute-start(bf16[256,128]{1,0:T(8,128)(2,1)} %param.5), channel_id=1, source_target_pairs={{0,4},{1,5},{2,6},{3,7},{4,0},{5,1},{6,2},{7,3},{8,12},{9,13},{10,... | collective-permute-start | bytes 196616 | tf_op jit(solution)/shard_map/ppermute | solution.py:59
  7.6 3.3 %collective-permute-done.2 = bf16[256,128]{1,0:T(8,128)(2,1)S(1)} collective-permute-done((bf16[256,128]{1,0:T(8,128)(2,1)}, bf16[256,128]{1,0:T(8,128)(2,1)S(1)}, u32[]{:S(2)}, u32[]{:S(2)}) %collective-permute-start.2) | collective-permute-done | bytes 65568 | tf_op jit(solution)/shard_map/ppermute | solution.py:59
  10.9 1.6 %collective-permute-start.3 = (bf16[1024,128]{1,0:T(8,128)(2,1)S(1)}, bf16[1024,128]{1,0:T(8,128)(2,1)S(1)}, u32[]{:S(2)}, u32[]{:S(2)}) collective-permute-start(bf16[1024,128]{1,0:T(8,128)(2,1)S(1)} %constant_dynamic-update-slice_fusion.refs_0_), channel_id=1, source_target_pairs={{0,8},{1,9},{2,10},{3,11},{4,12},{5,13},{6,14},{7,15},{8,16},{9,17... | collective-permute-start | bytes 786440 | tf_op jit(solution)/shard_map/ppermute | solution.py:59
  12.5 1.7 %collective-permute-start.4 = (bf16[1024,128]{1,0:T(8,128)(2,1)S(1)}, bf16[1024,128]{1,0:T(8,128)(2,1)S(1)}, u32[]{:S(2)}, u32[]{:S(2)}) collective-permute-start(bf16[1024,128]{1,0:T(8,128)(2,1)S(1)} %constant_dynamic-update-slice_fusion.refs_0_), channel_id=1, source_target_pairs={{0,24},{1,25},{2,26},{3,27},{4,28},{5,29},{6,30},{7,31},{8,0},{9,1... | collective-permute-start | bytes 786440 | tf_op jit(solution)/shard_map/ppermute | solution.py:59
  14.2 2.0 %collective-permute-start.5 = (bf16[1024,128]{1,0:T(8,128)(2,1)S(1)}, bf16[1024,128]{1,0:T(8,128)(2,1)S(1)}, u32[]{:S(2)}, u32[]{:S(2)}) collective-permute-start(bf16[1024,128]{1,0:T(8,128)(2,1)S(1)} %constant_dynamic-update-slice_fusion.refs_0_), channel_id=1, source_target_pairs={{0,16},{1,17},{2,18},{3,19},{4,20},{5,21},{6,22},{7,23},{8,24},{9,... | collective-permute-start | bytes 786440 | tf_op jit(solution)/shard_map/ppermute | solution.py:59
  16.3 1.7 %copy.10 = bf16[8,4,19456]{2,0,1:T(8,128)(2,1)S(1)} copy(bf16[8,4,19456]{2,1,0:T(4,128)(2,1)} %param.7) | data formatting | bytes 2490368 | tf_op jit(solution)/shard_map/optimization_barrier | solution.py:38
  19.3 4.3 %all-to-all-start = ((bf16[4,64,2432]{2,1,0:T(8,128)(2,1)}), bf16[4,64,2432]{2,1,0:T(8,128)(2,1)}, u32[]{:S(2)}, u32[]{:S(2)}) async-start(bf16[4,64,2432]{2,1,0:T(8,128)(2,1)} %bitcast.20), calls=%async_computation | async-start | bytes 2490368 | tf_op jit(solution)/shard_map/all_to_all | solution.py:454
  25.7 6.7 %load_head.1.refs_8_ = bf16[4096,2432]{1,0:T(8,128)(2,1)S(1)} custom-call(bf16[4096,2432]{1,0:T(8,128)(2,1)} %refs_8_.1), custom_call_target="tpu_custom_call" | custom-call | bytes 19922944 | tf_op jit(solution)/shard_map/load_head/pallas_call | solution.py:83
  32.4 7.5 %student_logits.1 = (f32[256,2432]{1,0:T(8,128)}, f32[8,256]{1,0:T(8,128)S(1)}) custom-call(s32[19]{0:T(128)S(1)} %stack.79.meta_ref, bf16[1024,128]{1,0:T(8,128)(2,1)S(1)} %constant_dynamic-update-slice_fusion.refs_0_, bf16[1024,128]{1,0:T(8,128)(2,1)S(1)} %collective-permute-done.3.refs_1_, bf16[1024,128]{1,0:T(8,128)(2,1)S(1)} %collective-permute-done.4.refs_2_, ...), custom_call_target="tpu_custom_call" | custom-call | flops 5100273664 | bytes 19922944 | tf_op jit(solution)/shard_map/student_logits/pallas_call | solution.py:206
  39.9 5.3 %all-to-all-start.1 = ((bf16[32,8,2432]{2,1,0:T(8,128)(2,1)}), bf16[32,8,2432]{2,1,0:T(8,128)(2,1)S(1)}, u32[]{:S(2)}, u32[]{:S(2)}) async-start(bf16[32,8,2432]{2,1,0:T(8,128)(2,1)} %bitcast.22), calls=%async_computation.1 | async-start | bytes 2490368 | tf_op jit(solution)/shard_map/all_to_all | solution.py:459
  45.2 2.4 %teacher_lse.1.refs_0_ = f32[8,256]{1,0:T(8,128)S(1)} custom-call(s32[19]{0:T(128)S(1)} %stack.79.meta_ref, bf16[256,2432]{1,0:T(8,128)(2,1)} %bitcast.21.x_ref, f32[8,256]{1,0:T(8,128)S(1)} %get-tuple-element.15.stat_ref), custom_call_target="tpu_custom_call" | custom-call | tf_op jit(solution)/shard_map/teacher_lse/pallas_call | solution.py:156
  48.8 1.9 %collective-permute-start.11 = (f32[8,256]{1,0:T(8,128)S(1)}, f32[8,256]{1,0:T(8,128)S(1)}, u32[]{:S(2)}, u32[]{:S(2)}) collective-permute-start(f32[8,256]{1,0:T(8,128)S(1)} %merge_stats.2.refs_0_), channel_id=1, source_target_pairs={{0,2},{1,3},{2,4},{3,5},{4,6},{5,7},{6,0},{7,1},{8,10},{9,11},{10,... | collective-permute-start | bytes 24584 | tf_op jit(solution)/shard_map/ppermute | solution.py:59
  50.7 1.4 %collective-permute-start.12 = (f32[8,256]{1,0:T(8,128)S(1)}, f32[8,256]{1,0:T(8,128)S(1)}, u32[]{:S(2)}, u32[]{:S(2)}) collective-permute-start(f32[8,256]{1,0:T(8,128)S(1)} %merge_stats.2.refs_0_), channel_id=1, source_target_pairs={{0,6},{1,7},{2,0},{3,1},{4,2},{5,3},{6,4},{7,5},{8,14},{9,15},{10,... | collective-permute-start | bytes 24584 | tf_op jit(solution)/shard_map/ppermute | solution.py:59
  52.1 2.1 %collective-permute-start.13 = (f32[8,256]{1,0:T(8,128)S(1)}, f32[8,256]{1,0:T(8,128)S(1)}, u32[]{:S(2)}, u32[]{:S(2)}) collective-permute-start(f32[8,256]{1,0:T(8,128)S(1)} %merge_stats.2.refs_0_), channel_id=1, source_target_pairs={{0,4},{1,5},{2,6},{3,7},{4,0},{5,1},{6,2},{7,3},{8,12},{9,13},{10,... | collective-permute-start | bytes 24584 | tf_op jit(solution)/shard_map/ppermute | solution.py:59
  54.2 1.9 %collective-permute-done.11.refs_1_ = f32[8,256]{1,0:T(8,128)S(1)} collective-permute-done((f32[8,256]{1,0:T(8,128)S(1)}, f32[8,256]{1,0:T(8,128)S(1)}, u32[]{:S(2)}, u32[]{:S(2)}) %collective-permute-start.11) | collective-permute-done | bytes 8224 | tf_op jit(solution)/shard_map/ppermute | solution.py:59
  56.1 4.0 %collective-permute-done.12.refs_2_ = f32[8,256]{1,0:T(8,128)S(1)} collective-permute-done((f32[8,256]{1,0:T(8,128)S(1)}, f32[8,256]{1,0:T(8,128)S(1)}, u32[]{:S(2)}, u32[]{:S(2)}) %collective-permute-start.12) | collective-permute-done | bytes 8224 | tf_op jit(solution)/shard_map/ppermute | solution.py:59
  60.1 4.7 %collective-permute-start.14 = (f32[8,256]{1,0:T(8,128)S(1)}, f32[8,256]{1,0:T(8,128)S(1)}, u32[]{:S(2)}, u32[]{:S(2)}) collective-permute-start(f32[8,256]{1,0:T(8,128)S(1)} %merge_stats.3.refs_0_), channel_id=1, source_target_pairs={{0,8},{1,9},{2,10},{3,11},{4,12},{5,13},{6,14},{7,15},{8,16},{9,17... | collective-permute-start | bytes 24584 | tf_op jit(solution)/shard_map/ppermute | solution.py:59
  66.2 2.2 %collective-permute-start.16 = (f32[8,256]{1,0:T(8,128)S(1)}, f32[8,256]{1,0:T(8,128)S(1)}, u32[]{:S(2)}, u32[]{:S(2)}) collective-permute-start(f32[8,256]{1,0:T(8,128)S(1)} %merge_stats.3.refs_0_), channel_id=1, source_target_pairs={{0,16},{1,17},{2,18},{3,19},{4,20},{5,21},{6,22},{7,23},{8,24},{9,... | collective-permute-start | bytes 24584 | tf_op jit(solution)/shard_map/ppermute | solution.py:59
  68.5 2.9 %collective-permute-done.16.refs_3_ = f32[8,256]{1,0:T(8,128)S(1)} collective-permute-done((f32[8,256]{1,0:T(8,128)S(1)}, f32[8,256]{1,0:T(8,128)S(1)}, u32[]{:S(2)}, u32[]{:S(2)}) %collective-permute-start.16) | collective-permute-done | bytes 8224 | tf_op jit(solution)/shard_map/ppermute | solution.py:59
  71.4 9.9 %logit_grad.1 = (bf16[256,2432]{1,0:T(8,128)(2,1)S(1)}, bf16[16,128,256]{2,1,0:T(8,128)(2,1)S(1)}, bf16[16,256]{1,0:T(8,128)(2,1)S(1)}, bf16[16,128,2432]{2,1,0:T(8,128)(2,1)S(1)}) custom-call(s32[19]{0:T(128)S(1)} %stack.79.meta_ref, f32[8,256]{1,0:T(8,128)S(1)} %merge_stats.3.refs_0_, f32[8,256]{1,0:T(8,128)S(1)} %collective-permute-done.14.refs_1_, ...), custom_call_target="tpu_custom_call" | custom-call | flops 2550136832 | bytes 19922944 | tf_op jit(solution)/shard_map/logit_grad/pallas_call | solution.py:335
  81.9 2.9 %own_share.1.a_ref = bf16[16,128,256]{2,1,0:T(8,128)(2,1)S(1)} custom-call(bf16[256,2432]{1,0:T(8,128)(2,1)S(1)} %get-tuple-element.18.grad_ref, bf16[16,128,2432]{2,1,0:T(8,128)(2,1)S(1)} %get-tuple-element.19.w_ref), custom_call_target="tpu_custom_call" | custom-call | flops 2550136832 | bytes 9961472 | tf_op jit(solution)/shard_map/own_share/pallas_call | solution.py:368
  85.2 22.6 %all_to_all.29.x_ref = bf16[16,144,256]{2,1,0:T(8,128)(2,1)S(1)} all-to-all(bf16[16,144,256]{2,1,0:T(8,128)(2,1)S(1)} %chip_sum.1), channel_id=1, replica_groups={{0,2,4,6,8,10,12,14,16,18,20,22,24,26,28,30},{1,3,5,7,9,11,13,15,17,19,..., dimensions={0} | all-to-all | bytes 2359296 | tf_op jit(solution)/shard_map/all_to_all | solution.py:472
  (39 shorter events, 8.9 us)
Async XLA Ops:
  0.6 6.9 %collective-permute-start = (bf16[256,128]{1,0:T(8,128)(2,1)}, bf16[256,128]{1,0:T(8,128)(2,1)S(1)}, u32[]{:S(2)}, u32[]{:S(2)}) collective-permute-start(bf16[256,128]{1,0:T(8,128)(2,1)} %param.5), channel_id=1, source_target_pairs={{0,2},{1,3},{2,4},{3,5},{4,6},{5,7},{6,0},{7,1},{8,10},{9,11},{10,... | collective-permute-start | bytes 196616 | tf_op jit(solution)/shard_map/ppermute | solution.py:59
  2.7 4.9 %collective-permute-start.1 = (bf16[256,128]{1,0:T(8,128)(2,1)}, bf16[256,128]{1,0:T(8,128)(2,1)S(1)}, u32[]{:S(2)}, u32[]{:S(2)}) collective-permute-start(bf16[256,128]{1,0:T(8,128)(2,1)} %param.5), channel_id=1, source_target_pairs={{0,6},{1,7},{2,0},{3,1},{4,2},{5,3},{6,4},{7,5},{8,14},{9,15},{10,... | collective-permute-start | bytes 196616 | tf_op jit(solution)/shard_map/ppermute | solution.py:59
  4.9 6.0 %collective-permute-start.2 = (bf16[256,128]{1,0:T(8,128)(2,1)}, bf16[256,128]{1,0:T(8,128)(2,1)S(1)}, u32[]{:S(2)}, u32[]{:S(2)}) collective-permute-start(bf16[256,128]{1,0:T(8,128)(2,1)} %param.5), channel_id=1, source_target_pairs={{0,4},{1,5},{2,6},{3,7},{4,0},{5,1},{6,2},{7,3},{8,12},{9,13},{10,... | collective-permute-start | bytes 196616 | tf_op jit(solution)/shard_map/ppermute | solution.py:59
  10.9 12.8 %collective-permute-start.3 = (bf16[1024,128]{1,0:T(8,128)(2,1)S(1)}, bf16[1024,128]{1,0:T(8,128)(2,1)S(1)}, u32[]{:S(2)}, u32[]{:S(2)}) collective-permute-start(bf16[1024,128]{1,0:T(8,128)(2,1)S(1)} %constant_dynamic-update-slice_fusion.refs_0_), channel_id=1, source_target_pairs={{0,8},{1,9},{2,10},{3,11},{4,12},{5,13},{6,14},{7,15},{8,16},{9,17... | collective-permute-start | bytes 786440 | tf_op jit(solution)/shard_map/ppermute | solution.py:59
  12.5 11.6 %collective-permute-start.4 = (bf16[1024,128]{1,0:T(8,128)(2,1)S(1)}, bf16[1024,128]{1,0:T(8,128)(2,1)S(1)}, u32[]{:S(2)}, u32[]{:S(2)}) collective-permute-start(bf16[1024,128]{1,0:T(8,128)(2,1)S(1)} %constant_dynamic-update-slice_fusion.refs_0_), channel_id=1, source_target_pairs={{0,24},{1,25},{2,26},{3,27},{4,28},{5,29},{6,30},{7,31},{8,0},{9,1... | collective-permute-start | bytes 786440 | tf_op jit(solution)/shard_map/ppermute | solution.py:59
  14.2 11.4 %collective-permute-start.5 = (bf16[1024,128]{1,0:T(8,128)(2,1)S(1)}, bf16[1024,128]{1,0:T(8,128)(2,1)S(1)}, u32[]{:S(2)}, u32[]{:S(2)}) collective-permute-start(bf16[1024,128]{1,0:T(8,128)(2,1)S(1)} %constant_dynamic-update-slice_fusion.refs_0_), channel_id=1, source_target_pairs={{0,16},{1,17},{2,18},{3,19},{4,20},{5,21},{6,22},{7,23},{8,24},{9,... | collective-permute-start | bytes 786440 | tf_op jit(solution)/shard_map/ppermute | solution.py:59
  19.3 20.7 %all-to-all-start = ((bf16[4,64,2432]{2,1,0:T(8,128)(2,1)}), bf16[4,64,2432]{2,1,0:T(8,128)(2,1)}, u32[]{:S(2)}, u32[]{:S(2)}) async-start(bf16[4,64,2432]{2,1,0:T(8,128)(2,1)} %bitcast.20), calls=%async_computation | async-start | bytes 2490368 | tf_op jit(solution)/shard_map/all_to_all | solution.py:454
  23.6 8.7 %collective-permute-start.6 = (bf16[1024,128]{1,0:T(8,128)(2,1)S(1)}, bf16[1024,128]{1,0:T(8,128)(2,1)S(1)}, u32[]{:S(2)}, u32[]{:S(2)}) collective-permute-start(bf16[1024,128]{1,0:T(8,128)(2,1)S(1)} %constant_dynamic-update-slice_fusion.refs_0_), channel_id=1, source_target_pairs={{0,1},{1,0},{2,3},{3,2},{4,5},{5,4},{6,7},{7,6},{8,9},{9,8},{10,11... | collective-permute-start | bytes 786440 | tf_op jit(solution)/shard_map/ppermute | solution.py:55
  23.7 8.7 %collective-permute-start.7 = (bf16[1024,128]{1,0:T(8,128)(2,1)S(1)}, bf16[1024,128]{1,0:T(8,128)(2,1)S(1)}, u32[]{:S(2)}, u32[]{:S(2)}) collective-permute-start(bf16[1024,128]{1,0:T(8,128)(2,1)S(1)} %collective-permute-done.3.refs_1_), channel_id=1, source_target_pairs={{0,1},{1,0},{2,3},{3,2},{4,5},{5,4},{6,7},{7,6},{8,9},{9,8},{10,11... | collective-permute-start | bytes 786440 | tf_op jit(solution)/shard_map/ppermute | solution.py:55
  24.2 8.2 %collective-permute-start.8 = (bf16[1024,128]{1,0:T(8,128)(2,1)S(1)}, bf16[1024,128]{1,0:T(8,128)(2,1)S(1)}, u32[]{:S(2)}, u32[]{:S(2)}) collective-permute-start(bf16[1024,128]{1,0:T(8,128)(2,1)S(1)} %collective-permute-done.4.refs_2_), channel_id=1, source_target_pairs={{0,1},{1,0},{2,3},{3,2},{4,5},{5,4},{6,7},{7,6},{8,9},{9,8},{10,11... | collective-permute-start | bytes 786440 | tf_op jit(solution)/shard_map/ppermute | solution.py:55
  25.6 6.7 %collective-permute-start.9 = (bf16[1024,128]{1,0:T(8,128)(2,1)S(1)}, bf16[1024,128]{1,0:T(8,128)(2,1)S(1)}, u32[]{:S(2)}, u32[]{:S(2)}) collective-permute-start(bf16[1024,128]{1,0:T(8,128)(2,1)S(1)} %collective-permute-done.5.refs_3_), channel_id=1, source_target_pairs={{0,1},{1,0},{2,3},{3,2},{4,5},{5,4},{6,7},{7,6},{8,9},{9,8},{10,11... | collective-permute-start | bytes 786440 | tf_op jit(solution)/shard_map/ppermute | solution.py:55
  39.9 31.4 %all-to-all-start.1 = ((bf16[32,8,2432]{2,1,0:T(8,128)(2,1)}), bf16[32,8,2432]{2,1,0:T(8,128)(2,1)S(1)}, u32[]{:S(2)}, u32[]{:S(2)}) async-start(bf16[32,8,2432]{2,1,0:T(8,128)(2,1)} %bitcast.22), calls=%async_computation.1 | async-start | bytes 2490368 | tf_op jit(solution)/shard_map/all_to_all | solution.py:459
  45.2 26.2 %copy-start = (s32[256]{0:T(256)S(1)}, s32[256]{0:T(256)}, u32[]{:S(2)}) copy-start(s32[256]{0:T(256)} %param.8) | copy-start | bytes 3076
  45.2 26.2 %copy-start.1 = (f32[256]{0:T(256)S(1)}, f32[256]{0:T(256)}, u32[]{:S(2)}) copy-start(f32[256]{0:T(256)} %param.9) | copy-start | bytes 3076
  47.6 1.2 %collective-permute-start.10 = (f32[8,256]{1,0:T(8,128)S(1)}, f32[8,256]{1,0:T(8,128)S(1)}, u32[]{:S(2)}, u32[]{:S(2)}) collective-permute-start(f32[8,256]{1,0:T(8,128)S(1)} %teacher_lse.1.refs_0_), channel_id=1, source_target_pairs={{0,1},{1,0},{2,3},{3,2},{4,5},{5,4},{6,7},{7,6},{8,9},{9,8},{10,11... | collective-permute-start | bytes 24584 | tf_op jit(solution)/shard_map/ppermute | solution.py:55
  48.8 7.3 %collective-permute-start.11 = (f32[8,256]{1,0:T(8,128)S(1)}, f32[8,256]{1,0:T(8,128)S(1)}, u32[]{:S(2)}, u32[]{:S(2)}) collective-permute-start(f32[8,256]{1,0:T(8,128)S(1)} %merge_stats.2.refs_0_), channel_id=1, source_target_pairs={{0,2},{1,3},{2,4},{3,5},{4,6},{5,7},{6,0},{7,1},{8,10},{9,11},{10,... | collective-permute-start | bytes 24584 | tf_op jit(solution)/shard_map/ppermute | solution.py:59
  50.7 9.4 %collective-permute-start.12 = (f32[8,256]{1,0:T(8,128)S(1)}, f32[8,256]{1,0:T(8,128)S(1)}, u32[]{:S(2)}, u32[]{:S(2)}) collective-permute-start(f32[8,256]{1,0:T(8,128)S(1)} %merge_stats.2.refs_0_), channel_id=1, source_target_pairs={{0,6},{1,7},{2,0},{3,1},{4,2},{5,3},{6,4},{7,5},{8,14},{9,15},{10,... | collective-permute-start | bytes 24584 | tf_op jit(solution)/shard_map/ppermute | solution.py:59
  52.1 8.0 %collective-permute-start.13 = (f32[8,256]{1,0:T(8,128)S(1)}, f32[8,256]{1,0:T(8,128)S(1)}, u32[]{:S(2)}, u32[]{:S(2)}) collective-permute-start(f32[8,256]{1,0:T(8,128)S(1)} %merge_stats.2.refs_0_), channel_id=1, source_target_pairs={{0,4},{1,5},{2,6},{3,7},{4,0},{5,1},{6,2},{7,3},{8,12},{9,13},{10,... | collective-permute-start | bytes 24584 | tf_op jit(solution)/shard_map/ppermute | solution.py:59
  60.1 8.2 %collective-permute-start.14 = (f32[8,256]{1,0:T(8,128)S(1)}, f32[8,256]{1,0:T(8,128)S(1)}, u32[]{:S(2)}, u32[]{:S(2)}) collective-permute-start(f32[8,256]{1,0:T(8,128)S(1)} %merge_stats.3.refs_0_), channel_id=1, source_target_pairs={{0,8},{1,9},{2,10},{3,11},{4,12},{5,13},{6,14},{7,15},{8,16},{9,17... | collective-permute-start | bytes 24584 | tf_op jit(solution)/shard_map/ppermute | solution.py:59
  64.8 3.7 %collective-permute-start.15 = (f32[8,256]{1,0:T(8,128)S(1)}, f32[8,256]{1,0:T(8,128)S(1)}, u32[]{:S(2)}, u32[]{:S(2)}) collective-permute-start(f32[8,256]{1,0:T(8,128)S(1)} %merge_stats.3.refs_0_), channel_id=1, source_target_pairs={{0,24},{1,25},{2,26},{3,27},{4,28},{5,29},{6,30},{7,31},{8,0},{9,1... | collective-permute-start | bytes 24584 | tf_op jit(solution)/shard_map/ppermute | solution.py:59
  66.2 5.2 %collective-permute-start.16 = (f32[8,256]{1,0:T(8,128)S(1)}, f32[8,256]{1,0:T(8,128)S(1)}, u32[]{:S(2)}, u32[]{:S(2)}) collective-permute-start(f32[8,256]{1,0:T(8,128)S(1)} %merge_stats.3.refs_0_), channel_id=1, source_target_pairs={{0,16},{1,17},{2,18},{3,19},{4,20},{5,21},{6,22},{7,23},{8,24},{9,... | collective-permute-start | bytes 24584 | tf_op jit(solution)/shard_map/ppermute | solution.py:59
  81.3 3.5 %collective-permute-start.17 = (bf16[16,128,256]{2,1,0:T(8,128)(2,1)S(1)}, bf16[16,128,256]{2,1,0:T(8,128)(2,1)S(1)}, u32[]{:S(2)}, u32[]{:S(2)}) collective-permute-start(bf16[16,128,256]{2,1,0:T(8,128)(2,1)S(1)} %get-tuple-element.20), channel_id=1, source_target_pairs={{0,1},{1,0},{2,3},{3,2},{4,5},{5,4},{6,7},{7,6},{8,9},{9,8},{10,11... | collective-permute-start | bytes 3145736 | tf_op jit(solution)/shard_map/ppermute | solution.py:55
  81.4 3.4 %collective-permute-start.18 = (bf16[16,256]{1,0:T(8,128)(2,1)S(1)}, bf16[16,256]{1,0:T(8,128)(2,1)S(1)}, u32[]{:S(2)}, u32[]{:S(2)}) collective-permute-start(bf16[16,256]{1,0:T(8,128)(2,1)S(1)} %get-tuple-element.21.ta_ref), channel_id=1, source_target_pairs={{0,1},{1,0},{2,3},{3,2},{4,5},{5,4},{6,7},{7,6},{8,9},{9,8},{10,11... | collective-permute-start | bytes 24584 | tf_op jit(solution)/shard_map/ppermute | solution.py:55

commit v3 on v2

--- a/solution.py
+++ b/solution.py
@@ -71,25 +71,6 @@
 def to_row(column):
     n = column.shape[0]
     return jnp.sum(jnp.where(eye(n), column, 0.0), axis=0, keepdims=True)
-
-
-def load_kernel(x_ref, o_ref, sem):
-    copy = pltpu.make_async_copy(x_ref, o_ref, sem)
-    copy.start()
-    copy.wait()
-
-
-def load(x):
-    return pl.pallas_call(
-        load_kernel,
-        in_specs=[HBM],
-        out_specs=VMEM,
-        out_shape=jax.ShapeDtypeStruct(x.shape, x.dtype),
-        scratch_shapes=[pltpu.SemaphoreType.DMA],
-        compiler_params=params(4),
-        cost_estimate=cost(0, 2 * x.size),
-        name="load_head",
-    )(in_hbm(x))
 
 
 def regroup_kernel(x_ref, o_ref, sem):
@@ -119,93 +100,99 @@
     )(teacher_logits)
 
 
-def teacher_lse_kernel(meta_ref, x_ref, stat_ref, o_ref, acc):
-    pairs = x_ref.shape[0] // 16
-
-    def block(i):
-        x = x_ref[pl.ds(pl.multiple_of(i * 16, 16), 16), :].astype(jnp.float32)
-        return x[:8], x[8:]
-
-    first, second = block(0)
-    acc[...] = jnp.maximum(first, second)
-
-    def widen(i, _):
-        a, b = block(i)
-        acc[...] = jnp.maximum(acc[...], jnp.maximum(a, b))
-        return 0
-
-    lax.fori_loop(1, pairs, widen, 0)
-    top = jnp.max(acc[...], axis=1, keepdims=True)
-    acc[...] = jnp.zeros_like(acc)
-
-    def add(i, _):
-        a, b = block(i)
-        acc[...] += jnp.exp(a - top) + jnp.exp(b - top)
-        return 0
-
-    lax.fori_loop(0, pairs, add, 0)
-    lse = top + jnp.log(jnp.sum(acc[...], axis=1, keepdims=True))
-    lane = lax.broadcasted_iota(jnp.int32, o_ref.shape, 1)
-    row = lax.broadcasted_iota(jnp.int32, o_ref.shape, 0)
-    placed = jnp.where(lane == meta_ref[2] * 8 + row, lse, 0.0)
-    o_ref[...] = jnp.where(row == 2, jnp.sum(placed, axis=0, keepdims=True), stat_ref[...])
-
-
-def teacher_lse(rows, meta, stat):
-    n, width = rows.shape
-    return pl.pallas_call(
-        teacher_lse_kernel,
-        in_specs=[SMEM, VMEM, VMEM],
-        out_specs=VMEM,
-        scratch_shapes=[pltpu.VMEM((8, width), jnp.float32)],
-        out_shape=jax.ShapeDtypeStruct((8, n), jnp.float32),
-        compiler_params=params(4),
-        name="teacher_lse",
-    )(meta, rows, stat)
-
-
 ROWS = 32
 BLOCK = 512
+AHEAD = 2
 
 
 def column_blocks(width):
     return [(first, min(BLOCK, width - first)) for first in range(0, width, BLOCK)]
 
 
+def halves(width):
+    last = column_blocks(width)[-1][0]
+    return [pl.ds(0, last), pl.ds(last, width - last)]
+
+
 def student_kernel(meta_ref, *refs):
     own, other = refs[0:RING], refs[RING : 2 * RING]
-    w_ref, s_ref, stat_ref, hidden, logits, sem = refs[2 * RING :]
+    w_ref, t_ref, s_ref, stat_ref, hidden, logits, peaks, totals, t_peaks, t_totals, head_sem, sem, *heads = refs[2 * RING :]
     rows, width = s_ref.shape
     share = own[0].shape[1]
     core = meta_ref[0]
+    blocks = [pl.ds(first, size) for first, size in column_blocks(width)]
+    copies = [
+        pltpu.make_async_copy(w_ref.at[:, cols], heads[k], head_sem.at[k]) for k, cols in enumerate(blocks)
+    ]
+    for copy in copies[:AHEAD]:
+        copy.start()
     for i in range(CHIPS):
         at = slice((i % RING) * rows, (i % RING + 1) * rows)
         chip = meta_ref[3 + i] * 2
         hidden[:, pl.ds(pl.multiple_of((chip + core) * share, share), share)] = own[i // RING][at, :]
         hidden[:, pl.ds(pl.multiple_of((chip + 1 - core) * share, share), share)] = other[i // RING][at, :]
-    peaks, totals, copies = [], [], []
-    for k, (first, size) in enumerate(column_blocks(width)):
-        cols = pl.ds(first, size)
-        s = jnp.dot(hidden[...], w_ref[:, cols], preferred_element_type=jnp.float32)
-        logits[:, cols] = s
-        copies.append(pltpu.make_async_copy(logits.at[:, cols], s_ref.at[:, cols], sem.at[k]))
-        copies[k].start()
-        peaks.append(jnp.max(s, axis=1, keepdims=True))
-        totals.append(jnp.sum(jnp.exp(s - peaks[k]), axis=1, keepdims=True))
-    peak = functools.reduce(jnp.maximum, peaks)
-    total = functools.reduce(jnp.add, [t * jnp.exp(p - peak) for p, t in zip(peaks, totals)])
+    outs = [
+        pltpu.make_async_copy(logits.at[:, cols], s_ref.at[:, cols], sem.at[k]) for k, cols in enumerate(halves(width))
+    ]
+
+    def add(tiles, peak_ref, total_ref, k):
+        peak = functools.reduce(jnp.maximum, tiles)
+        if k > 0:
+            old = peak_ref[...]
+            peak = jnp.maximum(peak, old)
+        total = functools.reduce(jnp.add, [jnp.exp(x - peak) for x in tiles])
+        total_ref[...] = total if k == 0 else total + total_ref[...] * jnp.exp(old - peak)
+        peak_ref[...] = peak
+
+    def tally(k):
+        first, size = column_blocks(width)[k]
+        add([logits[:, j : j + 128] for j in range(first, first + size, 128)], peaks, totals, k)
+
+    def tally_teacher(k):
+        first, size = column_blocks(width)[k]
+        tiles = []
+        for j in range(first, first + size, 128):
+            x = t_ref[:, j : j + 128].astype(jnp.float32).reshape(rows // 8, 8, 128)
+            tiles += [x[i] for i in range(rows // 8)]
+        add(tiles, t_peaks, t_totals, k)
+
+    def across(peak_ref, total_ref):
+        peak = jnp.max(peak_ref[...], axis=1, keepdims=True)
+        return peak, jnp.sum(total_ref[...] * jnp.exp(peak_ref[...] - peak), axis=1, keepdims=True)
+
+    for k, cols in enumerate(blocks):
+        copies[k].wait()
+        if k + AHEAD < len(blocks):
+            copies[k + AHEAD].start()
+        if k + 1 == len(blocks):
+            outs[0].start()
+
+        @pl.when(core >= 0)
+        def _():
+            logits[:, cols] = jnp.dot(hidden[...], heads[k][...], preferred_element_type=jnp.float32)
+            tally_teacher(k)
+            if k > 0:
+                tally(k - 1)
+
+    outs[1].start()
+    tally(len(blocks) - 1)
+    peak, total = across(peaks, totals)
+    t_peak, t_total = across(t_peaks, t_totals)
     row = lax.broadcasted_iota(jnp.int32, stat_ref.shape, 0)
-    stat_ref[...] = jnp.where(row == 0, to_row(peak), jnp.where(row == 1, to_row(total), 0.0))
-    for copy in copies:
-        copy.wait()
-
-
-def student_logits(meta, own, other, head_weight):
+    lane = lax.broadcasted_iota(jnp.int32, stat_ref.shape, 1)
+    lse = jnp.where(lane == meta_ref[2] * 8 + row, t_peak + jnp.log(t_total), 0.0)
+    lse = jnp.sum(lse, axis=0, keepdims=True)
+    stat_ref[...] = jnp.where(row == 0, to_row(peak), jnp.where(row == 1, to_row(total), lse))
+    for out in outs:
+        out.wait()
+
+
+def student_logits(meta, own, other, head_weight, teacher_rows):
     depth, width = head_weight.shape
     rows = own[0].shape[0] // RING
     return pl.pallas_call(
         student_kernel,
-        in_specs=[SMEM] + [VMEM] * (2 * RING + 1),
+        in_specs=[SMEM] + [VMEM] * (2 * RING) + [HBM, VMEM],
         out_specs=[HBM, VMEM],
         out_shape=[
             pltpu.HBM((rows, width), jnp.float32),
@@ -214,12 +201,18 @@
         scratch_shapes=[
             pltpu.VMEM((rows, depth), jnp.bfloat16),
             pltpu.VMEM((rows, width), jnp.float32),
+            pltpu.VMEM((rows, 128), jnp.float32),
+            pltpu.VMEM((rows, 128), jnp.float32),
+            pltpu.VMEM((8, 128), jnp.float32),
+            pltpu.VMEM((8, 128), jnp.float32),
             pltpu.SemaphoreType.DMA((len(column_blocks(width)),)),
-        ],
-        compiler_params=params(12),
+            pltpu.SemaphoreType.DMA((2,)),
+        ]
+        + [pltpu.VMEM((depth, size), jnp.bfloat16) for _, size in column_blocks(width)],
+        compiler_params=params(36),
         cost_estimate=cost(2 * rows * depth * width, 2 * depth * width),
         name="student_logits",
-    )(meta, *own, *other, in_vmem(head_weight))
+    )(meta, *own, *other, in_hbm(head_weight), teacher_rows)
 
 
 def ring_sum(parts):
@@ -256,6 +249,7 @@
 
 
 CHIP_BLOCK = 4
+SECOND = 5
 
 
 def share_matmul(w_ref, grad_ref, part_ref):
@@ -281,6 +275,7 @@
     w_copy = pltpu.make_async_copy(heads.at[:, 1 - meta_ref[0]], head, w_sem)
     own_copy = pltpu.make_async_copy(heads.at[:, meta_ref[0]], own_w_ref, own_sem)
     s_copy.start()
+    w_copy.start()
 
     top, sums, teacher_row = merged([x[...] for x in stats])
     column[:, 0:1] = to_column(top + jnp.log(sums))
@@ -289,7 +284,6 @@
     column[:, 3:4] = to_column(id_ref[...].astype(jnp.float32))
     lane = lax.broadcasted_iota(jnp.int32, (ROWS, 128), 1)
     s_copy.wait()
-    w_copy.start()
 
     def chunk(i, _):
         at = pl.ds(pl.multiple_of(i * ROWS, ROWS), ROWS)
@@ -311,11 +305,15 @@
             grad_ref[at, cols] = grad.astype(jnp.bfloat16)
         cross[at, :] = gap
         picked[at, :] = pick
+
+        @pl.when(i == SECOND)
+        def _():
+            w_copy.wait()
+            own_copy.start()
+
         return 0
 
     lax.fori_loop(0, rows // ROWS, chunk, 0)
-    w_copy.wait()
-    own_copy.start()
     share_matmul(head, grad_ref, part_ref)
 
     gap = to_row(jnp.sum(cross[...], axis=1, keepdims=True))
@@ -447,17 +445,15 @@
     meta = jnp.stack([core, me * width, me] + sources).astype(jnp.int32)
 
     along_z = jnp.concatenate(from_ring(hidden, "dz"), axis=0)
+    blocks = jnp.transpose(teacher_logits, (1, 0, 2)).reshape(rows // 8, -1)
+    blocks = lax.all_to_all(after(blocks, along_z, meta), "tok", 0, 0, tiled=True)
     own = from_ring(along_z, "dy")
-    blocks = jnp.transpose(after(teacher_logits, along_z, meta), (1, 0, 2))
-    blocks = regroup(blocks, width).reshape(rows, width)
-    head = load(after(head_weight, blocks))
-    blocks = lax.all_to_all(blocks, "tok", 0, 0, tiled=True)
+    blocks = regroup(blocks.reshape(-1, 8, blocks.shape[1]), width).reshape(rows, width)
+
     other = [swap_core(x) for x in own]
-    student, stat = student_logits(meta, own, other, head)
-
-    blocks = after(blocks, stat)
+    blocks = after(blocks, *other)
     teacher = lax.all_to_all(blocks, "vocab", 0, 0, tiled=True)
-    stat = teacher_lse(blocks, meta, stat)
+    student, stat = student_logits(meta, own, other, head_weight, blocks)
     stat = merge(stat, swap_core(stat))
     stats = from_ring(merge(*from_ring(stat, "dz")), "dy")
 

time: 109 us -> 106 us (0.972)
  waiting for transfers between devices: 14.5 us -> 20.6 us
  Pallas kernels: 31.9 us -> 25.9 us
  starting transfers between devices: 36.1 us -> 34.3 us
  blocking collectives: 22.6 us -> 21.5 us
    pallas_call x3 -> x1, Pallas kernels: 16.6 us -> 11.5 us  [student_logits(): pl.pallas_call(student_kernel, in_specs=[SMEM] + [VMEM] * (2 * RING) + [H...]
    ppermute x12, waiting for transfers between devices: 13.5 us -> 18.3 us  [from_ring(): lax.ppermute(x, 'vocab', moves(**{axis: d}))]
    ppermute x12, starting transfers between devices: 25 us -> 21.8 us  [from_ring(): lax.ppermute(x, 'vocab', moves(**{axis: d}))]
    unnamed x7 -> x10, local copies, waits for them, and re-layouts: 0.92 us -> 2.79 us
    optimization_barrier x1 -> x0, local copies, waits for them, and re-layouts: 1.66 us -> none  [after(): return lax.optimization_barrier((x,) + others)[0]]
    all_to_all x1, starting transfers between devices: 5.26 us -> 6.81 us  [on_device(): teacher = lax.all_to_all(blocks, 'vocab', 0, 0, tiled=True)]
    all_to_all x1, waiting for transfers between devices: 0.01 us -> 1.41 us  [on_device(): lax.all_to_all(after(blocks, along_z, meta), 'tok', 0, 0, tiled=True)]
    all_to_all x1, blocking collectives: 22.6 us -> 21.5 us  [on_device(): lax.all_to_all(summed.reshape(CHIPS * (share + TAIL), rows), 'vocab', 0,...]
  transfers between devices with their start and end apart: 21 -> 21, of which waited for: 7 -> 11; matrix products, arithmetic and copies ran while one was open for 2% -> 3% of each run, Pallas kernels for 19% -> 15%
where the time goes in v3:
time: 106 us
  starting transfers between devices  34.3 us (32%)
  Pallas kernels  25.9 us (24%)
  blocking collectives  21.5 us (20%)
  waiting for transfers between devices  20.6 us (19%)
  local copies, waits for them, and re-layouts  2.89 us (3%)
    ppermute x12, starting transfers between devices, from_ring(): lax.ppermute(x, 'vocab', moves(**{axis: d}))  21.8 us
    all_to_all x1, blocking collectives, on_device(): lax.all_to_all(summed.reshape(CHIPS * (share + TAIL), rows), 'vocab', 0,...  21.5 us
    ppermute x12, waiting for transfers between devices, from_ring(): lax.ppermute(x, 'vocab', moves(**{axis: d}))  18.3 us
    pallas_call x1, Pallas kernels, student_logits(): pl.pallas_call(student_kernel, in_specs=[SMEM] + [VMEM] * (2 * RING) + [H...  11.5 us
    pallas_call x1, Pallas kernels, logit_grad(): pl.pallas_call(grad_kernel, in_specs=[SMEM] + [VMEM] * RING + [HBM] + [VM...  9.02 us
    all_to_all x1, starting transfers between devices, on_device(): teacher = lax.all_to_all(blocks, 'vocab', 0, 0, tiled=True)  6.81 us
    all_to_all x1, starting transfers between devices, on_device(): lax.all_to_all(after(blocks, along_z, meta), 'tok', 0, 0, tiled=True)  4.3 us
    pallas_call x1, Pallas kernels, own_share(): pl.pallas_call(own_kernel, in_specs=[VMEM, VMEM], out_specs=VMEM, out_sha...  2.9 us
  transfers between devices with their start and end apart: 21, of which 11 were waited for; matrix products, arithmetic and copies ran while one was open for 3% of the time, Pallas kernels for 15%

profile of v3, /device:TPU:0, one launch (start us, length us, event | category | flops | bytes accessed | tf_op | source)
XLA Modules:
  0.0 106.0 jit_solution(6448131210503389174)
XLA Ops:
  0.6 4.2 %collective-permute-start.1 = (bf16[256,128]{1,0:T(8,128)(2,1)}, bf16[256,128]{1,0:T(8,128)(2,1)S(1)}, u32[]{:S(2)}, u32[]{:S(2)}) collective-permute-start(bf16[256,128]{1,0:T(8,128)(2,1)} %param.5), channel_id=1, source_target_pairs={{0,6},{1,7},{2,0},{3,1},{4,2},{5,3},{6,4},{7,5},{8,14},{9,15},{10,... | collective-permute-start | bytes 196616 | tf_op jit(solution)/shard_map/ppermute | solution.py:59
  4.8 1.9 %collective-permute-start.2 = (bf16[256,128]{1,0:T(8,128)(2,1)}, bf16[256,128]{1,0:T(8,128)(2,1)S(1)}, u32[]{:S(2)}, u32[]{:S(2)}) collective-permute-start(bf16[256,128]{1,0:T(8,128)(2,1)} %param.5), channel_id=1, source_target_pairs={{0,4},{1,5},{2,6},{3,7},{4,0},{5,1},{6,2},{7,3},{8,12},{9,13},{10,... | collective-permute-start | bytes 196616 | tf_op jit(solution)/shard_map/ppermute | solution.py:59
  6.7 2.7 %copy.10 = bf16[8,4,19456]{2,0,1:T(8,128)(2,1)} copy(bf16[8,4,19456]{2,1,0:T(4,128)(2,1)} %param.7) | data formatting | bytes 2490368 | tf_op args[2]
  9.5 1.7 %collective-permute-done = bf16[256,128]{1,0:T(8,128)(2,1)S(1)} collective-permute-done((bf16[256,128]{1,0:T(8,128)(2,1)}, bf16[256,128]{1,0:T(8,128)(2,1)S(1)}, u32[]{:S(2)}, u32[]{:S(2)}) %collective-permute-start) | collective-permute-done | bytes 65568 | tf_op jit(solution)/shard_map/ppermute | solution.py:59
  11.3 4.3 %all-to-all-start = ((bf16[4,8,19456]{2,1,0:T(8,128)(2,1)}), bf16[4,8,19456]{2,1,0:T(8,128)(2,1)S(1)}, u32[]{:S(2)}, u32[]{:S(2)}) async-start(bf16[4,8,19456]{2,1,0:T(8,128)(2,1)} %bitcast.21), calls=%async_computation | async-start | bytes 2490368 | tf_op jit(solution)/shard_map/all_to_all | solution.py:449
  15.6 3.2 %collective-permute-start.5 = (bf16[1024,128]{1,0:T(8,128)(2,1)S(1)}, bf16[1024,128]{1,0:T(8,128)(2,1)S(1)}, u32[]{:S(2)}, u32[]{:S(2)}) collective-permute-start(bf16[1024,128]{1,0:T(8,128)(2,1)S(1)} %constant_dynamic-update-slice_fusion.refs_0_), channel_id=1, source_target_pairs={{0,16},{1,17},{2,18},{3,19},{4,20},{5,21},{6,22},{7,23},{8,24},{9,... | collective-permute-start | bytes 786440 | tf_op jit(solution)/shard_map/ppermute | solution.py:59
  18.8 1.1 collective-permute-start.4
  20.8 5.5 %collective-permute-done.5.refs_3_ = bf16[1024,128]{1,0:T(8,128)(2,1)S(1)} collective-permute-done((bf16[1024,128]{1,0:T(8,128)(2,1)S(1)}, bf16[1024,128]{1,0:T(8,128)(2,1)S(1)}, u32[]{:S(2)}, u32[]{:S(2)}) %collective-permute-start.5) | collective-permute-done | bytes 262176 | tf_op jit(solution)/shard_map/ppermute | solution.py:59
  26.3 3.1 %collective-permute-done.4.refs_2_ = bf16[1024,128]{1,0:T(8,128)(2,1)S(1)} collective-permute-done((bf16[1024,128]{1,0:T(8,128)(2,1)S(1)}, bf16[1024,128]{1,0:T(8,128)(2,1)S(1)}, u32[]{:S(2)}, u32[]{:S(2)}) %collective-permute-start.4) | collective-permute-done | bytes 262176 | tf_op jit(solution)/shard_map/ppermute | solution.py:59
  29.9 1.4 %all-to-all-done.x_ref = bf16[4,8,19456]{2,1,0:T(8,128)(2,1)S(1)} async-done(((bf16[4,8,19456]{2,1,0:T(8,128)(2,1)}), bf16[4,8,19456]{2,1,0:T(8,128)(2,1)S(1)}, u32[]{:S(2)}, u32[]{:S(2)}) %all-to-all-start) | async-done | bytes 1245216 | tf_op jit(solution)/shard_map/all_to_all | solution.py:449
  31.3 1.3 %teacher_regroup.1 = bf16[4,8,8,2432]{3,2,1,0:T(8,128)(2,1)} custom-call(bf16[4,8,19456]{2,1,0:T(8,128)(2,1)S(1)} %all-to-all-done.x_ref), custom_call_target="tpu_custom_call" | custom-call | tf_op jit(solution)/shard_map/teacher_regroup/pallas_call | solution.py:92
  32.7 6.8 %all-to-all-start.1 = ((bf16[32,8,2432]{2,1,0:T(8,128)(2,1)}), bf16[32,8,2432]{2,1,0:T(8,128)(2,1)S(1)}, u32[]{:S(2)}, u32[]{:S(2)}) async-start(bf16[32,8,2432]{2,1,0:T(8,128)(2,1)} %bitcast.23), calls=%async_computation.1 | async-start | bytes 2490368 | tf_op jit(solution)/shard_map/all_to_all | solution.py:455
  39.6 11.5 %student_logits.1 = (f32[256,2432]{1,0:T(8,128)}, f32[8,256]{1,0:T(8,128)S(1)}) custom-call(s32[19]{0:T(128)S(1)} %stack.79.meta_ref, bf16[1024,128]{1,0:T(8,128)(2,1)S(1)} %constant_dynamic-update-slice_fusion.refs_0_, bf16[1024,128]{1,0:T(8,128)(2,1)S(1)} %collective-permute-done.3.refs_1_, bf16[1024,128]{1,0:T(8,128)(2,1)S(1)} %collective-permute-done.4.refs_2_, ...), custom_call_target="tpu_custom_call" | custom-call | flops 5100273664 | bytes 19922944 | tf_op jit(solution)/shard_map/student_logits/pallas_call | solution.py:193
  52.4 3.4 %collective-permute-start.13 = (f32[8,256]{1,0:T(8,128)S(1)}, f32[8,256]{1,0:T(8,128)S(1)}, u32[]{:S(2)}, u32[]{:S(2)}) collective-permute-start(f32[8,256]{1,0:T(8,128)S(1)} %merge_stats.2.refs_0_), channel_id=1, source_target_pairs={{0,4},{1,5},{2,6},{3,7},{4,0},{5,1},{6,2},{7,3},{8,12},{9,13},{10,... | collective-permute-start | bytes 24584 | tf_op jit(solution)/shard_map/ppermute | solution.py:59
  55.7 1.2 %collective-permute-start.12 = (f32[8,256]{1,0:T(8,128)S(1)}, f32[8,256]{1,0:T(8,128)S(1)}, u32[]{:S(2)}, u32[]{:S(2)}) collective-permute-start(f32[8,256]{1,0:T(8,128)S(1)} %merge_stats.2.refs_0_), channel_id=1, source_target_pairs={{0,6},{1,7},{2,0},{3,1},{4,2},{5,3},{6,4},{7,5},{8,14},{9,15},{10,... | collective-permute-start | bytes 24584 | tf_op jit(solution)/shard_map/ppermute | solution.py:59
  57.8 1.4 %collective-permute-done.13.refs_3_ = f32[8,256]{1,0:T(8,128)S(1)} collective-permute-done((f32[8,256]{1,0:T(8,128)S(1)}, f32[8,256]{1,0:T(8,128)S(1)}, u32[]{:S(2)}, u32[]{:S(2)}) %collective-permute-start.13) | collective-permute-done | bytes 8224 | tf_op jit(solution)/shard_map/ppermute | solution.py:59
  59.4 2.4 %collective-permute-done.11.refs_1_ = f32[8,256]{1,0:T(8,128)S(1)} collective-permute-done((f32[8,256]{1,0:T(8,128)S(1)}, f32[8,256]{1,0:T(8,128)S(1)}, u32[]{:S(2)}, u32[]{:S(2)}) %collective-permute-start.11) | collective-permute-done | bytes 8224 | tf_op jit(solution)/shard_map/ppermute | solution.py:59
  61.8 3.1 %collective-permute-start.16 = (f32[8,256]{1,0:T(8,128)S(1)}, f32[8,256]{1,0:T(8,128)S(1)}, u32[]{:S(2)}, u32[]{:S(2)}) collective-permute-start(f32[8,256]{1,0:T(8,128)S(1)} %merge_stats.3.refs_0_), channel_id=1, source_target_pairs={{0,16},{1,17},{2,18},{3,19},{4,20},{5,21},{6,22},{7,23},{8,24},{9,... | collective-permute-start | bytes 24584 | tf_op jit(solution)/shard_map/ppermute | solution.py:59
  64.9 1.2 %collective-permute-start.15 = (f32[8,256]{1,0:T(8,128)S(1)}, f32[8,256]{1,0:T(8,128)S(1)}, u32[]{:S(2)}, u32[]{:S(2)}) collective-permute-start(f32[8,256]{1,0:T(8,128)S(1)} %merge_stats.3.refs_0_), channel_id=1, source_target_pairs={{0,24},{1,25},{2,26},{3,27},{4,28},{5,29},{6,30},{7,31},{8,0},{9,1... | collective-permute-start | bytes 24584 | tf_op jit(solution)/shard_map/ppermute | solution.py:59
  67.0 1.5 %collective-permute-done.15.refs_2_ = f32[8,256]{1,0:T(8,128)S(1)} collective-permute-done((f32[8,256]{1,0:T(8,128)S(1)}, f32[8,256]{1,0:T(8,128)S(1)}, u32[]{:S(2)}, u32[]{:S(2)}) %collective-permute-start.15) | collective-permute-done | bytes 8224 | tf_op jit(solution)/shard_map/ppermute | solution.py:59
  68.5 2.4 %collective-permute-done.14.refs_1_ = f32[8,256]{1,0:T(8,128)S(1)} collective-permute-done((f32[8,256]{1,0:T(8,128)S(1)}, f32[8,256]{1,0:T(8,128)S(1)}, u32[]{:S(2)}, u32[]{:S(2)}) %collective-permute-start.14) | collective-permute-done | bytes 8224 | tf_op jit(solution)/shard_map/ppermute | solution.py:59
  70.9 9.0 %logit_grad.1 = (bf16[256,2432]{1,0:T(8,128)(2,1)S(1)}, bf16[16,128,256]{2,1,0:T(8,128)(2,1)S(1)}, bf16[16,256]{1,0:T(8,128)(2,1)S(1)}, bf16[16,128,2432]{2,1,0:T(8,128)(2,1)S(1)}) custom-call(s32[19]{0:T(128)S(1)} %stack.79.meta_ref, f32[8,256]{1,0:T(8,128)S(1)} %merge_stats.3.refs_0_, f32[8,256]{1,0:T(8,128)S(1)} %collective-permute-done.14.refs_1_, ...), custom_call_target="tpu_custom_call" | custom-call | flops 2550136832 | bytes 19922944 | tf_op jit(solution)/shard_map/logit_grad/pallas_call | solution.py:333
  80.5 2.9 %own_share.1.a_ref = bf16[16,128,256]{2,1,0:T(8,128)(2,1)S(1)} custom-call(bf16[256,2432]{1,0:T(8,128)(2,1)S(1)} %get-tuple-element.18.grad_ref, bf16[16,128,2432]{2,1,0:T(8,128)(2,1)S(1)} %get-tuple-element.19.w_ref), custom_call_target="tpu_custom_call" | custom-call | flops 2550136832 | bytes 9961472 | tf_op jit(solution)/shard_map/own_share/pallas_call | solution.py:366
  83.7 21.5 %all_to_all.26.x_ref = bf16[16,144,256]{2,1,0:T(8,128)(2,1)S(1)} all-to-all(bf16[16,144,256]{2,1,0:T(8,128)(2,1)S(1)} %chip_sum.1), channel_id=1, replica_groups={{0,2,4,6,8,10,12,14,16,18,20,22,24,26,28,30},{1,3,5,7,9,11,13,15,17,19,..., dimensions={0} | all-to-all | bytes 2359296 | tf_op jit(solution)/shard_map/all_to_all | solution.py:468
  (39 shorter events, 6.7 us)
Async XLA Ops:
  0.6 10.6 %collective-permute-start.1 = (bf16[256,128]{1,0:T(8,128)(2,1)}, bf16[256,128]{1,0:T(8,128)(2,1)S(1)}, u32[]{:S(2)}, u32[]{:S(2)}) collective-permute-start(bf16[256,128]{1,0:T(8,128)(2,1)} %param.5), channel_id=1, source_target_pairs={{0,6},{1,7},{2,0},{3,1},{4,2},{5,3},{6,4},{7,5},{8,14},{9,15},{10,... | collective-permute-start | bytes 196616 | tf_op jit(solution)/shard_map/ppermute | solution.py:59
  4.8 6.4 %collective-permute-start = (bf16[256,128]{1,0:T(8,128)(2,1)}, bf16[256,128]{1,0:T(8,128)(2,1)S(1)}, u32[]{:S(2)}, u32[]{:S(2)}) collective-permute-start(bf16[256,128]{1,0:T(8,128)(2,1)} %param.5), channel_id=1, source_target_pairs={{0,2},{1,3},{2,4},{3,5},{4,6},{5,7},{6,0},{7,1},{8,10},{9,11},{10,... | collective-permute-start | bytes 196616 | tf_op jit(solution)/shard_map/ppermute | solution.py:59
  4.8 6.5 %collective-permute-start.2 = (bf16[256,128]{1,0:T(8,128)(2,1)}, bf16[256,128]{1,0:T(8,128)(2,1)S(1)}, u32[]{:S(2)}, u32[]{:S(2)}) collective-permute-start(bf16[256,128]{1,0:T(8,128)(2,1)} %param.5), channel_id=1, source_target_pairs={{0,4},{1,5},{2,6},{3,7},{4,0},{5,1},{6,2},{7,3},{8,12},{9,13},{10,... | collective-permute-start | bytes 196616 | tf_op jit(solution)/shard_map/ppermute | solution.py:59
  6.7 2.8 %copy-start.2 = (bf16[256,128]{1,0:T(8,128)(2,1)S(1)}, bf16[256,128]{1,0:T(8,128)(2,1)}, u32[]{:S(2)}) copy-start(bf16[256,128]{1,0:T(8,128)(2,1)} %param.5) | copy-start | bytes 196612
  11.3 20.0 %all-to-all-start = ((bf16[4,8,19456]{2,1,0:T(8,128)(2,1)}), bf16[4,8,19456]{2,1,0:T(8,128)(2,1)S(1)}, u32[]{:S(2)}, u32[]{:S(2)}) async-start(bf16[4,8,19456]{2,1,0:T(8,128)(2,1)} %bitcast.21), calls=%async_computation | async-start | bytes 2490368 | tf_op jit(solution)/shard_map/all_to_all | solution.py:449
  15.6 10.7 %collective-permute-start.5 = (bf16[1024,128]{1,0:T(8,128)(2,1)S(1)}, bf16[1024,128]{1,0:T(8,128)(2,1)S(1)}, u32[]{:S(2)}, u32[]{:S(2)}) collective-permute-start(bf16[1024,128]{1,0:T(8,128)(2,1)S(1)} %constant_dynamic-update-slice_fusion.refs_0_), channel_id=1, source_target_pairs={{0,16},{1,17},{2,18},{3,19},{4,20},{5,21},{6,22},{7,23},{8,24},{9,... | collective-permute-start | bytes 786440 | tf_op jit(solution)/shard_map/ppermute | solution.py:59
  18.8 10.6 %collective-permute-start.4 = (bf16[1024,128]{1,0:T(8,128)(2,1)S(1)}, bf16[1024,128]{1,0:T(8,128)(2,1)S(1)}, u32[]{:S(2)}, u32[]{:S(2)}) collective-permute-start(bf16[1024,128]{1,0:T(8,128)(2,1)S(1)} %constant_dynamic-update-slice_fusion.refs_0_), channel_id=1, source_target_pairs={{0,24},{1,25},{2,26},{3,27},{4,28},{5,29},{6,30},{7,31},{8,0},{9,1... | collective-permute-start | bytes 786440 | tf_op jit(solution)/shard_map/ppermute | solution.py:59
  19.9 9.6 %collective-permute-start.3 = (bf16[1024,128]{1,0:T(8,128)(2,1)S(1)}, bf16[1024,128]{1,0:T(8,128)(2,1)S(1)}, u32[]{:S(2)}, u32[]{:S(2)}) collective-permute-start(bf16[1024,128]{1,0:T(8,128)(2,1)S(1)} %constant_dynamic-update-slice_fusion.refs_0_), channel_id=1, source_target_pairs={{0,8},{1,9},{2,10},{3,11},{4,12},{5,13},{6,14},{7,15},{8,16},{9,17... | collective-permute-start | bytes 786440 | tf_op jit(solution)/shard_map/ppermute | solution.py:59
  20.8 11.8 %collective-permute-start.6 = (bf16[1024,128]{1,0:T(8,128)(2,1)S(1)}, bf16[1024,128]{1,0:T(8,128)(2,1)S(1)}, u32[]{:S(2)}, u32[]{:S(2)}) collective-permute-start(bf16[1024,128]{1,0:T(8,128)(2,1)S(1)} %constant_dynamic-update-slice_fusion.refs_0_), channel_id=1, source_target_pairs={{0,1},{1,0},{2,3},{3,2},{4,5},{5,4},{6,7},{7,6},{8,9},{9,8},{10,11... | collective-permute-start | bytes 786440 | tf_op jit(solution)/shard_map/ppermute | solution.py:55
  26.3 6.4 %collective-permute-start.9 = (bf16[1024,128]{1,0:T(8,128)(2,1)S(1)}, bf16[1024,128]{1,0:T(8,128)(2,1)S(1)}, u32[]{:S(2)}, u32[]{:S(2)}) collective-permute-start(bf16[1024,128]{1,0:T(8,128)(2,1)S(1)} %collective-permute-done.5.refs_3_), channel_id=1, source_target_pairs={{0,1},{1,0},{2,3},{3,2},{4,5},{5,4},{6,7},{7,6},{8,9},{9,8},{10,11... | collective-permute-start | bytes 786440 | tf_op jit(solution)/shard_map/ppermute | solution.py:55
  29.4 3.3 %collective-permute-start.8 = (bf16[1024,128]{1,0:T(8,128)(2,1)S(1)}, bf16[1024,128]{1,0:T(8,128)(2,1)S(1)}, u32[]{:S(2)}, u32[]{:S(2)}) collective-permute-start(bf16[1024,128]{1,0:T(8,128)(2,1)S(1)} %collective-permute-done.4.refs_2_), channel_id=1, source_target_pairs={{0,1},{1,0},{2,3},{3,2},{4,5},{5,4},{6,7},{7,6},{8,9},{9,8},{10,11... | collective-permute-start | bytes 786440 | tf_op jit(solution)/shard_map/ppermute | solution.py:55
  29.4 3.3 %collective-permute-start.7 = (bf16[1024,128]{1,0:T(8,128)(2,1)S(1)}, bf16[1024,128]{1,0:T(8,128)(2,1)S(1)}, u32[]{:S(2)}, u32[]{:S(2)}) collective-permute-start(bf16[1024,128]{1,0:T(8,128)(2,1)S(1)} %collective-permute-done.3.refs_1_), channel_id=1, source_target_pairs={{0,1},{1,0},{2,3},{3,2},{4,5},{5,4},{6,7},{7,6},{8,9},{9,8},{10,11... | collective-permute-start | bytes 786440 | tf_op jit(solution)/shard_map/ppermute | solution.py:55
  32.7 38.2 %all-to-all-start.1 = ((bf16[32,8,2432]{2,1,0:T(8,128)(2,1)}), bf16[32,8,2432]{2,1,0:T(8,128)(2,1)S(1)}, u32[]{:S(2)}, u32[]{:S(2)}) async-start(bf16[32,8,2432]{2,1,0:T(8,128)(2,1)} %bitcast.23), calls=%async_computation.1 | async-start | bytes 2490368 | tf_op jit(solution)/shard_map/all_to_all | solution.py:455
  39.5 31.3 %copy-start = (s32[256]{0:T(256)S(1)}, s32[256]{0:T(256)}, u32[]{:S(2)}) copy-start(s32[256]{0:T(256)} %param.8) | copy-start | bytes 3076
  39.6 31.3 %copy-start.1 = (f32[256]{0:T(256)S(1)}, f32[256]{0:T(256)}, u32[]{:S(2)}) copy-start(f32[256]{0:T(256)} %param.9) | copy-start | bytes 3076
  51.1 1.3 %collective-permute-start.10 = (f32[8,256]{1,0:T(8,128)S(1)}, f32[8,256]{1,0:T(8,128)S(1)}, u32[]{:S(2)}, u32[]{:S(2)}) collective-permute-start(f32[8,256]{1,0:T(8,128)S(1)} %get-tuple-element.16.refs_0_), channel_id=1, source_target_pairs={{0,1},{1,0},{2,3},{3,2},{4,5},{5,4},{6,7},{7,6},{8,9},{9,8},{10,11... | collective-permute-start | bytes 24584 | tf_op jit(solution)/shard_map/ppermute | solution.py:55
  52.4 6.8 %collective-permute-start.13 = (f32[8,256]{1,0:T(8,128)S(1)}, f32[8,256]{1,0:T(8,128)S(1)}, u32[]{:S(2)}, u32[]{:S(2)}) collective-permute-start(f32[8,256]{1,0:T(8,128)S(1)} %merge_stats.2.refs_0_), channel_id=1, source_target_pairs={{0,4},{1,5},{2,6},{3,7},{4,0},{5,1},{6,2},{7,3},{8,12},{9,13},{10,... | collective-permute-start | bytes 24584 | tf_op jit(solution)/shard_map/ppermute | solution.py:59
  55.7 3.7 %collective-permute-start.12 = (f32[8,256]{1,0:T(8,128)S(1)}, f32[8,256]{1,0:T(8,128)S(1)}, u32[]{:S(2)}, u32[]{:S(2)}) collective-permute-start(f32[8,256]{1,0:T(8,128)S(1)} %merge_stats.2.refs_0_), channel_id=1, source_target_pairs={{0,6},{1,7},{2,0},{3,1},{4,2},{5,3},{6,4},{7,5},{8,14},{9,15},{10,... | collective-permute-start | bytes 24584 | tf_op jit(solution)/shard_map/ppermute | solution.py:59
  56.9 4.9 %collective-permute-start.11 = (f32[8,256]{1,0:T(8,128)S(1)}, f32[8,256]{1,0:T(8,128)S(1)}, u32[]{:S(2)}, u32[]{:S(2)}) collective-permute-start(f32[8,256]{1,0:T(8,128)S(1)} %merge_stats.2.refs_0_), channel_id=1, source_target_pairs={{0,2},{1,3},{2,4},{3,5},{4,6},{5,7},{6,0},{7,1},{8,10},{9,11},{10,... | collective-permute-start | bytes 24584 | tf_op jit(solution)/shard_map/ppermute | solution.py:59
  61.8 5.2 %collective-permute-start.16 = (f32[8,256]{1,0:T(8,128)S(1)}, f32[8,256]{1,0:T(8,128)S(1)}, u32[]{:S(2)}, u32[]{:S(2)}) collective-permute-start(f32[8,256]{1,0:T(8,128)S(1)} %merge_stats.3.refs_0_), channel_id=1, source_target_pairs={{0,16},{1,17},{2,18},{3,19},{4,20},{5,21},{6,22},{7,23},{8,24},{9,... | collective-permute-start | bytes 24584 | tf_op jit(solution)/shard_map/ppermute | solution.py:59
  64.9 3.7 %collective-permute-start.15 = (f32[8,256]{1,0:T(8,128)S(1)}, f32[8,256]{1,0:T(8,128)S(1)}, u32[]{:S(2)}, u32[]{:S(2)}) collective-permute-start(f32[8,256]{1,0:T(8,128)S(1)} %merge_stats.3.refs_0_), channel_id=1, source_target_pairs={{0,24},{1,25},{2,26},{3,27},{4,28},{5,29},{6,30},{7,31},{8,0},{9,1... | collective-permute-start | bytes 24584 | tf_op jit(solution)/shard_map/ppermute | solution.py:59
  66.0 4.9 %collective-permute-start.14 = (f32[8,256]{1,0:T(8,128)S(1)}, f32[8,256]{1,0:T(8,128)S(1)}, u32[]{:S(2)}, u32[]{:S(2)}) collective-permute-start(f32[8,256]{1,0:T(8,128)S(1)} %merge_stats.3.refs_0_), channel_id=1, source_target_pairs={{0,8},{1,9},{2,10},{3,11},{4,12},{5,13},{6,14},{7,15},{8,16},{9,17... | collective-permute-start | bytes 24584 | tf_op jit(solution)/shard_map/ppermute | solution.py:59
  79.9 3.5 %collective-permute-start.17 = (bf16[16,128,256]{2,1,0:T(8,128)(2,1)S(1)}, bf16[16,128,256]{2,1,0:T(8,128)(2,1)S(1)}, u32[]{:S(2)}, u32[]{:S(2)}) collective-permute-start(bf16[16,128,256]{2,1,0:T(8,128)(2,1)S(1)} %get-tuple-element.20), channel_id=1, source_target_pairs={{0,1},{1,0},{2,3},{3,2},{4,5},{5,4},{6,7},{7,6},{8,9},{9,8},{10,11... | collective-permute-start | bytes 3145736 | tf_op jit(solution)/shard_map/ppermute | solution.py:55
  80.0 3.4 %collective-permute-start.18 = (bf16[16,256]{1,0:T(8,128)(2,1)S(1)}, bf16[16,256]{1,0:T(8,128)(2,1)S(1)}, u32[]{:S(2)}, u32[]{:S(2)}) collective-permute-start(bf16[16,256]{1,0:T(8,128)(2,1)S(1)} %get-tuple-element.21.ta_ref), channel_id=1, source_target_pairs={{0,1},{1,0},{2,3},{3,2},{4,5},{5,4},{6,7},{7,6},{8,9},{9,8},{10,11... | collective-permute-start | bytes 24584 | tf_op jit(solution)/shard_map/ppermute | solution.py:55

commit v4 on v3

v4 whole, which is shorter than its diff:
```python
import functools

import jax
import jax.numpy as jnp
from jax import lax
from jax.experimental import pallas as pl
from jax.experimental.pallas import tpu as pltpu
from jax.sharding import PartitionSpec as P

CE_WEIGHT = 0.5
RING = 4
CHIPS = RING * RING
SHIFTS = (0, 1, -1, 2)
MIB = 1 << 20
SMEM = pl.BlockSpec(memory_space=pltpu.SMEM)
VMEM = pl.BlockSpec(memory_space=pltpu.VMEM)
HBM = pl.BlockSpec(memory_space=pltpu.HBM)
TAIL = 16


def params(limit):
    return pltpu.CompilerParams(vmem_limit_bytes=limit * MIB)


def cost(flops, read):
    return pl.CostEstimate(flops=flops, bytes_accessed=read, transcendentals=0)


def in_vmem(x):
    return pltpu.with_memory_space_constraint(x, pltpu.VMEM)


def in_hbm(x):
    return pltpu.with_memory_space_constraint(x, pltpu.HBM)


def after(x, *others):
    return lax.optimization_barrier((x,) + others)[0]


def member(y, z, core):
    return ((y % RING) * RING + z % RING) * 2 + core % 2


def moves(dy=0, dz=0, dcore=0):
    return [
        (member(y, z, c), member(y + dy, z + dz, c + dcore))
        for y in range(RING)
        for z in range(RING)
        for c in range(2)
    ]


def swap_core(x):
    return lax.ppermute(x, "vocab", moves(dcore=1))


def from_ring(x, axis):
    return [x] + [lax.ppermute(x, "vocab", moves(**{axis: d})) for d in SHIFTS[1:]]


def eye(n):
    return lax.broadcasted_iota(jnp.int32, (n, n), 0) == lax.broadcasted_iota(jnp.int32, (n, n), 1)


def to_column(row):
    n = row.shape[1]
    return jnp.sum(jnp.where(eye(n), row, 0.0), axis=1, keepdims=True)


def to_row(column):
    n = column.shape[0]
    return jnp.sum(jnp.where(eye(n), column, 0.0), axis=0, keepdims=True)


ROWS = 32
BLOCK = 512
AHEAD = 2


def column_blocks(width):
    return [(first, min(BLOCK, width - first)) for first in range(0, width, BLOCK)]


def parts_of(x, count):
    parts = []
    for _ in range(count):
        parts.append(x.astype(jnp.bfloat16).astype(jnp.float32))
        x = x - parts[-1]
    return parts


def student_kernel(meta_ref, *refs):
    blocks = column_blocks(refs[2 * RING + 2].shape[1])
    n = len(blocks)
    own, other = refs[0:RING], refs[RING : 2 * RING]
    w_ref, x_ref, s_ref, send_ref = refs[2 * RING : 2 * RING + 4]
    heads = refs[2 * RING + 4 : 2 * RING + 4 + n]
    hidden, peaks, totals, t_peaks, t_totals, sem = refs[2 * RING + 4 + n :]
    rows, width = s_ref.shape
    tiles_x, shards = x_ref.shape[0], x_ref.shape[2] // width
    share = own[0].shape[1]
    core = meta_ref[0]
    copies = [
        pltpu.make_async_copy(w_ref.at[:, pl.ds(first, size)], heads[k], sem.at[k])
        for k, (first, size) in enumerate(blocks)
    ]
    for copy in copies[:AHEAD]:
        copy.start()
    for i in range(CHIPS):
        at = slice((i % RING) * rows, (i % RING + 1) * rows)
        chip = meta_ref[3 + i] * 2
        hidden[:, pl.ds(pl.multiple_of((chip + core) * share, share), share)] = own[i // RING][at, :]
        hidden[:, pl.ds(pl.multiple_of((chip + 1 - core) * share, share), share)] = other[i // RING][at, :]

    def add(tiles, peak_ref, total_ref, k):
        peak = functools.reduce(jnp.maximum, tiles)
        if k > 0:
            old = peak_ref[...]
            peak = jnp.maximum(peak, old)
        total = functools.reduce(jnp.add, [jnp.exp(x - peak) for x in tiles])
        total_ref[...] = total if k == 0 else total + total_ref[...] * jnp.exp(old - peak)
        peak_ref[...] = peak

    def tally(k):
        first, size = blocks[k]
        add([s_ref[:, j : j + 128] for j in range(first, first + size, 128)], peaks, totals, k)

    def tally_teacher(k):
        first, size = blocks[k]
        tiles = []
        for i in range(tiles_x):
            for j in range(shards):
                x = x_ref[i, :, j * width + first : j * width + first + size]
                send_ref[i * shards + j, :, first : first + size] = x
                x = x.astype(jnp.float32)
                tiles += [x[:, c : c + 128] for c in range(0, size, 128)]
        add(tiles, t_peaks, t_totals, k)

    for k, (first, size) in enumerate(blocks):
        copies[k].wait()
        if k + AHEAD < n:
            copies[k + AHEAD].start()

        @pl.when(core >= 0)
        def _():
            s_ref[:, first : first + size] = jnp.dot(
                hidden[...], heads[k][...], preferred_element_type=jnp.float32
            )
            tally_teacher(k)
            if k > 0:
                tally(k - 1)

    tally(n - 1)
    peak = parts_of(jnp.max(peaks[...], axis=1, keepdims=True), 2)
    total = jnp.sum(totals[...] * jnp.exp(peaks[...] - (peak[0] + peak[1])), axis=1, keepdims=True)
    t_peak = jnp.max(t_peaks[...], axis=1, keepdims=True)
    t_total = jnp.sum(t_totals[...] * jnp.exp(t_peaks[...] - t_peak), axis=1, keepdims=True)
    row = lax.broadcasted_iota(jnp.int32, (8, rows), 0)
    lane = lax.broadcasted_iota(jnp.int32, (8, rows), 1)
    lse = jnp.where(lane == meta_ref[2] * 8 + row, t_peak + jnp.log(t_total), 0.0)
    lse = jnp.sum(lse, axis=0, keepdims=True)
    lines = [to_row(x) for x in peak] + parts_of(to_row(total), 3) + parts_of(lse, 3)
    stat = jnp.zeros((8, rows), jnp.float32)
    for k, line in enumerate(lines):
        stat = jnp.where(row == k, line, stat)
    stat = stat.astype(jnp.bfloat16)
    for i in range(send_ref.shape[0]):
        send_ref[i, :, width:] = stat


def student_logits(meta, own, other, head_weight, teacher_rows):
    depth, width = head_weight.shape
    rows = own[0].shape[0] // RING
    blocks = column_blocks(width)
    return pl.pallas_call(
        student_kernel,
        in_specs=[SMEM] + [VMEM] * (2 * RING) + [HBM, VMEM],
        out_specs=[VMEM] * (2 + len(blocks)),
        out_shape=[
            jax.ShapeDtypeStruct((rows, width), jnp.float32),
            jax.ShapeDtypeStruct((2 * CHIPS, 8, width + rows), jnp.bfloat16),
        ]
        + [jax.ShapeDtypeStruct((depth, size), jnp.bfloat16) for _, size in blocks],
        scratch_shapes=[
            pltpu.VMEM((rows, depth), jnp.bfloat16),
            pltpu.VMEM((rows, 128), jnp.float32),
            pltpu.VMEM((rows, 128), jnp.float32),
            pltpu.VMEM((8, 128), jnp.float32),
            pltpu.VMEM((8, 128), jnp.float32),
            pltpu.SemaphoreType.DMA((len(blocks),)),
        ],
        compiler_params=params(10),
        cost_estimate=cost(2 * rows * depth * width, 2 * depth * width),
        name="student_logits",
    )(meta, *own, *other, in_hbm(head_weight), teacher_rows)


def merged(stats):
    peaks = [x[0:1] + x[1:2] for x in stats]
    top = functools.reduce(jnp.maximum, peaks)
    total = functools.reduce(
        jnp.add, [((x[2:3] + x[3:4]) + x[4:5]) * jnp.exp(p - top) for x, p in zip(stats, peaks)]
    )
    return top + jnp.log(total), functools.reduce(jnp.add, [(x[5:6] + x[6:7]) + x[7:8] for x in stats])


def head_rows(head, core, chips):
    depth, size = head.shape
    share = depth // CHIPS // 2
    return head.reshape(CHIPS, 2, share, size)[chips, core].reshape(-1, size)


def grad_kernel(meta_ref, x_ref, s_ref, id_ref, weight_ref, *refs):
    blocks = column_blocks(s_ref.shape[1])
    heads = refs[: len(blocks)]
    grad_ref, part_ref, tail_ref, column, cross, picked, total = refs[len(blocks) :]
    rows, width = s_ref.shape
    stats = [x_ref[i, :, width:].astype(jnp.float32) for i in range(x_ref.shape[0])]
    student_row, teacher_row = merged(stats)
    column[:, 0:1] = to_column(student_row)
    column[:, 1:2] = to_column(teacher_row)
    column[:, 2:3] = to_column(weight_ref[...])
    column[:, 3:4] = to_column(id_ref[...].astype(jnp.float32))
    lane = lax.broadcasted_iota(jnp.int32, (ROWS, 128), 1)

    for k, (first, size) in enumerate(blocks):
        for r in range(0, rows, ROWS):
            at = slice(r, r + ROWS)
            student_lse, teacher_lse, weight = column[at, 0:1], column[at, 1:2], column[at, 2:3]
            target = column[at, 3:4].astype(jnp.int32) - meta_ref[1]
            gap = jnp.zeros((ROWS, 128), jnp.float32) if k == 0 else cross[at, :]
            pick = jnp.zeros((ROWS, 128), jnp.float32) if k == 0 else picked[at, :]
            for j in range(first, first + size, 128):
                cols = slice(j, j + 128)
                student_logp = s_ref[at, cols] - student_lse
                teacher = x_ref[r // 8 : (r + ROWS) // 8, :, cols].astype(jnp.float32).reshape(ROWS, 128)
                teacher_logp = teacher - teacher_lse
                student_prob = jnp.exp(student_logp)
                teacher_prob = jnp.exp(teacher_logp)
                hit = lane == target - j
                onehot = jnp.where(hit, 1.0, 0.0)
                gap += teacher_prob * (teacher_logp - student_logp)
                pick += jnp.where(hit, -student_logp, 0.0)
                grad = weight * ((student_prob - teacher_prob) + CE_WEIGHT * (student_prob - onehot))
                grad_ref[at, cols] = grad.astype(jnp.bfloat16)
            cross[at, :] = gap
            picked[at, :] = pick
        out = lax.dot_general(
            head_rows(heads[k], 1 - meta_ref[0], slice(0, CHIPS)),
            grad_ref[:, first : first + size],
            (((1,), (1,)), ((), ())),
            preferred_element_type=jnp.float32,
        )
        if k == 0:
            total[...] = out
        elif k + 1 < len(blocks):
            total[...] += out
        else:
            part_ref[...] = (total[...] + out).astype(jnp.bfloat16).reshape(part_ref.shape)

    gap = to_row(jnp.sum(cross[...], axis=1, keepdims=True))
    pick = to_row(jnp.sum(picked[...], axis=1, keepdims=True))
    row = lax.broadcasted_iota(jnp.int32, tail_ref.shape, 0)
    tail = jnp.zeros(tail_ref.shape, jnp.float32)
    for k, line in enumerate(parts_of(gap, 3) + parts_of(pick, 3)):
        tail = jnp.where(row == k, line, tail)
    tail_ref[...] = tail.astype(jnp.bfloat16)


def logit_grad(meta, teacher, student, ids, weights, heads):
    rows, width = student.shape
    depth = heads[0].shape[0]
    share = depth // CHIPS // 2
    return pl.pallas_call(
        grad_kernel,
        in_specs=[SMEM] + [VMEM] * (4 + len(heads)),
        out_specs=[VMEM] * 3,
        out_shape=[
            jax.ShapeDtypeStruct((rows, width), jnp.bfloat16),
            jax.ShapeDtypeStruct((CHIPS, share, rows), jnp.bfloat16),
            jax.ShapeDtypeStruct((TAIL, rows), jnp.bfloat16),
        ],
        scratch_shapes=[
            pltpu.VMEM((rows, 128), jnp.float32),
            pltpu.VMEM((rows, 128), jnp.float32),
            pltpu.VMEM((rows, 128), jnp.float32),
            pltpu.VMEM((CHIPS * share, rows), jnp.float32),
        ],
        compiler_params=params(14),
        cost_estimate=cost(rows * depth * width, depth * width),
        name="logit_grad",
    )(meta, teacher, student, ids, weights, *[in_vmem(x) for x in heads])


CHIP_BLOCK = 4


def own_kernel(meta_ref, grad_ref, *refs):
    heads, part_ref = refs[:-1], refs[-1]
    chips, share, rows = part_ref.shape
    for i in range(0, chips, CHIP_BLOCK):
        total = 0.0
        for k, (first, size) in enumerate(column_blocks(grad_ref.shape[1])):
            total += lax.dot_general(
                head_rows(heads[k], meta_ref[0], slice(i, i + CHIP_BLOCK)),
                grad_ref[:, first : first + size],
                (((1,), (1,)), ((), ())),
                preferred_element_type=jnp.float32,
            )
        part_ref[i : i + CHIP_BLOCK] = total.astype(jnp.bfloat16).reshape(CHIP_BLOCK, share, rows)


def own_share(meta, grad, heads):
    rows, width = grad.shape
    depth = heads[0].shape[0]
    share = depth // CHIPS // 2
    return pl.pallas_call(
        own_kernel,
        in_specs=[SMEM] + [VMEM] * (1 + len(heads)),
        out_specs=VMEM,
        out_shape=jax.ShapeDtypeStruct((CHIPS, share, rows), jnp.bfloat16),
        compiler_params=params(8),
        cost_estimate=cost(rows * depth * width, depth * width),
        name="own_share",
    )(meta, grad, *[in_vmem(x) for x in heads])


def join_kernel(a_ref, b_ref, ta_ref, tb_ref, o_ref):
    share = a_ref.shape[1]
    total = a_ref[...].astype(jnp.float32) + b_ref[...].astype(jnp.float32)
    o_ref[:, 0:share, :] = total.astype(jnp.bfloat16)
    tail = jnp.concatenate(
        [ta_ref[...].astype(jnp.float32)[0 : TAIL // 2], tb_ref[...].astype(jnp.float32)[0 : TAIL // 2]]
    ).astype(jnp.bfloat16)
    for i in range(o_ref.shape[0]):
        o_ref[i, share : share + TAIL, :] = tail


def join(a, b, tail_a, tail_b):
    chips, share, rows = a.shape
    block = pl.BlockSpec((CHIP_BLOCK, share, rows), lambda i: (i, 0, 0))
    tail = pl.BlockSpec((TAIL, rows), lambda i: (0, 0))
    return pl.pallas_call(
        join_kernel,
        grid=(chips // CHIP_BLOCK,),
        in_specs=[block, block, tail, tail],
        out_specs=pl.BlockSpec((CHIP_BLOCK, share + TAIL, rows), lambda i: (i, 0, 0)),
        out_shape=jax.ShapeDtypeStruct((chips, share + TAIL, rows), jnp.bfloat16),
        compiler_params=params(16),
        name="chip_sum",
    )(a, b, tail_a, tail_b)


def final_kernel(x_ref, div_ref, ce_ref, o_ref):
    chips = x_ref.shape[0]
    share = x_ref.shape[1] - TAIL
    total = x_ref[0, 0:share, :].astype(jnp.float32)
    for i in range(1, chips):
        total += x_ref[i, 0:share, :].astype(jnp.float32)
    o_ref[...] = total.astype(jnp.bfloat16)
    div = jnp.zeros(div_ref.shape, jnp.float32)
    ce = jnp.zeros(ce_ref.shape, jnp.float32)
    for i in range(chips):
        tail = x_ref[i, share : share + TAIL, :].astype(jnp.float32)
        line = lambda k: tail[k : k + 1]
        value = lambda k: (line(k) + line(k + 1)) + line(k + 2)
        half = TAIL // 2
        div += value(0) + value(half)
        ce += value(3) + value(half + 3)
    div_ref[...] = div
    ce_ref[...] = ce


def final(blocks):
    chips, height, rows = blocks.shape
    return pl.pallas_call(
        final_kernel,
        out_shape=[
            jax.ShapeDtypeStruct((1, rows), jnp.float32),
            jax.ShapeDtypeStruct((1, rows), jnp.float32),
            jax.ShapeDtypeStruct((height - TAIL, rows), jnp.bfloat16),
        ],
        compiler_params=params(16),
        name="final_sum",
    )(blocks)


def on_device(hidden, head_weight, teacher_logits, token_ids, token_weight):
    rows, share = hidden.shape
    depth, width = head_weight.shape
    me = lax.axis_index("vocab")
    core, chip = me % 2, me // 2
    y, z = chip // RING, chip % RING
    sources = [((y - dy) % RING) * RING + (z - dz) % RING for dy in SHIFTS for dz in SHIFTS]

    meta = jnp.stack([core, me * width, me] + sources).astype(jnp.int32)

    along_z = jnp.concatenate(from_ring(hidden, "dz"), axis=0)
    blocks = jnp.transpose(teacher_logits, (1, 0, 2)).reshape(rows // 8, -1)
    blocks = lax.all_to_all(after(blocks, along_z, meta), "tok", 0, 0, tiled=True)
    own = from_ring(along_z, "dy")
    other = [swap_core(x) for x in own]
    student, send, *heads = student_logits(
        meta, own, other, head_weight, blocks.reshape(-1, 8, blocks.shape[1])
    )

    teacher = lax.all_to_all(send, "vocab", 0, 0, tiled=True)
    grad, part, tail = logit_grad(
        meta, teacher, student, token_ids.reshape(1, rows), token_weight.reshape(1, rows), heads
    )
    from_core, from_tail = swap_core(part), swap_core(tail)
    mine = own_share(meta, grad, heads)
    summed = join(mine, from_core, tail, from_tail)

    same_core = [[member(i // RING, i % RING, c) for i in range(CHIPS)] for c in range(2)]
    blocks = lax.all_to_all(
        summed.reshape(CHIPS * (share + TAIL), rows), "vocab", 0, 0, axis_index_groups=same_core, tiled=True
    )
    divergence, cross_entropy, hidden_grad = final(blocks.reshape(CHIPS, share + TAIL, rows))
    return divergence.reshape(rows), cross_entropy.reshape(rows), hidden_grad


def solution(mesh):
    return jax.shard_map(
        on_device,
        mesh=mesh,
        in_specs=(P("tok", "vocab"), P(None, "vocab"), P("vocab", None, "tok"), P("tok"), P("tok")),
        out_specs=(P("tok"), P("tok"), P("vocab", "tok")),
        check_vma=False,
    )
```

time: 106 us -> 102 us (0.962)
  blocking collectives: 21.5 us -> 49.2 us
  starting transfers between devices: 34.3 us -> 16.8 us
  waiting for transfers between devices: 20.6 us -> 11.7 us
  Pallas kernels: 25.9 us -> 20.5 us
    all_to_all x0 -> x1, blocking collectives: none -> 27.2 us  [on_device(): teacher = lax.all_to_all(send, 'vocab', 0, 0, tiled=True)]
    ppermute x12 -> x6, starting transfers between devices: 21.8 us -> 11.3 us  [from_ring(): lax.ppermute(x, 'vocab', moves(**{axis: d}))]
    ppermute x12 -> x6, waiting for transfers between devices: 18.3 us -> 10.3 us  [from_ring(): lax.ppermute(x, 'vocab', moves(**{axis: d}))]
    all_to_all x1 -> x0, starting transfers between devices: 6.81 us -> none  [on_device(): teacher = lax.all_to_all(blocks, 'vocab', 0, 0, tiled=True)]
    pallas_call x5 -> x2, Pallas kernels: 13.3 us -> 8.87 us  [the longest x1 5.44 us: logit_grad(): pl.pallas_call(grad_kernel, in_specs=[SMEM] + [VMEM] * (4 + len(heads)),...]
    all_to_all x1, waiting for transfers between devices: 1.41 us -> 0.02 us  [on_device(): lax.all_to_all(after(blocks, along_z, meta), 'tok', 0, 0, tiled=True)]
  transfers between devices with their start and end apart: 21 -> 13, of which waited for: 11 -> 5; matrix products, arithmetic and copies ran while one was open for 3% -> 3% of each run, Pallas kernels for 15% -> 3%
where the time goes in v4:
time: 102 us
  blocking collectives  49.2 us (48%)
  Pallas kernels  20.5 us (20%)
  starting transfers between devices  16.8 us (16%)
  waiting for transfers between devices  11.7 us (11%)
  local copies, waits for them, and re-layouts  2.9 us (3%)
    all_to_all x1, blocking collectives, on_device(): teacher = lax.all_to_all(send, 'vocab', 0, 0, tiled=True)  27.2 us
    all_to_all x1, blocking collectives, on_device(): lax.all_to_all(summed.reshape(CHIPS * (share + TAIL), rows), 'vocab', 0,...  22 us
    ppermute x6, starting transfers between devices, from_ring(): lax.ppermute(x, 'vocab', moves(**{axis: d}))  11.3 us
    pallas_call x1, Pallas kernels, student_logits(): pl.pallas_call(student_kernel, in_specs=[SMEM] + [VMEM] * (2 * RING) + [H...  10.5 us
    ppermute x6, waiting for transfers between devices, from_ring(): lax.ppermute(x, 'vocab', moves(**{axis: d}))  10.3 us
    pallas_call x1, Pallas kernels, logit_grad(): pl.pallas_call(grad_kernel, in_specs=[SMEM] + [VMEM] * (4 + len(heads)),...  5.44 us
    all_to_all x1, starting transfers between devices, on_device(): lax.all_to_all(after(blocks, along_z, meta), 'tok', 0, 0, tiled=True)  4.3 us
    pallas_call x1, Pallas kernels, own_share(): pl.pallas_call(own_kernel, in_specs=[SMEM] + [VMEM] * (1 + len(heads)), o...  3.44 us
  transfers between devices with their start and end apart: 13, of which 5 were waited for; matrix products, arithmetic and copies ran while one was open for 3% of the time, Pallas kernels for 3%

profile of v4, /device:TPU:0, one launch (start us, length us, event | category | flops | bytes accessed | tf_op | source)
XLA Modules:
  0.0 101.9 jit_solution(8422574592030285836)
XLA Ops:
  0.6 4.2 %collective-permute-start.1 = (bf16[256,128]{1,0:T(8,128)(2,1)}, bf16[256,128]{1,0:T(8,128)(2,1)S(1)}, u32[]{:S(2)}, u32[]{:S(2)}) collective-permute-start(bf16[256,128]{1,0:T(8,128)(2,1)} %param.5), channel_id=1, source_target_pairs={{0,6},{1,7},{2,0},{3,1},{4,2},{5,3},{6,4},{7,5},{8,14},{9,15},{10,... | collective-permute-start | bytes 196616 | tf_op jit(solution)/shard_map/ppermute | solution.py:59
  4.8 1.9 %collective-permute-start.2 = (bf16[256,128]{1,0:T(8,128)(2,1)}, bf16[256,128]{1,0:T(8,128)(2,1)S(1)}, u32[]{:S(2)}, u32[]{:S(2)}) collective-permute-start(bf16[256,128]{1,0:T(8,128)(2,1)} %param.5), channel_id=1, source_target_pairs={{0,4},{1,5},{2,6},{3,7},{4,0},{5,1},{6,2},{7,3},{8,12},{9,13},{10,... | collective-permute-start | bytes 196616 | tf_op jit(solution)/shard_map/ppermute | solution.py:59
  6.7 2.7 %copy.10 = bf16[8,4,19456]{2,0,1:T(8,128)(2,1)} copy(bf16[8,4,19456]{2,1,0:T(4,128)(2,1)} %param.7) | data formatting | bytes 2490368 | tf_op args[2]
  9.4 0.1 stack.79.meta_ref
  9.5 1.7 %collective-permute-done = bf16[256,128]{1,0:T(8,128)(2,1)S(1)} collective-permute-done((bf16[256,128]{1,0:T(8,128)(2,1)}, bf16[256,128]{1,0:T(8,128)(2,1)S(1)}, u32[]{:S(2)}, u32[]{:S(2)}) %collective-permute-start) | collective-permute-done | bytes 65568 | tf_op jit(solution)/shard_map/ppermute | solution.py:59
  11.3 4.3 %all-to-all-start = ((bf16[4,8,19456]{2,1,0:T(8,128)(2,1)}), bf16[4,8,19456]{2,1,0:T(8,128)(2,1)S(1)}, u32[]{:S(2)}, u32[]{:S(2)}) async-start(bf16[4,8,19456]{2,1,0:T(8,128)(2,1)} %bitcast.21), calls=%async_computation | async-start | bytes 2490368 | tf_op jit(solution)/shard_map/all_to_all | solution.py:401
  15.6 3.2 %collective-permute-start.5 = (bf16[1024,128]{1,0:T(8,128)(2,1)S(1)}, bf16[1024,128]{1,0:T(8,128)(2,1)S(1)}, u32[]{:S(2)}, u32[]{:S(2)}) collective-permute-start(bf16[1024,128]{1,0:T(8,128)(2,1)S(1)} %constant_dynamic-update-slice_fusion.refs_0_), channel_id=1, source_target_pairs={{0,16},{1,17},{2,18},{3,19},{4,20},{5,21},{6,22},{7,23},{8,24},{9,... | collective-permute-start | bytes 786440 | tf_op jit(solution)/shard_map/ppermute | solution.py:59
  18.8 1.1 %collective-permute-start.4 = (bf16[1024,128]{1,0:T(8,128)(2,1)S(1)}, bf16[1024,128]{1,0:T(8,128)(2,1)S(1)}, u32[]{:S(2)}, u32[]{:S(2)}) collective-permute-start(bf16[1024,128]{1,0:T(8,128)(2,1)S(1)} %constant_dynamic-update-slice_fusion.refs_0_), channel_id=1, source_target_pairs={{0,24},{1,25},{2,26},{3,27},{4,28},{5,29},{6,30},{7,31},{8,0},{9,1... | collective-permute-start | bytes 786440 | tf_op jit(solution)/shard_map/ppermute | solution.py:59
  19.9 1.0 collective-permute-start.3
  20.8 5.5 %collective-permute-done.5.refs_3_ = bf16[1024,128]{1,0:T(8,128)(2,1)S(1)} collective-permute-done((bf16[1024,128]{1,0:T(8,128)(2,1)S(1)}, bf16[1024,128]{1,0:T(8,128)(2,1)S(1)}, u32[]{:S(2)}, u32[]{:S(2)}) %collective-permute-start.5) | collective-permute-done | bytes 262176 | tf_op jit(solution)/shard_map/ppermute | solution.py:59
  26.3 3.1 %collective-permute-done.4.refs_2_ = bf16[1024,128]{1,0:T(8,128)(2,1)S(1)} collective-permute-done((bf16[1024,128]{1,0:T(8,128)(2,1)S(1)}, bf16[1024,128]{1,0:T(8,128)(2,1)S(1)}, u32[]{:S(2)}, u32[]{:S(2)}) %collective-permute-start.4) | collective-permute-done | bytes 262176 | tf_op jit(solution)/shard_map/ppermute | solution.py:59
  29.4 0.5 collective-permute-start.7
  29.9 1.0 collective-permute-done.8.refs_6_
  31.0 0.4 collective-permute-done.7.refs_5_
  31.3 0.0 all-to-all-done.refs_9_
  31.3 10.5 %student_logits.1 = (f32[256,2432]{1,0:T(8,128)S(1)}, bf16[32,8,2688]{2,1,0:T(8,128)(2,1)S(1)}, bf16[4096,512]{1,0:T(8,128)(2,1)S(1)}, bf16[4096,512]{1,0:T(8,12...) custom-call(s32[19]{0:T(128)S(1)} %stack.79.meta_ref, ...), custom_call_target="tpu_custom_call" | custom-call | flops 5100273664 | bytes 19922944 | tf_op jit(solution)/shard_map/student_logits/pallas_call | solution.py:176
  41.9 27.2 %all_to_all.20.x_ref = bf16[32,8,2688]{2,1,0:T(8,128)(2,1)S(1)} all-to-all(bf16[32,8,2688]{2,1,0:T(8,128)(2,1)S(1)} %get-tuple-element.18), channel_id=1, replica_groups=mesh['tok'=4,'vocab'=32] {'vocab'}, dimensions={0} | all-to-all | bytes 2752512 | tf_op jit(solution)/shard_map/all_to_all | solution.py:408
  69.1 5.4 %logit_grad.1 = (bf16[256,2432]{1,0:T(8,128)(2,1)S(1)}, bf16[16,128,256]{2,1,0:T(8,128)(2,1)S(1)}, bf16[16,256]{1,0:T(8,128)(2,1)S(1)}) custom-call(s32[19]{0:T(128)S(1)} %stack.79.meta_ref, bf16[32,8,2688]{2,1,0:T(8,128)(2,1)S(1)} %all_to_all.20.x_ref, f32[256,2432]{1,0:T(8,128)S(1)} %get-tuple-element.19.s_ref, s32[1,256]{1,0:T(1,128)S(1)} %bitcast.29, ...), custom_call_target="tpu_custom_call" | custom-call | flops 2550136832 | bytes 9961472 | tf_op jit(solution)/shard_map/logit_grad/pallas_call | solution.py:275
  74.6 0.6 collective-permute-start.10
  75.2 0.1 collective-permute-start.11
  75.3 3.4 %own_share.1.a_ref = bf16[16,128,256]{2,1,0:T(8,128)(2,1)S(1)} custom-call(s32[19]{0:T(128)S(1)} %stack.79.meta_ref, bf16[256,2432]{1,0:T(8,128)(2,1)S(1)} %get-tuple-element.25.grad_ref, bf16[4096,512]{1,0:T(8,128)(2,1)S(1)} %get-tuple-element.20.refs_0_, bf16[4096,512]{1,0:T(8,128)(2,1)S(1)} %get-tuple-element.21.refs_1_, ...), custom_call_target="tpu_custom_call" | custom-call | flops 2550136832 | bytes 9961472 | tf_op jit(solution)/shard_map/own_share/pallas_call | solution.py:318
  78.7 0.3 chip_sum.1
  79.1 22.0 %all_to_all.21.x_ref = bf16[16,144,256]{2,1,0:T(8,128)(2,1)S(1)} all-to-all(bf16[16,144,256]{2,1,0:T(8,128)(2,1)S(1)} %chip_sum.1), channel_id=1, replica_groups={{0,2,4,6,8,10,12,14,16,18,20,22,24,26,28,30},{1,3,5,7,9,11,13,15,17,19,..., dimensions={0} | all-to-all | bytes 2359296 | tf_op jit(solution)/shard_map/all_to_all | solution.py:417
  101.1 0.8 final_sum.1
  (21 shorter events, 0.1 us)
Async XLA Ops:
  0.6 10.6 %collective-permute-start.1 = (bf16[256,128]{1,0:T(8,128)(2,1)}, bf16[256,128]{1,0:T(8,128)(2,1)S(1)}, u32[]{:S(2)}, u32[]{:S(2)}) collective-permute-start(bf16[256,128]{1,0:T(8,128)(2,1)} %param.5), channel_id=1, source_target_pairs={{0,6},{1,7},{2,0},{3,1},{4,2},{5,3},{6,4},{7,5},{8,14},{9,15},{10,... | collective-permute-start | bytes 196616 | tf_op jit(solution)/shard_map/ppermute | solution.py:59
  4.8 6.4 %collective-permute-start = (bf16[256,128]{1,0:T(8,128)(2,1)}, bf16[256,128]{1,0:T(8,128)(2,1)S(1)}, u32[]{:S(2)}, u32[]{:S(2)}) collective-permute-start(bf16[256,128]{1,0:T(8,128)(2,1)} %param.5), channel_id=1, source_target_pairs={{0,2},{1,3},{2,4},{3,5},{4,6},{5,7},{6,0},{7,1},{8,10},{9,11},{10,... | collective-permute-start | bytes 196616 | tf_op jit(solution)/shard_map/ppermute | solution.py:59
  4.8 6.5 %collective-permute-start.2 = (bf16[256,128]{1,0:T(8,128)(2,1)}, bf16[256,128]{1,0:T(8,128)(2,1)S(1)}, u32[]{:S(2)}, u32[]{:S(2)}) collective-permute-start(bf16[256,128]{1,0:T(8,128)(2,1)} %param.5), channel_id=1, source_target_pairs={{0,4},{1,5},{2,6},{3,7},{4,0},{5,1},{6,2},{7,3},{8,12},{9,13},{10,... | collective-permute-start | bytes 196616 | tf_op jit(solution)/shard_map/ppermute | solution.py:59
  6.7 2.8 %copy-start.2 = (bf16[256,128]{1,0:T(8,128)(2,1)S(1)}, bf16[256,128]{1,0:T(8,128)(2,1)}, u32[]{:S(2)}) copy-start(bf16[256,128]{1,0:T(8,128)(2,1)} %param.5) | copy-start | bytes 196612
  11.3 20.0 %all-to-all-start = ((bf16[4,8,19456]{2,1,0:T(8,128)(2,1)}), bf16[4,8,19456]{2,1,0:T(8,128)(2,1)S(1)}, u32[]{:S(2)}, u32[]{:S(2)}) async-start(bf16[4,8,19456]{2,1,0:T(8,128)(2,1)} %bitcast.21), calls=%async_computation | async-start | bytes 2490368 | tf_op jit(solution)/shard_map/all_to_all | solution.py:401
  15.6 10.7 %collective-permute-start.5 = (bf16[1024,128]{1,0:T(8,128)(2,1)S(1)}, bf16[1024,128]{1,0:T(8,128)(2,1)S(1)}, u32[]{:S(2)}, u32[]{:S(2)}) collective-permute-start(bf16[1024,128]{1,0:T(8,128)(2,1)S(1)} %constant_dynamic-update-slice_fusion.refs_0_), channel_id=1, source_target_pairs={{0,16},{1,17},{2,18},{3,19},{4,20},{5,21},{6,22},{7,23},{8,24},{9,... | collective-permute-start | bytes 786440 | tf_op jit(solution)/shard_map/ppermute | solution.py:59
  18.8 10.6 %collective-permute-start.4 = (bf16[1024,128]{1,0:T(8,128)(2,1)S(1)}, bf16[1024,128]{1,0:T(8,128)(2,1)S(1)}, u32[]{:S(2)}, u32[]{:S(2)}) collective-permute-start(bf16[1024,128]{1,0:T(8,128)(2,1)S(1)} %constant_dynamic-update-slice_fusion.refs_0_), channel_id=1, source_target_pairs={{0,24},{1,25},{2,26},{3,27},{4,28},{5,29},{6,30},{7,31},{8,0},{9,1... | collective-permute-start | bytes 786440 | tf_op jit(solution)/shard_map/ppermute | solution.py:59
  19.9 9.6 %collective-permute-start.3 = (bf16[1024,128]{1,0:T(8,128)(2,1)S(1)}, bf16[1024,128]{1,0:T(8,128)(2,1)S(1)}, u32[]{:S(2)}, u32[]{:S(2)}) collective-permute-start(bf16[1024,128]{1,0:T(8,128)(2,1)S(1)} %constant_dynamic-update-slice_fusion.refs_0_), channel_id=1, source_target_pairs={{0,8},{1,9},{2,10},{3,11},{4,12},{5,13},{6,14},{7,15},{8,16},{9,17... | collective-permute-start | bytes 786440 | tf_op jit(solution)/shard_map/ppermute | solution.py:59
  20.8 9.1 %collective-permute-start.6 = (bf16[1024,128]{1,0:T(8,128)(2,1)S(1)}, bf16[1024,128]{1,0:T(8,128)(2,1)S(1)}, u32[]{:S(2)}, u32[]{:S(2)}) collective-permute-start(bf16[1024,128]{1,0:T(8,128)(2,1)S(1)} %constant_dynamic-update-slice_fusion.refs_0_), channel_id=1, source_target_pairs={{0,1},{1,0},{2,3},{3,2},{4,5},{5,4},{6,7},{7,6},{8,9},{9,8},{10,11... | collective-permute-start | bytes 786440 | tf_op jit(solution)/shard_map/ppermute | solution.py:55
  26.3 3.6 %collective-permute-start.9 = (bf16[1024,128]{1,0:T(8,128)(2,1)S(1)}, bf16[1024,128]{1,0:T(8,128)(2,1)S(1)}, u32[]{:S(2)}, u32[]{:S(2)}) collective-permute-start(bf16[1024,128]{1,0:T(8,128)(2,1)S(1)} %collective-permute-done.5.refs_3_), channel_id=1, source_target_pairs={{0,1},{1,0},{2,3},{3,2},{4,5},{5,4},{6,7},{7,6},{8,9},{9,8},{10,11... | collective-permute-start | bytes 786440 | tf_op jit(solution)/shard_map/ppermute | solution.py:55
  29.4 1.5 %collective-permute-start.8 = (bf16[1024,128]{1,0:T(8,128)(2,1)S(1)}, bf16[1024,128]{1,0:T(8,128)(2,1)S(1)}, u32[]{:S(2)}, u32[]{:S(2)}) collective-permute-start(bf16[1024,128]{1,0:T(8,128)(2,1)S(1)} %collective-permute-done.4.refs_2_), channel_id=1, source_target_pairs={{0,1},{1,0},{2,3},{3,2},{4,5},{5,4},{6,7},{7,6},{8,9},{9,8},{10,11... | collective-permute-start | bytes 786440 | tf_op jit(solution)/shard_map/ppermute | solution.py:55
  29.4 1.9 %collective-permute-start.7 = (bf16[1024,128]{1,0:T(8,128)(2,1)S(1)}, bf16[1024,128]{1,0:T(8,128)(2,1)S(1)}, u32[]{:S(2)}, u32[]{:S(2)}) collective-permute-start(bf16[1024,128]{1,0:T(8,128)(2,1)S(1)} %collective-permute-done.3.refs_1_), channel_id=1, source_target_pairs={{0,1},{1,0},{2,3},{3,2},{4,5},{5,4},{6,7},{7,6},{8,9},{9,8},{10,11... | collective-permute-start | bytes 786440 | tf_op jit(solution)/shard_map/ppermute | solution.py:55
  41.9 27.3 %copy-start = (s32[256]{0:T(256)S(1)}, s32[256]{0:T(256)}, u32[]{:S(2)}) copy-start(s32[256]{0:T(256)} %param.8) | copy-start | bytes 3076
  41.9 27.3 %copy-start.1 = (f32[256]{0:T(256)S(1)}, f32[256]{0:T(256)}, u32[]{:S(2)}) copy-start(f32[256]{0:T(256)} %param.9) | copy-start | bytes 3076
  74.6 4.1 %collective-permute-start.10 = (bf16[16,128,256]{2,1,0:T(8,128)(2,1)S(1)}, bf16[16,128,256]{2,1,0:T(8,128)(2,1)S(1)}, u32[]{:S(2)}, u32[]{:S(2)}) collective-permute-start(bf16[16,128,256]{2,1,0:T(8,128)(2,1)S(1)} %get-tuple-element.26), channel_id=1, source_target_pairs={{0,1},{1,0},{2,3},{3,2},{4,5},{5,4},{6,7},{7,6},{8,9},{9,8},{10,11... | collective-permute-start | bytes 3145736 | tf_op jit(solution)/shard_map/ppermute | solution.py:55
  75.2 3.5 %collective-permute-start.11 = (bf16[16,256]{1,0:T(8,128)(2,1)S(1)}, bf16[16,256]{1,0:T(8,128)(2,1)S(1)}, u32[]{:S(2)}, u32[]{:S(2)}) collective-permute-start(bf16[16,256]{1,0:T(8,128)(2,1)S(1)} %get-tuple-element.27.ta_ref), channel_id=1, source_target_pairs={{0,1},{1,0},{2,3},{3,2},{4,5},{5,4},{6,7},{7,6},{8,9},{9,8},{10,11... | collective-permute-start | bytes 24584 | tf_op jit(solution)/shard_map/ppermute | solution.py:55

commit v5 on v4

--- a/solution.py
+++ b/solution.py
@@ -398,7 +398,7 @@
 
     along_z = jnp.concatenate(from_ring(hidden, "dz"), axis=0)
     blocks = jnp.transpose(teacher_logits, (1, 0, 2)).reshape(rows // 8, -1)
-    blocks = lax.all_to_all(after(blocks, along_z, meta), "tok", 0, 0, tiled=True)
+    blocks = lax.all_to_all(after(blocks, meta), "tok", 0, 0, tiled=True)
     own = from_ring(along_z, "dy")
     other = [swap_core(x) for x in own]
     student, send, *heads = student_logits(

time: 102 us -> 101 us (level)
  waiting for transfers between devices: 11.7 us -> 10.6 us
    ppermute x6, waiting for transfers between devices: 10.3 us -> 9.21 us  [from_ring(): lax.ppermute(x, 'vocab', moves(**{axis: d}))]
  transfers between devices with their start and end apart: 13 -> 13, of which waited for: 5 -> 4; matrix products, arithmetic and copies ran while one was open for 3% -> 3% of each run, Pallas kernels for 3% -> 3%
where the time goes in v5:
time: 101 us; the launch traced here: 100 us
  blocking collectives  48.8 us (48%)
  Pallas kernels  20.5 us (20%)
  starting transfers between devices  16.8 us (17%)
  waiting for transfers between devices  10.6 us (10%)
  local copies, waits for them, and re-layouts  2.86 us (3%)
    all_to_all x1, blocking collectives, on_device(): teacher = lax.all_to_all(send, 'vocab', 0, 0, tiled=True)  26.8 us
    all_to_all x1, blocking collectives, on_device(): lax.all_to_all(summed.reshape(CHIPS * (share + TAIL), rows), 'vocab', 0,...  22 us
    ppermute x6, starting transfers between devices, from_ring(): lax.ppermute(x, 'vocab', moves(**{axis: d}))  11.4 us
    pallas_call x1, Pallas kernels, student_logits(): pl.pallas_call(student_kernel, in_specs=[SMEM] + [VMEM] * (2 * RING) + [H...  10.5 us
    ppermute x6, waiting for transfers between devices, from_ring(): lax.ppermute(x, 'vocab', moves(**{axis: d}))  9.21 us
    pallas_call x1, Pallas kernels, logit_grad(): pl.pallas_call(grad_kernel, in_specs=[SMEM] + [VMEM] * (4 + len(heads)),...  5.44 us
    all_to_all x1, starting transfers between devices, on_device(): blocks = lax.all_to_all(after(blocks, meta), 'tok', 0, 0, tiled=True)  4.3 us
    pallas_call x1, Pallas kernels, own_share(): pl.pallas_call(own_kernel, in_specs=[SMEM] + [VMEM] * (1 + len(heads)), o...  3.43 us
  transfers between devices with their start and end apart: 13, of which 4 were waited for; matrix products, arithmetic and copies ran while one was open for 3% of the time, Pallas kernels for 3%

profile of v5, /device:TPU:0, one launch (start us, length us, event | category | flops | bytes accessed | tf_op | source)
XLA Modules:
  0.0 100.4 jit_solution(10371135499379787078)
XLA Ops:
  0.6 4.2 %collective-permute-start.1 = (bf16[256,128]{1,0:T(8,128)(2,1)}, bf16[256,128]{1,0:T(8,128)(2,1)S(1)}, u32[]{:S(2)}, u32[]{:S(2)}) collective-permute-start(bf16[256,128]{1,0:T(8,128)(2,1)} %param.5), channel_id=1, source_target_pairs={{0,6},{1,7},{2,0},{3,1},{4,2},{5,3},{6,4},{7,5},{8,14},{9,15},{10,... | collective-permute-start | bytes 196616 | tf_op jit(solution)/shard_map/ppermute | solution.py:59
  4.8 1.9 %collective-permute-start.2 = (bf16[256,128]{1,0:T(8,128)(2,1)}, bf16[256,128]{1,0:T(8,128)(2,1)S(1)}, u32[]{:S(2)}, u32[]{:S(2)}) collective-permute-start(bf16[256,128]{1,0:T(8,128)(2,1)} %param.5), channel_id=1, source_target_pairs={{0,4},{1,5},{2,6},{3,7},{4,0},{5,1},{6,2},{7,3},{8,12},{9,13},{10,... | collective-permute-start | bytes 196616 | tf_op jit(solution)/shard_map/ppermute | solution.py:59
  6.7 2.7 %copy.10 = bf16[8,4,19456]{2,0,1:T(8,128)(2,1)} copy(bf16[8,4,19456]{2,1,0:T(4,128)(2,1)} %param.7) | data formatting | bytes 2490368 | tf_op args[2]
  9.4 0.1 stack.79.meta_ref
  9.5 4.3 %all-to-all-start = ((bf16[4,8,19456]{2,1,0:T(8,128)(2,1)}), bf16[4,8,19456]{2,1,0:T(8,128)(2,1)S(1)}, u32[]{:S(2)}, u32[]{:S(2)}) async-start(bf16[4,8,19456]{2,1,0:T(8,128)(2,1)} %bitcast.21), calls=%async_computation | async-start | bytes 2490368 | tf_op jit(solution)/shard_map/all_to_all | solution.py:401
  13.9 3.3 %collective-permute-start.5 = (bf16[1024,128]{1,0:T(8,128)(2,1)S(1)}, bf16[1024,128]{1,0:T(8,128)(2,1)S(1)}, u32[]{:S(2)}, u32[]{:S(2)}) collective-permute-start(bf16[1024,128]{1,0:T(8,128)(2,1)S(1)} %constant_dynamic-update-slice_fusion.refs_0_), channel_id=1, source_target_pairs={{0,16},{1,17},{2,18},{3,19},{4,20},{5,21},{6,22},{7,23},{8,24},{9,... | collective-permute-start | bytes 786440 | tf_op jit(solution)/shard_map/ppermute | solution.py:59
  17.2 1.1 %collective-permute-start.4 = (bf16[1024,128]{1,0:T(8,128)(2,1)S(1)}, bf16[1024,128]{1,0:T(8,128)(2,1)S(1)}, u32[]{:S(2)}, u32[]{:S(2)}) collective-permute-start(bf16[1024,128]{1,0:T(8,128)(2,1)S(1)} %constant_dynamic-update-slice_fusion.refs_0_), channel_id=1, source_target_pairs={{0,24},{1,25},{2,26},{3,27},{4,28},{5,29},{6,30},{7,31},{8,0},{9,1... | collective-permute-start | bytes 786440 | tf_op jit(solution)/shard_map/ppermute | solution.py:59
  18.2 1.0 collective-permute-start.3
  19.2 5.5 %collective-permute-done.5.refs_3_ = bf16[1024,128]{1,0:T(8,128)(2,1)S(1)} collective-permute-done((bf16[1024,128]{1,0:T(8,128)(2,1)S(1)}, bf16[1024,128]{1,0:T(8,128)(2,1)S(1)}, u32[]{:S(2)}, u32[]{:S(2)}) %collective-permute-start.5) | collective-permute-done | bytes 262176 | tf_op jit(solution)/shard_map/ppermute | solution.py:59
  24.7 3.7 %collective-permute-done.4.refs_2_ = bf16[1024,128]{1,0:T(8,128)(2,1)S(1)} collective-permute-done((bf16[1024,128]{1,0:T(8,128)(2,1)S(1)}, bf16[1024,128]{1,0:T(8,128)(2,1)S(1)}, u32[]{:S(2)}, u32[]{:S(2)}) %collective-permute-start.4) | collective-permute-done | bytes 262176 | tf_op jit(solution)/shard_map/ppermute | solution.py:59
  28.4 0.5 collective-permute-start.7
  28.9 1.0 %collective-permute-done.8.refs_6_ = bf16[1024,128]{1,0:T(8,128)(2,1)S(1)} collective-permute-done((bf16[1024,128]{1,0:T(8,128)(2,1)S(1)}, bf16[1024,128]{1,0:T(8,128)(2,1)S(1)}, u32[]{:S(2)}, u32[]{:S(2)}) %collective-permute-start.8) | collective-permute-done | bytes 262176 | tf_op jit(solution)/shard_map/ppermute | solution.py:55
  29.9 0.4 collective-permute-done.7.refs_5_
  30.3 10.5 %student_logits.1 = (f32[256,2432]{1,0:T(8,128)S(1)}, bf16[32,8,2688]{2,1,0:T(8,128)(2,1)S(1)}, bf16[4096,512]{1,0:T(8,128)(2,1)S(1)}, bf16[4096,512]{1,0:T(8,12...) custom-call(s32[19]{0:T(128)S(1)} %stack.79.meta_ref, ...), custom_call_target="tpu_custom_call" | custom-call | flops 5100273664 | bytes 19922944 | tf_op jit(solution)/shard_map/student_logits/pallas_call | solution.py:176
  40.8 0.0 copy-start
  40.9 0.0 copy-start.1
  40.9 26.8 %all_to_all.20.x_ref = bf16[32,8,2688]{2,1,0:T(8,128)(2,1)S(1)} all-to-all(bf16[32,8,2688]{2,1,0:T(8,128)(2,1)S(1)} %get-tuple-element.18), channel_id=1, replica_groups=mesh['tok'=4,'vocab'=32] {'vocab'}, dimensions={0} | all-to-all | bytes 2752512 | tf_op jit(solution)/shard_map/all_to_all | solution.py:408
  67.7 5.4 %logit_grad.1 = (bf16[256,2432]{1,0:T(8,128)(2,1)S(1)}, bf16[16,128,256]{2,1,0:T(8,128)(2,1)S(1)}, bf16[16,256]{1,0:T(8,128)(2,1)S(1)}) custom-call(s32[19]{0:T(128)S(1)} %stack.79.meta_ref, bf16[32,8,2688]{2,1,0:T(8,128)(2,1)S(1)} %all_to_all.20.x_ref, f32[256,2432]{1,0:T(8,128)S(1)} %get-tuple-element.19.s_ref, s32[1,256]{1,0:T(1,128)S(1)} %bitcast.29, ...), custom_call_target="tpu_custom_call" | custom-call | flops 2550136832 | bytes 9961472 | tf_op jit(solution)/shard_map/logit_grad/pallas_call | solution.py:275
  73.1 0.6 collective-permute-start.10
  73.7 0.1 collective-permute-start.11
  73.8 3.4 %own_share.1.a_ref = bf16[16,128,256]{2,1,0:T(8,128)(2,1)S(1)} custom-call(s32[19]{0:T(128)S(1)} %stack.79.meta_ref, bf16[256,2432]{1,0:T(8,128)(2,1)S(1)} %get-tuple-element.25.grad_ref, bf16[4096,512]{1,0:T(8,128)(2,1)S(1)} %get-tuple-element.20.refs_0_, bf16[4096,512]{1,0:T(8,128)(2,1)S(1)} %get-tuple-element.21.refs_1_, ...), custom_call_target="tpu_custom_call" | custom-call | flops 2550136832 | bytes 9961472 | tf_op jit(solution)/shard_map/own_share/pallas_call | solution.py:318
  77.3 0.3 chip_sum.1
  77.6 22.0 %all_to_all.21.x_ref = bf16[16,144,256]{2,1,0:T(8,128)(2,1)S(1)} all-to-all(bf16[16,144,256]{2,1,0:T(8,128)(2,1)S(1)} %chip_sum.1), channel_id=1, replica_groups={{0,2,4,6,8,10,12,14,16,18,20,22,24,26,28,30},{1,3,5,7,9,11,13,15,17,19,..., dimensions={0} | all-to-all | bytes 2359296 | tf_op jit(solution)/shard_map/all_to_all | solution.py:417
  99.6 0.8 final_sum.1
  (21 shorter events, 0.1 us)
Async XLA Ops:
  0.6 13.2 %collective-permute-start.1 = (bf16[256,128]{1,0:T(8,128)(2,1)}, bf16[256,128]{1,0:T(8,128)(2,1)S(1)}, u32[]{:S(2)}, u32[]{:S(2)}) collective-permute-start(bf16[256,128]{1,0:T(8,128)(2,1)} %param.5), channel_id=1, source_target_pairs={{0,6},{1,7},{2,0},{3,1},{4,2},{5,3},{6,4},{7,5},{8,14},{9,15},{10,... | collective-permute-start | bytes 196616 | tf_op jit(solution)/shard_map/ppermute | solution.py:59
  4.8 9.0 %collective-permute-start = (bf16[256,128]{1,0:T(8,128)(2,1)}, bf16[256,128]{1,0:T(8,128)(2,1)S(1)}, u32[]{:S(2)}, u32[]{:S(2)}) collective-permute-start(bf16[256,128]{1,0:T(8,128)(2,1)} %param.5), channel_id=1, source_target_pairs={{0,2},{1,3},{2,4},{3,5},{4,6},{5,7},{6,0},{7,1},{8,10},{9,11},{10,... | collective-permute-start | bytes 196616 | tf_op jit(solution)/shard_map/ppermute | solution.py:59
  4.8 9.0 %collective-permute-start.2 = (bf16[256,128]{1,0:T(8,128)(2,1)}, bf16[256,128]{1,0:T(8,128)(2,1)S(1)}, u32[]{:S(2)}, u32[]{:S(2)}) collective-permute-start(bf16[256,128]{1,0:T(8,128)(2,1)} %param.5), channel_id=1, source_target_pairs={{0,4},{1,5},{2,6},{3,7},{4,0},{5,1},{6,2},{7,3},{8,12},{9,13},{10,... | collective-permute-start | bytes 196616 | tf_op jit(solution)/shard_map/ppermute | solution.py:59
  9.4 4.4 %copy-start.2 = (bf16[256,128]{1,0:T(8,128)(2,1)S(1)}, bf16[256,128]{1,0:T(8,128)(2,1)}, u32[]{:S(2)}) copy-start(bf16[256,128]{1,0:T(8,128)(2,1)} %param.5) | copy-start | bytes 196612
  9.5 20.8 %all-to-all-start = ((bf16[4,8,19456]{2,1,0:T(8,128)(2,1)}), bf16[4,8,19456]{2,1,0:T(8,128)(2,1)S(1)}, u32[]{:S(2)}, u32[]{:S(2)}) async-start(bf16[4,8,19456]{2,1,0:T(8,128)(2,1)} %bitcast.21), calls=%async_computation | async-start | bytes 2490368 | tf_op jit(solution)/shard_map/all_to_all | solution.py:401
  13.9 10.8 %collective-permute-start.5 = (bf16[1024,128]{1,0:T(8,128)(2,1)S(1)}, bf16[1024,128]{1,0:T(8,128)(2,1)S(1)}, u32[]{:S(2)}, u32[]{:S(2)}) collective-permute-start(bf16[1024,128]{1,0:T(8,128)(2,1)S(1)} %constant_dynamic-update-slice_fusion.refs_0_), channel_id=1, source_target_pairs={{0,16},{1,17},{2,18},{3,19},{4,20},{5,21},{6,22},{7,23},{8,24},{9,... | collective-permute-start | bytes 786440 | tf_op jit(solution)/shard_map/ppermute | solution.py:59
  17.2 11.2 %collective-permute-start.4 = (bf16[1024,128]{1,0:T(8,128)(2,1)S(1)}, bf16[1024,128]{1,0:T(8,128)(2,1)S(1)}, u32[]{:S(2)}, u32[]{:S(2)}) collective-permute-start(bf16[1024,128]{1,0:T(8,128)(2,1)S(1)} %constant_dynamic-update-slice_fusion.refs_0_), channel_id=1, source_target_pairs={{0,24},{1,25},{2,26},{3,27},{4,28},{5,29},{6,30},{7,31},{8,0},{9,1... | collective-permute-start | bytes 786440 | tf_op jit(solution)/shard_map/ppermute | solution.py:59
  18.2 10.2 %collective-permute-start.3 = (bf16[1024,128]{1,0:T(8,128)(2,1)S(1)}, bf16[1024,128]{1,0:T(8,128)(2,1)S(1)}, u32[]{:S(2)}, u32[]{:S(2)}) collective-permute-start(bf16[1024,128]{1,0:T(8,128)(2,1)S(1)} %constant_dynamic-update-slice_fusion.refs_0_), channel_id=1, source_target_pairs={{0,8},{1,9},{2,10},{3,11},{4,12},{5,13},{6,14},{7,15},{8,16},{9,17... | collective-permute-start | bytes 786440 | tf_op jit(solution)/shard_map/ppermute | solution.py:59
  19.2 9.7 %collective-permute-start.6 = (bf16[1024,128]{1,0:T(8,128)(2,1)S(1)}, bf16[1024,128]{1,0:T(8,128)(2,1)S(1)}, u32[]{:S(2)}, u32[]{:S(2)}) collective-permute-start(bf16[1024,128]{1,0:T(8,128)(2,1)S(1)} %constant_dynamic-update-slice_fusion.refs_0_), channel_id=1, source_target_pairs={{0,1},{1,0},{2,3},{3,2},{4,5},{5,4},{6,7},{7,6},{8,9},{9,8},{10,11... | collective-permute-start | bytes 786440 | tf_op jit(solution)/shard_map/ppermute | solution.py:55
  24.7 4.2 %collective-permute-start.9 = (bf16[1024,128]{1,0:T(8,128)(2,1)S(1)}, bf16[1024,128]{1,0:T(8,128)(2,1)S(1)}, u32[]{:S(2)}, u32[]{:S(2)}) collective-permute-start(bf16[1024,128]{1,0:T(8,128)(2,1)S(1)} %collective-permute-done.5.refs_3_), channel_id=1, source_target_pairs={{0,1},{1,0},{2,3},{3,2},{4,5},{5,4},{6,7},{7,6},{8,9},{9,8},{10,11... | collective-permute-start | bytes 786440 | tf_op jit(solution)/shard_map/ppermute | solution.py:55
  28.4 1.5 %collective-permute-start.8 = (bf16[1024,128]{1,0:T(8,128)(2,1)S(1)}, bf16[1024,128]{1,0:T(8,128)(2,1)S(1)}, u32[]{:S(2)}, u32[]{:S(2)}) collective-permute-start(bf16[1024,128]{1,0:T(8,128)(2,1)S(1)} %collective-permute-done.4.refs_2_), channel_id=1, source_target_pairs={{0,1},{1,0},{2,3},{3,2},{4,5},{5,4},{6,7},{7,6},{8,9},{9,8},{10,11... | collective-permute-start | bytes 786440 | tf_op jit(solution)/shard_map/ppermute | solution.py:55
  28.4 1.9 %collective-permute-start.7 = (bf16[1024,128]{1,0:T(8,128)(2,1)S(1)}, bf16[1024,128]{1,0:T(8,128)(2,1)S(1)}, u32[]{:S(2)}, u32[]{:S(2)}) collective-permute-start(bf16[1024,128]{1,0:T(8,128)(2,1)S(1)} %collective-permute-done.3.refs_1_), channel_id=1, source_target_pairs={{0,1},{1,0},{2,3},{3,2},{4,5},{5,4},{6,7},{7,6},{8,9},{9,8},{10,11... | collective-permute-start | bytes 786440 | tf_op jit(solution)/shard_map/ppermute | solution.py:55
  40.8 26.8 %copy-start = (s32[256]{0:T(256)S(1)}, s32[256]{0:T(256)}, u32[]{:S(2)}) copy-start(s32[256]{0:T(256)} %param.8) | copy-start | bytes 3076
  40.9 26.8 %copy-start.1 = (f32[256]{0:T(256)S(1)}, f32[256]{0:T(256)}, u32[]{:S(2)}) copy-start(f32[256]{0:T(256)} %param.9) | copy-start | bytes 3076
  73.1 4.1 %collective-permute-start.10 = (bf16[16,128,256]{2,1,0:T(8,128)(2,1)S(1)}, bf16[16,128,256]{2,1,0:T(8,128)(2,1)S(1)}, u32[]{:S(2)}, u32[]{:S(2)}) collective-permute-start(bf16[16,128,256]{2,1,0:T(8,128)(2,1)S(1)} %get-tuple-element.26), channel_id=1, source_target_pairs={{0,1},{1,0},{2,3},{3,2},{4,5},{5,4},{6,7},{7,6},{8,9},{9,8},{10,11... | collective-permute-start | bytes 3145736 | tf_op jit(solution)/shard_map/ppermute | solution.py:55
  73.7 3.5 %collective-permute-start.11 = (bf16[16,256]{1,0:T(8,128)(2,1)S(1)}, bf16[16,256]{1,0:T(8,128)(2,1)S(1)}, u32[]{:S(2)}, u32[]{:S(2)}) collective-permute-start(bf16[16,256]{1,0:T(8,128)(2,1)S(1)} %get-tuple-element.27.ta_ref), channel_id=1, source_target_pairs={{0,1},{1,0},{2,3},{3,2},{4,5},{5,4},{6,7},{7,6},{8,9},{9,8},{10,11... | collective-permute-start | bytes 24584 | tf_op jit(solution)/shard_map/ppermute | solution.py:55

commit v6 on v5

--- a/solution.py
+++ b/solution.py
@@ -152,16 +152,18 @@
                 tally(k - 1)
 
     tally(n - 1)
-    peak = parts_of(jnp.max(peaks[...], axis=1, keepdims=True), 2)
-    total = jnp.sum(totals[...] * jnp.exp(peaks[...] - (peak[0] + peak[1])), axis=1, keepdims=True)
+    peak = jnp.max(peaks[...], axis=1, keepdims=True)
+    lse = peak + jnp.log(jnp.sum(totals[...] * jnp.exp(peaks[...] - peak), axis=1, keepdims=True))
     t_peak = jnp.max(t_peaks[...], axis=1, keepdims=True)
-    t_total = jnp.sum(t_totals[...] * jnp.exp(t_peaks[...] - t_peak), axis=1, keepdims=True)
-    row = lax.broadcasted_iota(jnp.int32, (8, rows), 0)
-    lane = lax.broadcasted_iota(jnp.int32, (8, rows), 1)
-    lse = jnp.where(lane == meta_ref[2] * 8 + row, t_peak + jnp.log(t_total), 0.0)
-    lse = jnp.sum(lse, axis=0, keepdims=True)
-    lines = [to_row(x) for x in peak] + parts_of(to_row(total), 3) + parts_of(lse, 3)
-    stat = jnp.zeros((8, rows), jnp.float32)
+    t_lse = t_peak + jnp.log(jnp.sum(t_totals[...] * jnp.exp(t_peaks[...] - t_peak), axis=1, keepdims=True))
+    row = lax.broadcasted_iota(jnp.int32, (8, 128), 0)
+    lane = lax.broadcasted_iota(jnp.int32, (8, 128), 1)
+    lines = [part[:, h : h + 128] for part in parts_of(to_row(lse), 3) for h in range(0, rows, 128)]
+    t_line = jnp.zeros((8, 128), jnp.float32)
+    for k, part in enumerate(parts_of(t_lse, 3)):
+        t_line = jnp.where(lane == k * 8 + row, part, t_line)
+    lines.append(jnp.sum(t_line, axis=0, keepdims=True))
+    stat = jnp.zeros((8, 128), jnp.float32)
     for k, line in enumerate(lines):
         stat = jnp.where(row == k, line, stat)
     stat = stat.astype(jnp.bfloat16)
@@ -179,7 +181,7 @@
         out_specs=[VMEM] * (2 + len(blocks)),
         out_shape=[
             jax.ShapeDtypeStruct((rows, width), jnp.float32),
-            jax.ShapeDtypeStruct((2 * CHIPS, 8, width + rows), jnp.bfloat16),
+            jax.ShapeDtypeStruct((2 * CHIPS, 8, width + 128), jnp.bfloat16),
         ]
         + [jax.ShapeDtypeStruct((depth, size), jnp.bfloat16) for _, size in blocks],
         scratch_shapes=[
@@ -196,13 +198,18 @@
     )(meta, *own, *other, in_hbm(head_weight), teacher_rows)
 
 
-def merged(stats):
-    peaks = [x[0:1] + x[1:2] for x in stats]
-    top = functools.reduce(jnp.maximum, peaks)
-    total = functools.reduce(
-        jnp.add, [((x[2:3] + x[3:4]) + x[4:5]) * jnp.exp(p - top) for x, p in zip(stats, peaks)]
-    )
-    return top + jnp.log(total), functools.reduce(jnp.add, [(x[5:6] + x[6:7]) + x[7:8] for x in stats])
+def merged(stats, rows):
+    halves = rows // 128
+    line = lambda x, k: jnp.concatenate([x[k * halves + h : k * halves + h + 1] for h in range(halves)], axis=1)
+    lses = [(line(x, 0) + line(x, 1)) + line(x, 2) for x in stats]
+    top = functools.reduce(jnp.maximum, lses)
+    total = functools.reduce(jnp.add, [jnp.exp(x - top) for x in lses])
+    teacher = jnp.concatenate([x[3 * halves : 3 * halves + 1] for x in stats], axis=0)
+    teacher = jnp.broadcast_to(teacher[:, None, :], (len(stats), 8, 128)).reshape(rows, 128)
+    row = lax.broadcasted_iota(jnp.int32, (rows, 128), 0)
+    lane = lax.broadcasted_iota(jnp.int32, (rows, 128), 1)
+    mine = jnp.logical_and(lane < 24, lax.rem(lane, 8) == lax.rem(row, 8))
+    return top + jnp.log(total), jnp.sum(jnp.where(mine, teacher, 0.0), axis=1, keepdims=True)
 
 
 def head_rows(head, core, chips):
@@ -217,14 +224,19 @@
     grad_ref, part_ref, tail_ref, column, cross, picked, total = refs[len(blocks) :]
     rows, width = s_ref.shape
     stats = [x_ref[i, :, width:].astype(jnp.float32) for i in range(x_ref.shape[0])]
-    student_row, teacher_row = merged(stats)
+    student_row, teacher_column = merged(stats, rows)
     column[:, 0:1] = to_column(student_row)
-    column[:, 1:2] = to_column(teacher_row)
+    column[:, 1:2] = teacher_column
     column[:, 2:3] = to_column(weight_ref[...])
     column[:, 3:4] = to_column(id_ref[...].astype(jnp.float32))
     lane = lax.broadcasted_iota(jnp.int32, (ROWS, 128), 1)
 
-    for k, (first, size) in enumerate(blocks):
+    steps = [
+        (k, first + low, low, min(STEP, size - low))
+        for k, (first, size) in enumerate(blocks)
+        for low in range(0, size, STEP)
+    ]
+    for k, (block, first, low, size) in enumerate(steps):
         for r in range(0, rows, ROWS):
             at = slice(r, r + ROWS)
             student_lse, teacher_lse, weight = column[at, 0:1], column[at, 1:2], column[at, 2:3]
@@ -247,14 +259,14 @@
             cross[at, :] = gap
             picked[at, :] = pick
         out = lax.dot_general(
-            head_rows(heads[k], 1 - meta_ref[0], slice(0, CHIPS)),
+            head_rows(heads[block], 1 - meta_ref[0], slice(0, CHIPS))[:, low : low + size],
             grad_ref[:, first : first + size],
             (((1,), (1,)), ((), ())),
             preferred_element_type=jnp.float32,
         )
         if k == 0:
             total[...] = out
-        elif k + 1 < len(blocks):
+        elif k + 1 < len(steps):
             total[...] += out
         else:
             part_ref[...] = (total[...] + out).astype(jnp.bfloat16).reshape(part_ref.shape)
@@ -294,6 +306,7 @@
 
 
 CHIP_BLOCK = 4
+STEP = 256
 
 
 def own_kernel(meta_ref, grad_ref, *refs):

time: 101 us -> 99.8 us (0.988)
  no operation moved by 1% of the time
where the time goes in v6:
time: 99.8 us; the launch traced here: 99.5 us
  blocking collectives  48.2 us (48%)
  Pallas kernels  20.3 us (20%)
  starting transfers between devices  16.8 us (17%)
  waiting for transfers between devices  10.6 us (11%)
  local copies, waits for them, and re-layouts  2.86 us (3%)
    all_to_all x1, blocking collectives, on_device(): teacher = lax.all_to_all(send, 'vocab', 0, 0, tiled=True)  26.3 us
    all_to_all x1, blocking collectives, on_device(): lax.all_to_all(summed.reshape(CHIPS * (share + TAIL), rows), 'vocab', 0,...  21.9 us
    ppermute x6, starting transfers between devices, from_ring(): lax.ppermute(x, 'vocab', moves(**{axis: d}))  11.4 us
    pallas_call x1, Pallas kernels, student_logits(): pl.pallas_call(student_kernel, in_specs=[SMEM] + [VMEM] * (2 * RING) + [H...  10.5 us
    ppermute x6, waiting for transfers between devices, from_ring(): lax.ppermute(x, 'vocab', moves(**{axis: d}))  9.21 us
    pallas_call x1, Pallas kernels, logit_grad(): pl.pallas_call(grad_kernel, in_specs=[SMEM] + [VMEM] * (4 + len(heads)),...  5.24 us
    all_to_all x1, starting transfers between devices, on_device(): blocks = lax.all_to_all(after(blocks, meta), 'tok', 0, 0, tiled=True)  4.3 us
    pallas_call x1, Pallas kernels, own_share(): pl.pallas_call(own_kernel, in_specs=[SMEM] + [VMEM] * (1 + len(heads)), o...  3.43 us
  transfers between devices with their start and end apart: 13, of which 4 were waited for; matrix products, arithmetic and copies ran while one was open for 3% of the time, Pallas kernels for 3%

profile of v6, /device:TPU:0, one launch (start us, length us, event | category | flops | bytes accessed | tf_op | source)
XLA Modules:
  0.0 99.5 jit_solution(14767262503497561341)
XLA Ops:
  0.6 4.2 %collective-permute-start.1 = (bf16[256,128]{1,0:T(8,128)(2,1)}, bf16[256,128]{1,0:T(8,128)(2,1)S(1)}, u32[]{:S(2)}, u32[]{:S(2)}) collective-permute-start(bf16[256,128]{1,0:T(8,128)(2,1)} %param.5), channel_id=1, source_target_pairs={{0,6},{1,7},{2,0},{3,1},{4,2},{5,3},{6,4},{7,5},{8,14},{9,15},{10,... | collective-permute-start | bytes 196616 | tf_op jit(solution)/shard_map/ppermute | solution.py:59
  4.8 1.9 %collective-permute-start.2 = (bf16[256,128]{1,0:T(8,128)(2,1)}, bf16[256,128]{1,0:T(8,128)(2,1)S(1)}, u32[]{:S(2)}, u32[]{:S(2)}) collective-permute-start(bf16[256,128]{1,0:T(8,128)(2,1)} %param.5), channel_id=1, source_target_pairs={{0,4},{1,5},{2,6},{3,7},{4,0},{5,1},{6,2},{7,3},{8,12},{9,13},{10,... | collective-permute-start | bytes 196616 | tf_op jit(solution)/shard_map/ppermute | solution.py:59
  6.7 2.7 %copy.10 = bf16[8,4,19456]{2,0,1:T(8,128)(2,1)} copy(bf16[8,4,19456]{2,1,0:T(4,128)(2,1)} %param.7) | data formatting | bytes 2490368 | tf_op args[2]
  9.4 0.1 stack.79.meta_ref
  9.5 4.3 %all-to-all-start = ((bf16[4,8,19456]{2,1,0:T(8,128)(2,1)}), bf16[4,8,19456]{2,1,0:T(8,128)(2,1)S(1)}, u32[]{:S(2)}, u32[]{:S(2)}) async-start(bf16[4,8,19456]{2,1,0:T(8,128)(2,1)} %bitcast.21), calls=%async_computation | async-start | bytes 2490368 | tf_op jit(solution)/shard_map/all_to_all | solution.py:414
  13.9 3.3 %collective-permute-start.5 = (bf16[1024,128]{1,0:T(8,128)(2,1)S(1)}, bf16[1024,128]{1,0:T(8,128)(2,1)S(1)}, u32[]{:S(2)}, u32[]{:S(2)}) collective-permute-start(bf16[1024,128]{1,0:T(8,128)(2,1)S(1)} %constant_dynamic-update-slice_fusion.refs_0_), channel_id=1, source_target_pairs={{0,16},{1,17},{2,18},{3,19},{4,20},{5,21},{6,22},{7,23},{8,24},{9,... | collective-permute-start | bytes 786440 | tf_op jit(solution)/shard_map/ppermute | solution.py:59
  17.2 1.1 %collective-permute-start.4 = (bf16[1024,128]{1,0:T(8,128)(2,1)S(1)}, bf16[1024,128]{1,0:T(8,128)(2,1)S(1)}, u32[]{:S(2)}, u32[]{:S(2)}) collective-permute-start(bf16[1024,128]{1,0:T(8,128)(2,1)S(1)} %constant_dynamic-update-slice_fusion.refs_0_), channel_id=1, source_target_pairs={{0,24},{1,25},{2,26},{3,27},{4,28},{5,29},{6,30},{7,31},{8,0},{9,1... | collective-permute-start | bytes 786440 | tf_op jit(solution)/shard_map/ppermute | solution.py:59
  18.2 1.0 collective-permute-start.3
  19.2 5.5 %collective-permute-done.5.refs_3_ = bf16[1024,128]{1,0:T(8,128)(2,1)S(1)} collective-permute-done((bf16[1024,128]{1,0:T(8,128)(2,1)S(1)}, bf16[1024,128]{1,0:T(8,128)(2,1)S(1)}, u32[]{:S(2)}, u32[]{:S(2)}) %collective-permute-start.5) | collective-permute-done | bytes 262176 | tf_op jit(solution)/shard_map/ppermute | solution.py:59
  24.7 3.7 %collective-permute-done.4.refs_2_ = bf16[1024,128]{1,0:T(8,128)(2,1)S(1)} collective-permute-done((bf16[1024,128]{1,0:T(8,128)(2,1)S(1)}, bf16[1024,128]{1,0:T(8,128)(2,1)S(1)}, u32[]{:S(2)}, u32[]{:S(2)}) %collective-permute-start.4) | collective-permute-done | bytes 262176 | tf_op jit(solution)/shard_map/ppermute | solution.py:59
  28.4 0.5 collective-permute-start.7
  28.9 1.0 %collective-permute-done.8.refs_6_ = bf16[1024,128]{1,0:T(8,128)(2,1)S(1)} collective-permute-done((bf16[1024,128]{1,0:T(8,128)(2,1)S(1)}, bf16[1024,128]{1,0:T(8,128)(2,1)S(1)}, u32[]{:S(2)}, u32[]{:S(2)}) %collective-permute-start.8) | collective-permute-done | bytes 262176 | tf_op jit(solution)/shard_map/ppermute | solution.py:55
  29.9 0.4 collective-permute-done.7.refs_5_
  30.3 10.5 %student_logits.1 = (f32[256,2432]{1,0:T(8,128)S(1)}, bf16[32,8,2560]{2,1,0:T(8,128)(2,1)S(1)}, bf16[4096,512]{1,0:T(8,128)(2,1)S(1)}, bf16[4096,512]{1,0:T(8,12...) custom-call(s32[19]{0:T(128)S(1)} %stack.79.meta_ref, ...), custom_call_target="tpu_custom_call" | custom-call | flops 5100273664 | bytes 19922944 | tf_op jit(solution)/shard_map/student_logits/pallas_call | solution.py:178
  40.8 0.0 copy-start
  40.8 0.0 copy-start.1
  40.8 26.3 %all_to_all.20.x_ref = bf16[32,8,2560]{2,1,0:T(8,128)(2,1)S(1)} all-to-all(bf16[32,8,2560]{2,1,0:T(8,128)(2,1)S(1)} %get-tuple-element.18), channel_id=1, replica_groups=mesh['tok'=4,'vocab'=32] {'vocab'}, dimensions={0} | all-to-all | bytes 2621440 | tf_op jit(solution)/shard_map/all_to_all | solution.py:421
  67.2 5.2 %logit_grad.1 = (bf16[256,2432]{1,0:T(8,128)(2,1)S(1)}, bf16[16,128,256]{2,1,0:T(8,128)(2,1)S(1)}, bf16[16,256]{1,0:T(8,128)(2,1)S(1)}) custom-call(s32[19]{0:T(128)S(1)} %stack.79.meta_ref, bf16[32,8,2560]{2,1,0:T(8,128)(2,1)S(1)} %all_to_all.20.x_ref, f32[256,2432]{1,0:T(8,128)S(1)} %get-tuple-element.19.s_ref, s32[1,256]{1,0:T(1,128)S(1)} %bitcast.29, ...), custom_call_target="tpu_custom_call" | custom-call | flops 2550136832 | bytes 9961472 | tf_op jit(solution)/shard_map/logit_grad/pallas_call | solution.py:287
  72.4 0.4 collective-permute-start.10
  72.8 0.2 collective-permute-start.11
  73.0 3.4 %own_share.1.a_ref = bf16[16,128,256]{2,1,0:T(8,128)(2,1)S(1)} custom-call(s32[19]{0:T(128)S(1)} %stack.79.meta_ref, bf16[256,2432]{1,0:T(8,128)(2,1)S(1)} %get-tuple-element.25.grad_ref, bf16[4096,512]{1,0:T(8,128)(2,1)S(1)} %get-tuple-element.20.refs_0_, bf16[4096,512]{1,0:T(8,128)(2,1)S(1)} %get-tuple-element.21.refs_1_, ...), custom_call_target="tpu_custom_call" | custom-call | flops 2550136832 | bytes 9961472 | tf_op jit(solution)/shard_map/own_share/pallas_call | solution.py:331
  76.5 0.3 chip_sum.1
  76.8 21.9 %all_to_all.21.x_ref = bf16[16,144,256]{2,1,0:T(8,128)(2,1)S(1)} all-to-all(bf16[16,144,256]{2,1,0:T(8,128)(2,1)S(1)} %chip_sum.1), channel_id=1, replica_groups={{0,2,4,6,8,10,12,14,16,18,20,22,24,26,28,30},{1,3,5,7,9,11,13,15,17,19,..., dimensions={0} | all-to-all | bytes 2359296 | tf_op jit(solution)/shard_map/all_to_all | solution.py:430
  98.7 0.8 final_sum.1
  (21 shorter events, 0.1 us)
Async XLA Ops:
  0.6 13.2 %collective-permute-start.1 = (bf16[256,128]{1,0:T(8,128)(2,1)}, bf16[256,128]{1,0:T(8,128)(2,1)S(1)}, u32[]{:S(2)}, u32[]{:S(2)}) collective-permute-start(bf16[256,128]{1,0:T(8,128)(2,1)} %param.5), channel_id=1, source_target_pairs={{0,6},{1,7},{2,0},{3,1},{4,2},{5,3},{6,4},{7,5},{8,14},{9,15},{10,... | collective-permute-start | bytes 196616 | tf_op jit(solution)/shard_map/ppermute | solution.py:59
  4.8 9.0 %collective-permute-start = (bf16[256,128]{1,0:T(8,128)(2,1)}, bf16[256,128]{1,0:T(8,128)(2,1)S(1)}, u32[]{:S(2)}, u32[]{:S(2)}) collective-permute-start(bf16[256,128]{1,0:T(8,128)(2,1)} %param.5), channel_id=1, source_target_pairs={{0,2},{1,3},{2,4},{3,5},{4,6},{5,7},{6,0},{7,1},{8,10},{9,11},{10,... | collective-permute-start | bytes 196616 | tf_op jit(solution)/shard_map/ppermute | solution.py:59
  4.8 9.0 %collective-permute-start.2 = (bf16[256,128]{1,0:T(8,128)(2,1)}, bf16[256,128]{1,0:T(8,128)(2,1)S(1)}, u32[]{:S(2)}, u32[]{:S(2)}) collective-permute-start(bf16[256,128]{1,0:T(8,128)(2,1)} %param.5), channel_id=1, source_target_pairs={{0,4},{1,5},{2,6},{3,7},{4,0},{5,1},{6,2},{7,3},{8,12},{9,13},{10,... | collective-permute-start | bytes 196616 | tf_op jit(solution)/shard_map/ppermute | solution.py:59
  9.4 4.4 %copy-start.2 = (bf16[256,128]{1,0:T(8,128)(2,1)S(1)}, bf16[256,128]{1,0:T(8,128)(2,1)}, u32[]{:S(2)}) copy-start(bf16[256,128]{1,0:T(8,128)(2,1)} %param.5) | copy-start | bytes 196612
  9.5 20.8 %all-to-all-start = ((bf16[4,8,19456]{2,1,0:T(8,128)(2,1)}), bf16[4,8,19456]{2,1,0:T(8,128)(2,1)S(1)}, u32[]{:S(2)}, u32[]{:S(2)}) async-start(bf16[4,8,19456]{2,1,0:T(8,128)(2,1)} %bitcast.21), calls=%async_computation | async-start | bytes 2490368 | tf_op jit(solution)/shard_map/all_to_all | solution.py:414
  13.9 10.8 %collective-permute-start.5 = (bf16[1024,128]{1,0:T(8,128)(2,1)S(1)}, bf16[1024,128]{1,0:T(8,128)(2,1)S(1)}, u32[]{:S(2)}, u32[]{:S(2)}) collective-permute-start(bf16[1024,128]{1,0:T(8,128)(2,1)S(1)} %constant_dynamic-update-slice_fusion.refs_0_), channel_id=1, source_target_pairs={{0,16},{1,17},{2,18},{3,19},{4,20},{5,21},{6,22},{7,23},{8,24},{9,... | collective-permute-start | bytes 786440 | tf_op jit(solution)/shard_map/ppermute | solution.py:59
  17.2 11.2 %collective-permute-start.4 = (bf16[1024,128]{1,0:T(8,128)(2,1)S(1)}, bf16[1024,128]{1,0:T(8,128)(2,1)S(1)}, u32[]{:S(2)}, u32[]{:S(2)}) collective-permute-start(bf16[1024,128]{1,0:T(8,128)(2,1)S(1)} %constant_dynamic-update-slice_fusion.refs_0_), channel_id=1, source_target_pairs={{0,24},{1,25},{2,26},{3,27},{4,28},{5,29},{6,30},{7,31},{8,0},{9,1... | collective-permute-start | bytes 786440 | tf_op jit(solution)/shard_map/ppermute | solution.py:59
  18.2 10.2 %collective-permute-start.3 = (bf16[1024,128]{1,0:T(8,128)(2,1)S(1)}, bf16[1024,128]{1,0:T(8,128)(2,1)S(1)}, u32[]{:S(2)}, u32[]{:S(2)}) collective-permute-start(bf16[1024,128]{1,0:T(8,128)(2,1)S(1)} %constant_dynamic-update-slice_fusion.refs_0_), channel_id=1, source_target_pairs={{0,8},{1,9},{2,10},{3,11},{4,12},{5,13},{6,14},{7,15},{8,16},{9,17... | collective-permute-start | bytes 786440 | tf_op jit(solution)/shard_map/ppermute | solution.py:59
  19.2 9.7 %collective-permute-start.6 = (bf16[1024,128]{1,0:T(8,128)(2,1)S(1)}, bf16[1024,128]{1,0:T(8,128)(2,1)S(1)}, u32[]{:S(2)}, u32[]{:S(2)}) collective-permute-start(bf16[1024,128]{1,0:T(8,128)(2,1)S(1)} %constant_dynamic-update-slice_fusion.refs_0_), channel_id=1, source_target_pairs={{0,1},{1,0},{2,3},{3,2},{4,5},{5,4},{6,7},{7,6},{8,9},{9,8},{10,11... | collective-permute-start | bytes 786440 | tf_op jit(solution)/shard_map/ppermute | solution.py:55
  24.7 4.2 %collective-permute-start.9 = (bf16[1024,128]{1,0:T(8,128)(2,1)S(1)}, bf16[1024,128]{1,0:T(8,128)(2,1)S(1)}, u32[]{:S(2)}, u32[]{:S(2)}) collective-permute-start(bf16[1024,128]{1,0:T(8,128)(2,1)S(1)} %collective-permute-done.5.refs_3_), channel_id=1, source_target_pairs={{0,1},{1,0},{2,3},{3,2},{4,5},{5,4},{6,7},{7,6},{8,9},{9,8},{10,11... | collective-permute-start | bytes 786440 | tf_op jit(solution)/shard_map/ppermute | solution.py:55
  28.4 1.5 %collective-permute-start.8 = (bf16[1024,128]{1,0:T(8,128)(2,1)S(1)}, bf16[1024,128]{1,0:T(8,128)(2,1)S(1)}, u32[]{:S(2)}, u32[]{:S(2)}) collective-permute-start(bf16[1024,128]{1,0:T(8,128)(2,1)S(1)} %collective-permute-done.4.refs_2_), channel_id=1, source_target_pairs={{0,1},{1,0},{2,3},{3,2},{4,5},{5,4},{6,7},{7,6},{8,9},{9,8},{10,11... | collective-permute-start | bytes 786440 | tf_op jit(solution)/shard_map/ppermute | solution.py:55
  28.4 1.9 %collective-permute-start.7 = (bf16[1024,128]{1,0:T(8,128)(2,1)S(1)}, bf16[1024,128]{1,0:T(8,128)(2,1)S(1)}, u32[]{:S(2)}, u32[]{:S(2)}) collective-permute-start(bf16[1024,128]{1,0:T(8,128)(2,1)S(1)} %collective-permute-done.3.refs_1_), channel_id=1, source_target_pairs={{0,1},{1,0},{2,3},{3,2},{4,5},{5,4},{6,7},{7,6},{8,9},{9,8},{10,11... | collective-permute-start | bytes 786440 | tf_op jit(solution)/shard_map/ppermute | solution.py:55
  40.8 26.4 %copy-start = (s32[256]{0:T(256)S(1)}, s32[256]{0:T(256)}, u32[]{:S(2)}) copy-start(s32[256]{0:T(256)} %param.8) | copy-start | bytes 3076
  40.8 26.3 %copy-start.1 = (f32[256]{0:T(256)S(1)}, f32[256]{0:T(256)}, u32[]{:S(2)}) copy-start(f32[256]{0:T(256)} %param.9) | copy-start | bytes 3076
  72.4 4.0 %collective-permute-start.10 = (bf16[16,128,256]{2,1,0:T(8,128)(2,1)S(1)}, bf16[16,128,256]{2,1,0:T(8,128)(2,1)S(1)}, u32[]{:S(2)}, u32[]{:S(2)}) collective-permute-start(bf16[16,128,256]{2,1,0:T(8,128)(2,1)S(1)} %get-tuple-element.26), channel_id=1, source_target_pairs={{0,1},{1,0},{2,3},{3,2},{4,5},{5,4},{6,7},{7,6},{8,9},{9,8},{10,11... | collective-permute-start | bytes 3145736 | tf_op jit(solution)/shard_map/ppermute | solution.py:55
  72.8 3.6 %collective-permute-start.11 = (bf16[16,256]{1,0:T(8,128)(2,1)S(1)}, bf16[16,256]{1,0:T(8,128)(2,1)S(1)}, u32[]{:S(2)}, u32[]{:S(2)}) collective-permute-start(bf16[16,256]{1,0:T(8,128)(2,1)S(1)} %get-tuple-element.27.ta_ref), channel_id=1, source_target_pairs={{0,1},{1,0},{2,3},{3,2},{4,5},{5,4},{6,7},{7,6},{8,9},{9,8},{10,11... | collective-permute-start | bytes 24584 | tf_op jit(solution)/shard_map/ppermute | solution.py:55

commit v7 on v6

--- a/solution.py
+++ b/solution.py
@@ -74,12 +74,34 @@
 
 
 ROWS = 32
+FIRST = 384
 BLOCK = 512
 AHEAD = 2
 
 
 def column_blocks(width):
-    return [(first, min(BLOCK, width - first)) for first in range(0, width, BLOCK)]
+    sizes = [FIRST] + [min(BLOCK, width - at) for at in range(FIRST, width, BLOCK)]
+    return [(sum(sizes[:i]), size) for i, size in enumerate(sizes)]
+
+
+def first_kernel(w_ref, head_ref, sem):
+    copy = pltpu.make_async_copy(w_ref.at[:, pl.ds(0, head_ref.shape[1])], head_ref, sem)
+    copy.start()
+    copy.wait()
+
+
+def first_block(head_weight):
+    depth, width = head_weight.shape
+    return pl.pallas_call(
+        first_kernel,
+        in_specs=[HBM],
+        out_specs=VMEM,
+        out_shape=jax.ShapeDtypeStruct((depth, column_blocks(width)[0][1]), head_weight.dtype),
+        scratch_shapes=[pltpu.SemaphoreType.DMA],
+        compiler_params=params(2),
+        cost_estimate=cost(0, 4 * depth * BLOCK),
+        name="first_block",
+    )(in_hbm(head_weight))
 
 
 def parts_of(x, count):
@@ -91,21 +113,22 @@
 
 
 def student_kernel(meta_ref, *refs):
-    blocks = column_blocks(refs[2 * RING + 2].shape[1])
+    own, other = refs[0:RING], refs[RING : 2 * RING]
+    w_ref, x_ref, first_ref, s_ref, send_ref = refs[2 * RING : 2 * RING + 5]
+    blocks = column_blocks(s_ref.shape[1])
     n = len(blocks)
-    own, other = refs[0:RING], refs[RING : 2 * RING]
-    w_ref, x_ref, s_ref, send_ref = refs[2 * RING : 2 * RING + 4]
-    heads = refs[2 * RING + 4 : 2 * RING + 4 + n]
+    heads = refs[2 * RING + 2 : 2 * RING + 3] + refs[2 * RING + 5 : 2 * RING + 4 + n]
     hidden, peaks, totals, t_peaks, t_totals, sem = refs[2 * RING + 4 + n :]
     rows, width = s_ref.shape
     tiles_x, shards = x_ref.shape[0], x_ref.shape[2] // width
     share = own[0].shape[1]
     core = meta_ref[0]
-    copies = [
+    copies = [None] + [
         pltpu.make_async_copy(w_ref.at[:, pl.ds(first, size)], heads[k], sem.at[k])
         for k, (first, size) in enumerate(blocks)
+        if k > 0
     ]
-    for copy in copies[:AHEAD]:
+    for copy in copies[1 : 1 + AHEAD]:
         copy.start()
     for i in range(CHIPS):
         at = slice((i % RING) * rows, (i % RING + 1) * rows)
@@ -138,9 +161,10 @@
         add(tiles, t_peaks, t_totals, k)
 
     for k, (first, size) in enumerate(blocks):
-        copies[k].wait()
-        if k + AHEAD < n:
-            copies[k + AHEAD].start()
+        if k > 0:
+            copies[k].wait()
+            if k + AHEAD < n:
+                copies[k + AHEAD].start()
 
         @pl.when(core >= 0)
         def _():
@@ -171,19 +195,19 @@
         send_ref[i, :, width:] = stat
 
 
-def student_logits(meta, own, other, head_weight, teacher_rows):
+def student_logits(meta, own, other, head_weight, teacher_rows, first):
     depth, width = head_weight.shape
     rows = own[0].shape[0] // RING
     blocks = column_blocks(width)
     return pl.pallas_call(
         student_kernel,
-        in_specs=[SMEM] + [VMEM] * (2 * RING) + [HBM, VMEM],
-        out_specs=[VMEM] * (2 + len(blocks)),
+        in_specs=[SMEM] + [VMEM] * (2 * RING) + [HBM, VMEM, VMEM],
+        out_specs=[VMEM] * (1 + len(blocks)),
         out_shape=[
             jax.ShapeDtypeStruct((rows, width), jnp.float32),
             jax.ShapeDtypeStruct((2 * CHIPS, 8, width + 128), jnp.bfloat16),
         ]
-        + [jax.ShapeDtypeStruct((depth, size), jnp.bfloat16) for _, size in blocks],
+        + [jax.ShapeDtypeStruct((depth, size), jnp.bfloat16) for _, size in blocks[1:]],
         scratch_shapes=[
             pltpu.VMEM((rows, depth), jnp.bfloat16),
             pltpu.VMEM((rows, 128), jnp.float32),
@@ -195,7 +219,7 @@
         compiler_params=params(10),
         cost_estimate=cost(2 * rows * depth * width, 2 * depth * width),
         name="student_logits",
-    )(meta, *own, *other, in_hbm(head_weight), teacher_rows)
+    )(meta, *own, *other, in_hbm(head_weight), teacher_rows, in_vmem(first))
 
 
 def merged(stats, rows):
@@ -414,9 +438,10 @@
     blocks = lax.all_to_all(after(blocks, meta), "tok", 0, 0, tiled=True)
     own = from_ring(along_z, "dy")
     other = [swap_core(x) for x in own]
-    student, send, *heads = student_logits(
-        meta, own, other, head_weight, blocks.reshape(-1, 8, blocks.shape[1])
-    )
+    blocks = blocks.reshape(-1, 8, blocks.shape[1])
+    first = first_block(after(head_weight, blocks))
+    student, send, *heads = student_logits(meta, own, other, head_weight, blocks, first)
+    heads = [first] + heads
 
     teacher = lax.all_to_all(send, "vocab", 0, 0, tiled=True)
     grad, part, tail = logit_grad(

time: 99.8 us -> 101 us (1.012)
    pallas_call x0 -> x1, Pallas kernels: none -> 1.9 us  [first_block(): pl.pallas_call(first_kernel, in_specs=[HBM], out_specs=VMEM, out_shape=ja...]
    ppermute x6, waiting for transfers between devices: 1.4 us -> 0.02 us  [swap_core(): return lax.ppermute(x, 'vocab', moves(dcore=1))]
    pallas_call x1, Pallas kernels: 10.5 us -> 9.17 us  [student_logits(): pl.pallas_call(student_kernel, in_specs=[SMEM] + [VMEM] * (2 * RING) + [H...]
    all_to_all x1, waiting for transfers between devices: 0.01 us -> 1.23 us  [on_device(): blocks = lax.all_to_all(after(blocks, meta), 'tok', 0, 0, tiled=True)]
  transfers between devices with their start and end apart: 13 -> 13, of which waited for: 4 -> 3; matrix products, arithmetic and copies ran while one was open for 3% -> 3% of each run, Pallas kernels for 3% -> 5%
where the time goes in v7:
time: 101 us; the launch traced here: 100 us
  blocking collectives  48.4 us (48%)
  Pallas kernels  20.9 us (21%)
  starting transfers between devices  16.8 us (17%)
  waiting for transfers between devices  10.5 us (10%)
  local copies, waits for them, and re-layouts  2.86 us (3%)
    all_to_all x1, blocking collectives, on_device(): teacher = lax.all_to_all(send, 'vocab', 0, 0, tiled=True)  26.5 us
    all_to_all x1, blocking collectives, on_device(): lax.all_to_all(summed.reshape(CHIPS * (share + TAIL), rows), 'vocab', 0,...  21.9 us
    ppermute x6, starting transfers between devices, from_ring(): lax.ppermute(x, 'vocab', moves(**{axis: d}))  11.4 us
    ppermute x6, waiting for transfers between devices, from_ring(): lax.ppermute(x, 'vocab', moves(**{axis: d}))  9.21 us
    pallas_call x1, Pallas kernels, student_logits(): pl.pallas_call(student_kernel, in_specs=[SMEM] + [VMEM] * (2 * RING) + [H...  9.17 us
    pallas_call x1, Pallas kernels, logit_grad(): pl.pallas_call(grad_kernel, in_specs=[SMEM] + [VMEM] * (4 + len(heads)),...  5.29 us
    all_to_all x1, starting transfers between devices, on_device(): blocks = lax.all_to_all(after(blocks, meta), 'tok', 0, 0, tiled=True)  4.3 us
    pallas_call x1, Pallas kernels, own_share(): pl.pallas_call(own_kernel, in_specs=[SMEM] + [VMEM] * (1 + len(heads)), o...  3.44 us
  transfers between devices with their start and end apart: 13, of which 3 were waited for; matrix products, arithmetic and copies ran while one was open for 3% of the time, Pallas kernels for 5%

profile of v7, /device:TPU:0, one launch (start us, length us, event | category | flops | bytes accessed | tf_op | source)
XLA Modules:
  0.0 100.2 jit_solution(7768224635865087966)
XLA Ops:
  0.6 4.2 %collective-permute-start.1 = (bf16[256,128]{1,0:T(8,128)(2,1)}, bf16[256,128]{1,0:T(8,128)(2,1)S(1)}, u32[]{:S(2)}, u32[]{:S(2)}) collective-permute-start(bf16[256,128]{1,0:T(8,128)(2,1)} %param.5), channel_id=1, source_target_pairs={{0,6},{1,7},{2,0},{3,1},{4,2},{5,3},{6,4},{7,5},{8,14},{9,15},{10,... | collective-permute-start | bytes 196616 | tf_op jit(solution)/shard_map/ppermute | solution.py:59
  4.8 1.9 %collective-permute-start.2 = (bf16[256,128]{1,0:T(8,128)(2,1)}, bf16[256,128]{1,0:T(8,128)(2,1)S(1)}, u32[]{:S(2)}, u32[]{:S(2)}) collective-permute-start(bf16[256,128]{1,0:T(8,128)(2,1)} %param.5), channel_id=1, source_target_pairs={{0,4},{1,5},{2,6},{3,7},{4,0},{5,1},{6,2},{7,3},{8,12},{9,13},{10,... | collective-permute-start | bytes 196616 | tf_op jit(solution)/shard_map/ppermute | solution.py:59
  6.7 2.7 %copy.10 = bf16[8,4,19456]{2,0,1:T(8,128)(2,1)} copy(bf16[8,4,19456]{2,1,0:T(4,128)(2,1)} %param.7) | data formatting | bytes 2490368 | tf_op args[2]
  9.4 0.1 stack.79.meta_ref
  9.5 4.3 %all-to-all-start = ((bf16[4,8,19456]{2,1,0:T(8,128)(2,1)}), bf16[4,8,19456]{2,1,0:T(8,128)(2,1)S(1)}, u32[]{:S(2)}, u32[]{:S(2)}) async-start(bf16[4,8,19456]{2,1,0:T(8,128)(2,1)} %bitcast.21), calls=%async_computation | async-start | bytes 2490368 | tf_op jit(solution)/shard_map/all_to_all | solution.py:438
  13.9 3.3 %collective-permute-start.5 = (bf16[1024,128]{1,0:T(8,128)(2,1)S(1)}, bf16[1024,128]{1,0:T(8,128)(2,1)S(1)}, u32[]{:S(2)}, u32[]{:S(2)}) collective-permute-start(bf16[1024,128]{1,0:T(8,128)(2,1)S(1)} %constant_dynamic-update-slice_fusion.refs_0_), channel_id=1, source_target_pairs={{0,16},{1,17},{2,18},{3,19},{4,20},{5,21},{6,22},{7,23},{8,24},{9,... | collective-permute-start | bytes 786440 | tf_op jit(solution)/shard_map/ppermute | solution.py:59
  17.2 1.1 %collective-permute-start.4 = (bf16[1024,128]{1,0:T(8,128)(2,1)S(1)}, bf16[1024,128]{1,0:T(8,128)(2,1)S(1)}, u32[]{:S(2)}, u32[]{:S(2)}) collective-permute-start(bf16[1024,128]{1,0:T(8,128)(2,1)S(1)} %constant_dynamic-update-slice_fusion.refs_0_), channel_id=1, source_target_pairs={{0,24},{1,25},{2,26},{3,27},{4,28},{5,29},{6,30},{7,31},{8,0},{9,1... | collective-permute-start | bytes 786440 | tf_op jit(solution)/shard_map/ppermute | solution.py:59
  18.2 1.0 collective-permute-start.3
  19.2 5.5 %collective-permute-done.5.refs_3_ = bf16[1024,128]{1,0:T(8,128)(2,1)S(1)} collective-permute-done((bf16[1024,128]{1,0:T(8,128)(2,1)S(1)}, bf16[1024,128]{1,0:T(8,128)(2,1)S(1)}, u32[]{:S(2)}, u32[]{:S(2)}) %collective-permute-start.5) | collective-permute-done | bytes 262176 | tf_op jit(solution)/shard_map/ppermute | solution.py:59
  24.7 3.7 %collective-permute-done.4.refs_2_ = bf16[1024,128]{1,0:T(8,128)(2,1)S(1)} collective-permute-done((bf16[1024,128]{1,0:T(8,128)(2,1)S(1)}, bf16[1024,128]{1,0:T(8,128)(2,1)S(1)}, u32[]{:S(2)}, u32[]{:S(2)}) %collective-permute-start.4) | collective-permute-done | bytes 262176 | tf_op jit(solution)/shard_map/ppermute | solution.py:59
  28.4 0.5 collective-permute-start.7
  28.9 1.2 %all-to-all-done.refs_9_ = bf16[4,8,19456]{2,1,0:T(8,128)(2,1)S(1)} async-done(((bf16[4,8,19456]{2,1,0:T(8,128)(2,1)}), bf16[4,8,19456]{2,1,0:T(8,128)(2,1)S(1)}, u32[]{:S(2)}, u32[]{:S(2)}) %all-to-all-start) | async-done | bytes 1245216 | tf_op jit(solution)/shard_map/all_to_all | solution.py:438
  30.2 1.9 %first_block.1.refs_10_.refs_0_ = bf16[4096,384]{1,0:T(8,128)(2,1)S(1)} custom-call(bf16[4096,2432]{1,0:T(8,128)(2,1)} %refs_8_.1), custom_call_target="tpu_custom_call" | custom-call | bytes 8388608 | tf_op jit(solution)/shard_map/first_block/pallas_call | solution.py:95
  32.1 9.2 %student_logits.1 = (f32[256,2432]{1,0:T(8,128)S(1)}, bf16[32,8,2560]{2,1,0:T(8,128)(2,1)S(1)}, bf16[4096,512]{1,0:T(8,128)(2,1)S(1)}, bf16[4096,512]{1,0:T(8,12...) custom-call(s32[19]{0:T(128)S(1)} %stack.79.meta_ref, ...), custom_call_target="tpu_custom_call" | custom-call | flops 5100273664 | bytes 19922944 | tf_op jit(solution)/shard_map/student_logits/pallas_call | solution.py:202
  41.3 0.0 copy-start
  41.3 0.0 copy-start.1
  41.3 26.5 %all_to_all.20.x_ref = bf16[32,8,2560]{2,1,0:T(8,128)(2,1)S(1)} all-to-all(bf16[32,8,2560]{2,1,0:T(8,128)(2,1)S(1)} %get-tuple-element.19), channel_id=1, replica_groups=mesh['tok'=4,'vocab'=32] {'vocab'}, dimensions={0} | all-to-all | bytes 2621440 | tf_op jit(solution)/shard_map/all_to_all | solution.py:446
  67.8 5.3 %logit_grad.1 = (bf16[256,2432]{1,0:T(8,128)(2,1)S(1)}, bf16[16,128,256]{2,1,0:T(8,128)(2,1)S(1)}, bf16[16,256]{1,0:T(8,128)(2,1)S(1)}) custom-call(s32[19]{0:T(128)S(1)} %stack.79.meta_ref, bf16[32,8,2560]{2,1,0:T(8,128)(2,1)S(1)} %all_to_all.20.x_ref, f32[256,2432]{1,0:T(8,128)S(1)} %get-tuple-element.20.s_ref, s32[1,256]{1,0:T(1,128)S(1)} %bitcast.29, ...), custom_call_target="tpu_custom_call" | custom-call | flops 2550136832 | bytes 9961472 | tf_op jit(solution)/shard_map/logit_grad/pallas_call | solution.py:311
  73.1 0.4 collective-permute-start.10
  73.5 0.2 collective-permute-start.11
  73.7 3.4 %own_share.1.a_ref = bf16[16,128,256]{2,1,0:T(8,128)(2,1)S(1)} custom-call(s32[19]{0:T(128)S(1)} %stack.79.meta_ref, bf16[256,2432]{1,0:T(8,128)(2,1)S(1)} %get-tuple-element.25.grad_ref, bf16[4096,384]{1,0:T(8,128)(2,1)S(1)} %first_block.1.refs_10_.refs_0_, bf16[4096,512]{1,0:T(8,128)(2,1)S(1)} %get-tuple-element.21.refs_1_, ...), custom_call_target="tpu_custom_call" | custom-call | flops 2550136832 | bytes 9961472 | tf_op jit(solution)/shard_map/own_share/pallas_call | solution.py:355
  77.2 0.3 chip_sum.1
  77.5 21.9 %all_to_all.21.x_ref = bf16[16,144,256]{2,1,0:T(8,128)(2,1)S(1)} all-to-all(bf16[16,144,256]{2,1,0:T(8,128)(2,1)S(1)} %chip_sum.1), channel_id=1, replica_groups={{0,2,4,6,8,10,12,14,16,18,20,22,24,26,28,30},{1,3,5,7,9,11,13,15,17,19,..., dimensions={0} | all-to-all | bytes 2359296 | tf_op jit(solution)/shard_map/all_to_all | solution.py:455
  99.4 0.8 final_sum.1
  (22 shorter events, 0.1 us)
Async XLA Ops:
  0.6 13.2 %collective-permute-start.1 = (bf16[256,128]{1,0:T(8,128)(2,1)}, bf16[256,128]{1,0:T(8,128)(2,1)S(1)}, u32[]{:S(2)}, u32[]{:S(2)}) collective-permute-start(bf16[256,128]{1,0:T(8,128)(2,1)} %param.5), channel_id=1, source_target_pairs={{0,6},{1,7},{2,0},{3,1},{4,2},{5,3},{6,4},{7,5},{8,14},{9,15},{10,... | collective-permute-start | bytes 196616 | tf_op jit(solution)/shard_map/ppermute | solution.py:59
  4.8 9.0 %collective-permute-start = (bf16[256,128]{1,0:T(8,128)(2,1)}, bf16[256,128]{1,0:T(8,128)(2,1)S(1)}, u32[]{:S(2)}, u32[]{:S(2)}) collective-permute-start(bf16[256,128]{1,0:T(8,128)(2,1)} %param.5), channel_id=1, source_target_pairs={{0,2},{1,3},{2,4},{3,5},{4,6},{5,7},{6,0},{7,1},{8,10},{9,11},{10,... | collective-permute-start | bytes 196616 | tf_op jit(solution)/shard_map/ppermute | solution.py:59
  4.8 9.0 %collective-permute-start.2 = (bf16[256,128]{1,0:T(8,128)(2,1)}, bf16[256,128]{1,0:T(8,128)(2,1)S(1)}, u32[]{:S(2)}, u32[]{:S(2)}) collective-permute-start(bf16[256,128]{1,0:T(8,128)(2,1)} %param.5), channel_id=1, source_target_pairs={{0,4},{1,5},{2,6},{3,7},{4,0},{5,1},{6,2},{7,3},{8,12},{9,13},{10,... | collective-permute-start | bytes 196616 | tf_op jit(solution)/shard_map/ppermute | solution.py:59
  9.4 4.4 %copy-start.2 = (bf16[256,128]{1,0:T(8,128)(2,1)S(1)}, bf16[256,128]{1,0:T(8,128)(2,1)}, u32[]{:S(2)}) copy-start(bf16[256,128]{1,0:T(8,128)(2,1)} %param.5) | copy-start | bytes 196612
  9.5 20.7 %all-to-all-start = ((bf16[4,8,19456]{2,1,0:T(8,128)(2,1)}), bf16[4,8,19456]{2,1,0:T(8,128)(2,1)S(1)}, u32[]{:S(2)}, u32[]{:S(2)}) async-start(bf16[4,8,19456]{2,1,0:T(8,128)(2,1)} %bitcast.21), calls=%async_computation | async-start | bytes 2490368 | tf_op jit(solution)/shard_map/all_to_all | solution.py:438
  13.9 10.8 %collective-permute-start.5 = (bf16[1024,128]{1,0:T(8,128)(2,1)S(1)}, bf16[1024,128]{1,0:T(8,128)(2,1)S(1)}, u32[]{:S(2)}, u32[]{:S(2)}) collective-permute-start(bf16[1024,128]{1,0:T(8,128)(2,1)S(1)} %constant_dynamic-update-slice_fusion.refs_0_), channel_id=1, source_target_pairs={{0,16},{1,17},{2,18},{3,19},{4,20},{5,21},{6,22},{7,23},{8,24},{9,... | collective-permute-start | bytes 786440 | tf_op jit(solution)/shard_map/ppermute | solution.py:59
  17.2 11.2 %collective-permute-start.4 = (bf16[1024,128]{1,0:T(8,128)(2,1)S(1)}, bf16[1024,128]{1,0:T(8,128)(2,1)S(1)}, u32[]{:S(2)}, u32[]{:S(2)}) collective-permute-start(bf16[1024,128]{1,0:T(8,128)(2,1)S(1)} %constant_dynamic-update-slice_fusion.refs_0_), channel_id=1, source_target_pairs={{0,24},{1,25},{2,26},{3,27},{4,28},{5,29},{6,30},{7,31},{8,0},{9,1... | collective-permute-start | bytes 786440 | tf_op jit(solution)/shard_map/ppermute | solution.py:59
  18.2 10.2 %collective-permute-start.3 = (bf16[1024,128]{1,0:T(8,128)(2,1)S(1)}, bf16[1024,128]{1,0:T(8,128)(2,1)S(1)}, u32[]{:S(2)}, u32[]{:S(2)}) collective-permute-start(bf16[1024,128]{1,0:T(8,128)(2,1)S(1)} %constant_dynamic-update-slice_fusion.refs_0_), channel_id=1, source_target_pairs={{0,8},{1,9},{2,10},{3,11},{4,12},{5,13},{6,14},{7,15},{8,16},{9,17... | collective-permute-start | bytes 786440 | tf_op jit(solution)/shard_map/ppermute | solution.py:59
  19.2 12.9 %collective-permute-start.6 = (bf16[1024,128]{1,0:T(8,128)(2,1)S(1)}, bf16[1024,128]{1,0:T(8,128)(2,1)S(1)}, u32[]{:S(2)}, u32[]{:S(2)}) collective-permute-start(bf16[1024,128]{1,0:T(8,128)(2,1)S(1)} %constant_dynamic-update-slice_fusion.refs_0_), channel_id=1, source_target_pairs={{0,1},{1,0},{2,3},{3,2},{4,5},{5,4},{6,7},{7,6},{8,9},{9,8},{10,11... | collective-permute-start | bytes 786440 | tf_op jit(solution)/shard_map/ppermute | solution.py:55
  24.7 7.3 %collective-permute-start.9 = (bf16[1024,128]{1,0:T(8,128)(2,1)S(1)}, bf16[1024,128]{1,0:T(8,128)(2,1)S(1)}, u32[]{:S(2)}, u32[]{:S(2)}) collective-permute-start(bf16[1024,128]{1,0:T(8,128)(2,1)S(1)} %collective-permute-done.5.refs_3_), channel_id=1, source_target_pairs={{0,1},{1,0},{2,3},{3,2},{4,5},{5,4},{6,7},{7,6},{8,9},{9,8},{10,11... | collective-permute-start | bytes 786440 | tf_op jit(solution)/shard_map/ppermute | solution.py:55
  28.4 3.7 %collective-permute-start.8 = (bf16[1024,128]{1,0:T(8,128)(2,1)S(1)}, bf16[1024,128]{1,0:T(8,128)(2,1)S(1)}, u32[]{:S(2)}, u32[]{:S(2)}) collective-permute-start(bf16[1024,128]{1,0:T(8,128)(2,1)S(1)} %collective-permute-done.4.refs_2_), channel_id=1, source_target_pairs={{0,1},{1,0},{2,3},{3,2},{4,5},{5,4},{6,7},{7,6},{8,9},{9,8},{10,11... | collective-permute-start | bytes 786440 | tf_op jit(solution)/shard_map/ppermute | solution.py:55
  28.4 3.7 %collective-permute-start.7 = (bf16[1024,128]{1,0:T(8,128)(2,1)S(1)}, bf16[1024,128]{1,0:T(8,128)(2,1)S(1)}, u32[]{:S(2)}, u32[]{:S(2)}) collective-permute-start(bf16[1024,128]{1,0:T(8,128)(2,1)S(1)} %collective-permute-done.3.refs_1_), channel_id=1, source_target_pairs={{0,1},{1,0},{2,3},{3,2},{4,5},{5,4},{6,7},{7,6},{8,9},{9,8},{10,11... | collective-permute-start | bytes 786440 | tf_op jit(solution)/shard_map/ppermute | solution.py:55
  41.3 26.5 %copy-start = (s32[256]{0:T(256)S(1)}, s32[256]{0:T(256)}, u32[]{:S(2)}) copy-start(s32[256]{0:T(256)} %param.8) | copy-start | bytes 3076
  41.3 26.5 %copy-start.1 = (f32[256]{0:T(256)S(1)}, f32[256]{0:T(256)}, u32[]{:S(2)}) copy-start(f32[256]{0:T(256)} %param.9) | copy-start | bytes 3076
  73.1 4.0 %collective-permute-start.10 = (bf16[16,128,256]{2,1,0:T(8,128)(2,1)S(1)}, bf16[16,128,256]{2,1,0:T(8,128)(2,1)S(1)}, u32[]{:S(2)}, u32[]{:S(2)}) collective-permute-start(bf16[16,128,256]{2,1,0:T(8,128)(2,1)S(1)} %get-tuple-element.26), channel_id=1, source_target_pairs={{0,1},{1,0},{2,3},{3,2},{4,5},{5,4},{6,7},{7,6},{8,9},{9,8},{10,11... | collective-permute-start | bytes 3145736 | tf_op jit(solution)/shard_map/ppermute | solution.py:55
  73.5 3.6 %collective-permute-start.11 = (bf16[16,256]{1,0:T(8,128)(2,1)S(1)}, bf16[16,256]{1,0:T(8,128)(2,1)S(1)}, u32[]{:S(2)}, u32[]{:S(2)}) collective-permute-start(bf16[16,256]{1,0:T(8,128)(2,1)S(1)} %get-tuple-element.27.ta_ref), channel_id=1, source_target_pairs={{0,1},{1,0},{2,3},{3,2},{4,5},{5,4},{6,7},{7,6},{8,9},{9,8},{10,11... | collective-permute-start | bytes 24584 | tf_op jit(solution)/shard_map/ppermute | solution.py:55

commit v8 on v6

--- a/solution.py
+++ b/solution.py
@@ -221,7 +221,7 @@
 def grad_kernel(meta_ref, x_ref, s_ref, id_ref, weight_ref, *refs):
     blocks = column_blocks(s_ref.shape[1])
     heads = refs[: len(blocks)]
-    grad_ref, part_ref, tail_ref, column, cross, picked, total = refs[len(blocks) :]
+    grad_ref, part_ref, column, cross, picked, total = refs[len(blocks) :]
     rows, width = s_ref.shape
     stats = [x_ref[i, :, width:].astype(jnp.float32) for i in range(x_ref.shape[0])]
     student_row, teacher_column = merged(stats, rows)
@@ -241,6 +241,7 @@
             at = slice(r, r + ROWS)
             student_lse, teacher_lse, weight = column[at, 0:1], column[at, 1:2], column[at, 2:3]
             target = column[at, 3:4].astype(jnp.int32) - meta_ref[1]
+            target_weight = CE_WEIGHT * weight
             gap = jnp.zeros((ROWS, 128), jnp.float32) if k == 0 else cross[at, :]
             pick = jnp.zeros((ROWS, 128), jnp.float32) if k == 0 else picked[at, :]
             for j in range(first, first + size, 128):
@@ -251,10 +252,9 @@
                 student_prob = jnp.exp(student_logp)
                 teacher_prob = jnp.exp(teacher_logp)
                 hit = lane == target - j
-                onehot = jnp.where(hit, 1.0, 0.0)
                 gap += teacher_prob * (teacher_logp - student_logp)
-                pick += jnp.where(hit, -student_logp, 0.0)
-                grad = weight * ((student_prob - teacher_prob) + CE_WEIGHT * (student_prob - onehot))
+                pick = jnp.where(hit, student_logp, pick)
+                grad = weight * ((1.0 + CE_WEIGHT) * student_prob - teacher_prob) - jnp.where(hit, target_weight, 0.0)
                 grad_ref[at, cols] = grad.astype(jnp.bfloat16)
             cross[at, :] = gap
             picked[at, :] = pick
@@ -269,15 +269,15 @@
         elif k + 1 < len(steps):
             total[...] += out
         else:
-            part_ref[...] = (total[...] + out).astype(jnp.bfloat16).reshape(part_ref.shape)
+            part_ref[0 : total.shape[0], :] = (total[...] + out).astype(jnp.bfloat16)
 
     gap = to_row(jnp.sum(cross[...], axis=1, keepdims=True))
-    pick = to_row(jnp.sum(picked[...], axis=1, keepdims=True))
-    row = lax.broadcasted_iota(jnp.int32, tail_ref.shape, 0)
-    tail = jnp.zeros(tail_ref.shape, jnp.float32)
+    pick = -to_row(jnp.sum(picked[...], axis=1, keepdims=True))
+    row = lax.broadcasted_iota(jnp.int32, (TAIL, rows), 0)
+    tail = jnp.zeros((TAIL, rows), jnp.float32)
     for k, line in enumerate(parts_of(gap, 3) + parts_of(pick, 3)):
         tail = jnp.where(row == k, line, tail)
-    tail_ref[...] = tail.astype(jnp.bfloat16)
+    part_ref[total.shape[0] :, :] = tail.astype(jnp.bfloat16)
 
 
 def logit_grad(meta, teacher, student, ids, weights, heads):
@@ -287,11 +287,10 @@
     return pl.pallas_call(
         grad_kernel,
         in_specs=[SMEM] + [VMEM] * (4 + len(heads)),
-        out_specs=[VMEM] * 3,
+        out_specs=[VMEM] * 2,
         out_shape=[
             jax.ShapeDtypeStruct((rows, width), jnp.bfloat16),
-            jax.ShapeDtypeStruct((CHIPS, share, rows), jnp.bfloat16),
-            jax.ShapeDtypeStruct((TAIL, rows), jnp.bfloat16),
+            jax.ShapeDtypeStruct((CHIPS * share + TAIL, rows), jnp.bfloat16),
         ],
         scratch_shapes=[
             pltpu.VMEM((rows, 128), jnp.float32),
@@ -340,29 +339,33 @@
 
 
 def join_kernel(a_ref, b_ref, ta_ref, tb_ref, o_ref):
-    share = a_ref.shape[1]
-    total = a_ref[...].astype(jnp.float32) + b_ref[...].astype(jnp.float32)
+    blocks, share, rows = a_ref.shape
+    total = a_ref[...].astype(jnp.float32) + b_ref[...].reshape(blocks, share, rows).astype(jnp.float32)
     o_ref[:, 0:share, :] = total.astype(jnp.bfloat16)
     tail = jnp.concatenate(
         [ta_ref[...].astype(jnp.float32)[0 : TAIL // 2], tb_ref[...].astype(jnp.float32)[0 : TAIL // 2]]
     ).astype(jnp.bfloat16)
-    for i in range(o_ref.shape[0]):
+    for i in range(blocks):
         o_ref[i, share : share + TAIL, :] = tail
 
 
-def join(a, b, tail_a, tail_b):
-    chips, share, rows = a.shape
-    block = pl.BlockSpec((CHIP_BLOCK, share, rows), lambda i: (i, 0, 0))
-    tail = pl.BlockSpec((TAIL, rows), lambda i: (0, 0))
+def join(mine, sent, received):
+    chips, share, rows = mine.shape
+    tail = pl.BlockSpec((TAIL, rows), lambda i: (chips * share // TAIL, 0))
     return pl.pallas_call(
         join_kernel,
         grid=(chips // CHIP_BLOCK,),
-        in_specs=[block, block, tail, tail],
+        in_specs=[
+            pl.BlockSpec((CHIP_BLOCK, share, rows), lambda i: (i, 0, 0)),
+            pl.BlockSpec((CHIP_BLOCK * share, rows), lambda i: (i, 0)),
+            tail,
+            tail,
+        ],
         out_specs=pl.BlockSpec((CHIP_BLOCK, share + TAIL, rows), lambda i: (i, 0, 0)),
         out_shape=jax.ShapeDtypeStruct((chips, share + TAIL, rows), jnp.bfloat16),
         compiler_params=params(16),
         name="chip_sum",
-    )(a, b, tail_a, tail_b)
+    )(mine, received, sent, received)
 
 
 def final_kernel(x_ref, div_ref, ce_ref, o_ref):
@@ -419,12 +422,12 @@
     )
 
     teacher = lax.all_to_all(send, "vocab", 0, 0, tiled=True)
-    grad, part, tail = logit_grad(
+    grad, part = logit_grad(
         meta, teacher, student, token_ids.reshape(1, rows), token_weight.reshape(1, rows), heads
     )
-    from_core, from_tail = swap_core(part), swap_core(tail)
+    from_core = swap_core(part)
     mine = own_share(meta, grad, heads)
-    summed = join(mine, from_core, tail, from_tail)
+    summed = join(mine, part, from_core)
 
     same_core = [[member(i // RING, i % RING, c) for i in range(CHIPS)] for c in range(2)]
     blocks = lax.all_to_all(

time: 99.8 us -> 100 us (level)
  transfers between devices with their start and end apart: 13 -> 12, of which waited for: 4 -> 4; matrix products, arithmetic and copies ran while one was open for 3% -> 3% of each run, Pallas kernels for 3% -> 3%
where the time goes in v8:
time: 100 us; the launch traced here: 99.7 us
  blocking collectives  48.3 us (48%)
  Pallas kernels  20.6 us (21%)
  starting transfers between devices  16.6 us (17%)
  waiting for transfers between devices  10.6 us (11%)
  local copies, waits for them, and re-layouts  2.87 us (3%)
    all_to_all x1, blocking collectives, on_device(): teacher = lax.all_to_all(send, 'vocab', 0, 0, tiled=True)  26.3 us
    all_to_all x1, blocking collectives, on_device(): lax.all_to_all(summed.reshape(CHIPS * (share + TAIL), rows), 'vocab', 0,...  21.9 us
    ppermute x6, starting transfers between devices, from_ring(): lax.ppermute(x, 'vocab', moves(**{axis: d}))  11.4 us
    pallas_call x1, Pallas kernels, student_logits(): pl.pallas_call(student_kernel, in_specs=[SMEM] + [VMEM] * (2 * RING) + [H...  10.5 us
    ppermute x6, waiting for transfers between devices, from_ring(): lax.ppermute(x, 'vocab', moves(**{axis: d}))  9.21 us
    pallas_call x1, Pallas kernels, logit_grad(): pl.pallas_call(grad_kernel, in_specs=[SMEM] + [VMEM] * (4 + len(heads)),...  5.59 us
    all_to_all x1, starting transfers between devices, on_device(): blocks = lax.all_to_all(after(blocks, meta), 'tok', 0, 0, tiled=True)  4.3 us
    pallas_call x1, Pallas kernels, own_share(): pl.pallas_call(own_kernel, in_specs=[SMEM] + [VMEM] * (1 + len(heads)), o...  3.44 us
  transfers between devices with their start and end apart: 12, of which 4 were waited for; matrix products, arithmetic and copies ran while one was open for 3% of the time, Pallas kernels for 3%

profile of v8, /device:TPU:0, one launch (start us, length us, event | category | flops | bytes accessed | tf_op | source)
XLA Modules:
  0.0 99.7 jit_solution(15806415155156104728)
XLA Ops:
  0.6 4.2 %collective-permute-start.1 = (bf16[256,128]{1,0:T(8,128)(2,1)}, bf16[256,128]{1,0:T(8,128)(2,1)S(1)}, u32[]{:S(2)}, u32[]{:S(2)}) collective-permute-start(bf16[256,128]{1,0:T(8,128)(2,1)} %param.5), channel_id=1, source_target_pairs={{0,6},{1,7},{2,0},{3,1},{4,2},{5,3},{6,4},{7,5},{8,14},{9,15},{10,... | collective-permute-start | bytes 196616 | tf_op jit(solution)/shard_map/ppermute | solution.py:59
  4.8 0.0 collective-permute-start
  4.8 1.9 %collective-permute-start.2 = (bf16[256,128]{1,0:T(8,128)(2,1)}, bf16[256,128]{1,0:T(8,128)(2,1)S(1)}, u32[]{:S(2)}, u32[]{:S(2)}) collective-permute-start(bf16[256,128]{1,0:T(8,128)(2,1)} %param.5), channel_id=1, source_target_pairs={{0,4},{1,5},{2,6},{3,7},{4,0},{5,1},{6,2},{7,3},{8,12},{9,13},{10,... | collective-permute-start | bytes 196616 | tf_op jit(solution)/shard_map/ppermute | solution.py:59
  6.7 2.7 %copy.10 = bf16[8,4,19456]{2,0,1:T(8,128)(2,1)} copy(bf16[8,4,19456]{2,1,0:T(4,128)(2,1)} %param.7) | data formatting | bytes 2490368 | tf_op args[2]
  9.4 0.1 stack.79.meta_ref
  9.5 4.3 %all-to-all-start = ((bf16[4,8,19456]{2,1,0:T(8,128)(2,1)}), bf16[4,8,19456]{2,1,0:T(8,128)(2,1)S(1)}, u32[]{:S(2)}, u32[]{:S(2)}) async-start(bf16[4,8,19456]{2,1,0:T(8,128)(2,1)} %bitcast.21), calls=%async_computation | async-start | bytes 2490368 | tf_op jit(solution)/shard_map/all_to_all | solution.py:417
  13.9 3.3 %collective-permute-start.5 = (bf16[1024,128]{1,0:T(8,128)(2,1)S(1)}, bf16[1024,128]{1,0:T(8,128)(2,1)S(1)}, u32[]{:S(2)}, u32[]{:S(2)}) collective-permute-start(bf16[1024,128]{1,0:T(8,128)(2,1)S(1)} %constant_dynamic-update-slice_fusion.refs_0_), channel_id=1, source_target_pairs={{0,16},{1,17},{2,18},{3,19},{4,20},{5,21},{6,22},{7,23},{8,24},{9,... | collective-permute-start | bytes 786440 | tf_op jit(solution)/shard_map/ppermute | solution.py:59
  17.2 1.1 %collective-permute-start.4 = (bf16[1024,128]{1,0:T(8,128)(2,1)S(1)}, bf16[1024,128]{1,0:T(8,128)(2,1)S(1)}, u32[]{:S(2)}, u32[]{:S(2)}) collective-permute-start(bf16[1024,128]{1,0:T(8,128)(2,1)S(1)} %constant_dynamic-update-slice_fusion.refs_0_), channel_id=1, source_target_pairs={{0,24},{1,25},{2,26},{3,27},{4,28},{5,29},{6,30},{7,31},{8,0},{9,1... | collective-permute-start | bytes 786440 | tf_op jit(solution)/shard_map/ppermute | solution.py:59
  18.2 1.0 collective-permute-start.3
  19.2 5.5 %collective-permute-done.5.refs_3_ = bf16[1024,128]{1,0:T(8,128)(2,1)S(1)} collective-permute-done((bf16[1024,128]{1,0:T(8,128)(2,1)S(1)}, bf16[1024,128]{1,0:T(8,128)(2,1)S(1)}, u32[]{:S(2)}, u32[]{:S(2)}) %collective-permute-start.5) | collective-permute-done | bytes 262176 | tf_op jit(solution)/shard_map/ppermute | solution.py:59
  24.7 3.7 %collective-permute-done.4.refs_2_ = bf16[1024,128]{1,0:T(8,128)(2,1)S(1)} collective-permute-done((bf16[1024,128]{1,0:T(8,128)(2,1)S(1)}, bf16[1024,128]{1,0:T(8,128)(2,1)S(1)}, u32[]{:S(2)}, u32[]{:S(2)}) %collective-permute-start.4) | collective-permute-done | bytes 262176 | tf_op jit(solution)/shard_map/ppermute | solution.py:59
  28.4 0.5 collective-permute-start.7
  28.9 1.0 %collective-permute-done.8.refs_6_ = bf16[1024,128]{1,0:T(8,128)(2,1)S(1)} collective-permute-done((bf16[1024,128]{1,0:T(8,128)(2,1)S(1)}, bf16[1024,128]{1,0:T(8,128)(2,1)S(1)}, u32[]{:S(2)}, u32[]{:S(2)}) %collective-permute-start.8) | collective-permute-done | bytes 262176 | tf_op jit(solution)/shard_map/ppermute | solution.py:55
  29.9 0.4 collective-permute-done.7.refs_5_
  30.3 10.5 %student_logits.1 = (f32[256,2432]{1,0:T(8,128)S(1)}, bf16[32,8,2560]{2,1,0:T(8,128)(2,1)S(1)}, bf16[4096,512]{1,0:T(8,128)(2,1)S(1)}, bf16[4096,512]{1,0:T(8,12...) custom-call(s32[19]{0:T(128)S(1)} %stack.79.meta_ref, ...), custom_call_target="tpu_custom_call" | custom-call | flops 5100273664 | bytes 19922944 | tf_op jit(solution)/shard_map/student_logits/pallas_call | solution.py:178
  40.8 0.0 copy-start
  40.8 0.0 copy-start.1
  40.8 26.3 %all_to_all.20.x_ref = bf16[32,8,2560]{2,1,0:T(8,128)(2,1)S(1)} all-to-all(bf16[32,8,2560]{2,1,0:T(8,128)(2,1)S(1)} %get-tuple-element.17), channel_id=1, replica_groups=mesh['tok'=4,'vocab'=32] {'vocab'}, dimensions={0} | all-to-all | bytes 2621440 | tf_op jit(solution)/shard_map/all_to_all | solution.py:424
  67.2 5.6 %logit_grad.1 = (bf16[256,2432]{1,0:T(8,128)(2,1)S(1)}, bf16[2064,256]{1,0:T(8,128)(2,1)S(1)}) custom-call(s32[19]{0:T(128)S(1)} %stack.79.meta_ref, bf16[32,8,2560]{2,1,0:T(8,128)(2,1)S(1)} %all_to_all.20.x_ref, f32[256,2432]{1,0:T(8,128)S(1)} %get-tuple-element.18.s_ref, s32[1,256]{1,0:T(1,128)S(1)} %bitcast.29, f32[1,256]{1,0:T(1,128)S(1)} %bitcast.30, ...), custom_call_target="tpu_custom_call" | custom-call | flops 2550136832 | bytes 9961472 | tf_op jit(solution)/shard_map/logit_grad/pallas_call | solution.py:287
  72.8 0.4 collective-permute-start.10
  73.2 3.4 %own_share.1.a_ref = bf16[16,128,256]{2,1,0:T(8,128)(2,1)S(1)} custom-call(s32[19]{0:T(128)S(1)} %stack.79.meta_ref, bf16[256,2432]{1,0:T(8,128)(2,1)S(1)} %get-tuple-element.24.grad_ref, bf16[4096,512]{1,0:T(8,128)(2,1)S(1)} %get-tuple-element.19.refs_0_, bf16[4096,512]{1,0:T(8,128)(2,1)S(1)} %get-tuple-element.20.refs_1_, ...), custom_call_target="tpu_custom_call" | custom-call | flops 2550136832 | bytes 9961472 | tf_op jit(solution)/shard_map/own_share/pallas_call | solution.py:330
  76.6 0.3 chip_sum.1
  77.0 21.9 %all_to_all.21.x_ref = bf16[16,144,256]{2,1,0:T(8,128)(2,1)S(1)} all-to-all(bf16[16,144,256]{2,1,0:T(8,128)(2,1)S(1)} %chip_sum.1), channel_id=1, replica_groups={{0,2,4,6,8,10,12,14,16,18,20,22,24,26,28,30},{1,3,5,7,9,11,13,15,17,19,..., dimensions={0} | all-to-all | bytes 2359296 | tf_op jit(solution)/shard_map/all_to_all | solution.py:433
  98.9 0.8 final_sum.1
  (19 shorter events, 0.1 us)
Async XLA Ops:
  0.6 13.2 %collective-permute-start.1 = (bf16[256,128]{1,0:T(8,128)(2,1)}, bf16[256,128]{1,0:T(8,128)(2,1)S(1)}, u32[]{:S(2)}, u32[]{:S(2)}) collective-permute-start(bf16[256,128]{1,0:T(8,128)(2,1)} %param.5), channel_id=1, source_target_pairs={{0,6},{1,7},{2,0},{3,1},{4,2},{5,3},{6,4},{7,5},{8,14},{9,15},{10,... | collective-permute-start | bytes 196616 | tf_op jit(solution)/shard_map/ppermute | solution.py:59
  4.8 9.0 %collective-permute-start = (bf16[256,128]{1,0:T(8,128)(2,1)}, bf16[256,128]{1,0:T(8,128)(2,1)S(1)}, u32[]{:S(2)}, u32[]{:S(2)}) collective-permute-start(bf16[256,128]{1,0:T(8,128)(2,1)} %param.5), channel_id=1, source_target_pairs={{0,2},{1,3},{2,4},{3,5},{4,6},{5,7},{6,0},{7,1},{8,10},{9,11},{10,... | collective-permute-start | bytes 196616 | tf_op jit(solution)/shard_map/ppermute | solution.py:59
  4.8 9.1 %collective-permute-start.2 = (bf16[256,128]{1,0:T(8,128)(2,1)}, bf16[256,128]{1,0:T(8,128)(2,1)S(1)}, u32[]{:S(2)}, u32[]{:S(2)}) collective-permute-start(bf16[256,128]{1,0:T(8,128)(2,1)} %param.5), channel_id=1, source_target_pairs={{0,4},{1,5},{2,6},{3,7},{4,0},{5,1},{6,2},{7,3},{8,12},{9,13},{10,... | collective-permute-start | bytes 196616 | tf_op jit(solution)/shard_map/ppermute | solution.py:59
  9.4 4.4 %copy-start.2 = (bf16[256,128]{1,0:T(8,128)(2,1)S(1)}, bf16[256,128]{1,0:T(8,128)(2,1)}, u32[]{:S(2)}) copy-start(bf16[256,128]{1,0:T(8,128)(2,1)} %param.5) | copy-start | bytes 196612
  9.5 20.8 %all-to-all-start = ((bf16[4,8,19456]{2,1,0:T(8,128)(2,1)}), bf16[4,8,19456]{2,1,0:T(8,128)(2,1)S(1)}, u32[]{:S(2)}, u32[]{:S(2)}) async-start(bf16[4,8,19456]{2,1,0:T(8,128)(2,1)} %bitcast.21), calls=%async_computation | async-start | bytes 2490368 | tf_op jit(solution)/shard_map/all_to_all | solution.py:417
  13.9 10.8 %collective-permute-start.5 = (bf16[1024,128]{1,0:T(8,128)(2,1)S(1)}, bf16[1024,128]{1,0:T(8,128)(2,1)S(1)}, u32[]{:S(2)}, u32[]{:S(2)}) collective-permute-start(bf16[1024,128]{1,0:T(8,128)(2,1)S(1)} %constant_dynamic-update-slice_fusion.refs_0_), channel_id=1, source_target_pairs={{0,16},{1,17},{2,18},{3,19},{4,20},{5,21},{6,22},{7,23},{8,24},{9,... | collective-permute-start | bytes 786440 | tf_op jit(solution)/shard_map/ppermute | solution.py:59
  17.2 11.2 %collective-permute-start.4 = (bf16[1024,128]{1,0:T(8,128)(2,1)S(1)}, bf16[1024,128]{1,0:T(8,128)(2,1)S(1)}, u32[]{:S(2)}, u32[]{:S(2)}) collective-permute-start(bf16[1024,128]{1,0:T(8,128)(2,1)S(1)} %constant_dynamic-update-slice_fusion.refs_0_), channel_id=1, source_target_pairs={{0,24},{1,25},{2,26},{3,27},{4,28},{5,29},{6,30},{7,31},{8,0},{9,1... | collective-permute-start | bytes 786440 | tf_op jit(solution)/shard_map/ppermute | solution.py:59
  18.2 10.2 %collective-permute-start.3 = (bf16[1024,128]{1,0:T(8,128)(2,1)S(1)}, bf16[1024,128]{1,0:T(8,128)(2,1)S(1)}, u32[]{:S(2)}, u32[]{:S(2)}) collective-permute-start(bf16[1024,128]{1,0:T(8,128)(2,1)S(1)} %constant_dynamic-update-slice_fusion.refs_0_), channel_id=1, source_target_pairs={{0,8},{1,9},{2,10},{3,11},{4,12},{5,13},{6,14},{7,15},{8,16},{9,17... | collective-permute-start | bytes 786440 | tf_op jit(solution)/shard_map/ppermute | solution.py:59
  19.2 9.7 %collective-permute-start.6 = (bf16[1024,128]{1,0:T(8,128)(2,1)S(1)}, bf16[1024,128]{1,0:T(8,128)(2,1)S(1)}, u32[]{:S(2)}, u32[]{:S(2)}) collective-permute-start(bf16[1024,128]{1,0:T(8,128)(2,1)S(1)} %constant_dynamic-update-slice_fusion.refs_0_), channel_id=1, source_target_pairs={{0,1},{1,0},{2,3},{3,2},{4,5},{5,4},{6,7},{7,6},{8,9},{9,8},{10,11... | collective-permute-start | bytes 786440 | tf_op jit(solution)/shard_map/ppermute | solution.py:55
  24.7 4.2 %collective-permute-start.9 = (bf16[1024,128]{1,0:T(8,128)(2,1)S(1)}, bf16[1024,128]{1,0:T(8,128)(2,1)S(1)}, u32[]{:S(2)}, u32[]{:S(2)}) collective-permute-start(bf16[1024,128]{1,0:T(8,128)(2,1)S(1)} %collective-permute-done.5.refs_3_), channel_id=1, source_target_pairs={{0,1},{1,0},{2,3},{3,2},{4,5},{5,4},{6,7},{7,6},{8,9},{9,8},{10,11... | collective-permute-start | bytes 786440 | tf_op jit(solution)/shard_map/ppermute | solution.py:55
  28.4 1.5 %collective-permute-start.8 = (bf16[1024,128]{1,0:T(8,128)(2,1)S(1)}, bf16[1024,128]{1,0:T(8,128)(2,1)S(1)}, u32[]{:S(2)}, u32[]{:S(2)}) collective-permute-start(bf16[1024,128]{1,0:T(8,128)(2,1)S(1)} %collective-permute-done.4.refs_2_), channel_id=1, source_target_pairs={{0,1},{1,0},{2,3},{3,2},{4,5},{5,4},{6,7},{7,6},{8,9},{9,8},{10,11... | collective-permute-start | bytes 786440 | tf_op jit(solution)/shard_map/ppermute | solution.py:55
  28.4 1.9 %collective-permute-start.7 = (bf16[1024,128]{1,0:T(8,128)(2,1)S(1)}, bf16[1024,128]{1,0:T(8,128)(2,1)S(1)}, u32[]{:S(2)}, u32[]{:S(2)}) collective-permute-start(bf16[1024,128]{1,0:T(8,128)(2,1)S(1)} %collective-permute-done.3.refs_1_), channel_id=1, source_target_pairs={{0,1},{1,0},{2,3},{3,2},{4,5},{5,4},{6,7},{7,6},{8,9},{9,8},{10,11... | collective-permute-start | bytes 786440 | tf_op jit(solution)/shard_map/ppermute | solution.py:55
  40.8 26.4 %copy-start = (s32[256]{0:T(256)S(1)}, s32[256]{0:T(256)}, u32[]{:S(2)}) copy-start(s32[256]{0:T(256)} %param.8) | copy-start | bytes 3076
  40.8 26.4 %copy-start.1 = (f32[256]{0:T(256)S(1)}, f32[256]{0:T(256)}, u32[]{:S(2)}) copy-start(f32[256]{0:T(256)} %param.9) | copy-start | bytes 3076
  72.8 3.9 %collective-permute-start.10 = (bf16[2064,256]{1,0:T(8,128)(2,1)S(1)}, bf16[2064,256]{1,0:T(8,128)(2,1)S(1)}, u32[]{:S(2)}, u32[]{:S(2)}) collective-permute-start(bf16[2064,256]{1,0:T(8,128)(2,1)S(1)} %get-tuple-element.25.ta_ref), channel_id=1, source_target_pairs={{0,1},{1,0},{2,3},{3,2},{4,5},{5,4},{6,7},{7,6},{8,9},{9,8},{10,11... | collective-permute-start | bytes 3170312 | tf_op jit(solution)/shard_map/ppermute | solution.py:55
